TPU v7x, 128 devices: a whole 4x4x4 slice. The times are simulated.
128 devices in a mesh: ctx: 32 (over z, y, core), tp: 2 (over x_lo), dp: 2 (over x_hi).
Axes of the slice: x: 4 (x_hi: 2, x_lo: 2; x = x_hi * 2 + x_lo), y: 4, z: 4, core: 2. Of those that a mesh axis runs over, the one named last changes fastest.
Arguments:
- base_ids: int32 [2, 8192], P('dp', 'ctx'), may hold values from 0 to 4
- stream: bfloat16 [2, 8192, 1024], P('dp', 'ctx'), may hold values from -6 to 6
- cotangent: bfloat16 [2, 8192, 1024], P('dp', 'ctx'), may hold values from -0.0625 to 0.0625
- table: float32 [5, 1024], replicated, may hold values from -6 to 6
- gain: float32 [1024], replicated, may hold values from 0.5 to 1.5
- projections: bfloat16 [1024, 3, 2048], P(None, None, 'tp'), may hold values from -0.1875 to 0.1875
- mixer_weight: bfloat16 [1024, 128], replicated, may hold values from -0.0625 to 0.0625
- step_weight: bfloat16 [1024, 32], P(None, 'tp'), may hold values from -0.1875 to 0.1875
- step_bias: float32 [32], P('tp'), may hold values from -4 to -0.5
- rate: float32 [32], P('tp'), may hold values from 0.0001 to 0.3
Outputs:
- grad_projections: float32 [1024, 3, 2048], P(('ctx', 'dp'), None, 'tp')
- grad_mixer: float32 [1024, 128], replicated
- grad_step_weight: float32 [1024, 32], P(None, 'tp')
- grad_step_bias: float32 [32], P('tp')
- grad_rate: float32 [32], P('tp')
- grad_table: float32 [5, 1024], replicated
- grad_gain: float32 [1024], replicated
- grad_stream: float32 [2, 8192, 1024], P('dp', 'ctx', 'tp')
All inputs are finite; a program needn't handle non-finite values.
Results may differ from a plain program's by a relative error of at most 0.011.
Values sent between devices are 32-bit elements; how exact they have to be, the bound alone decides.
A program may use at most 192 MiB of HBM per device.

v0:
```python
import jax
import jax.numpy as jnp
from jax import lax
from jax.sharding import PartitionSpec as P

HEAD_DIM = 64
STATE = 64
GROUP = 256


EPS = 1e-05
HIGH = lax.Precision.HIGHEST


def entering(value, axis, join, neutral, backward):
    count, mine = (lax.axis_size(axis), lax.axis_index(axis))
    pieces = jax.tree.map(lambda part: lax.all_gather(part, axis), value)
    if backward:
        pieces = jax.tree.map(lambda part: part[::-1], pieces)
        mine = count - 1 - mine
    running = jax.tree.map(
        lambda part, zero: jnp.full_like(part, 0) + jnp.asarray(zero, part.dtype), value, neutral
    )

    def step(position, running):
        longer = join(running, jax.tree.map(lambda part: part[position], pieces))
        return jax.tree.map(lambda new, old: jnp.where(position < mine, new, old), longer, running)

    return lax.fori_loop(0, count - 1, step, running)


def complement(bases):
    return jnp.where(bases == 4, 4, 3 - bases)


def one_hot(bases):
    letters = jnp.arange(5, dtype=jnp.int32)
    return (bases[:, None] == letters[None, :]).astype(jnp.float32)


def lower_ones(length):
    rows = lax.broadcasted_iota(jnp.int32, (length, length), 0)
    columns = lax.broadcasted_iota(jnp.int32, (length, length), 1)
    return (rows >= columns).astype(jnp.float32)


def cumulative(lower, series):
    return jnp.dot(lower, series, precision=HIGH)


def times_transposed(left, right):
    return lax.dot_general(
        left, right, (((1,), (1,)), ((), ())), preferred_element_type=jnp.float32
    )


def outer_sum(left, right):
    return lax.dot_general(
        left, right, (((0,), (0,)), ((), ())), preferred_element_type=jnp.float32
    )


def heads_view(array, heads):
    return array.reshape(array.shape[0], heads, array.shape[1] // heads)


def prepare(
    bases, incoming, upstream, table, gain, projections, mixer_weight, step_weight, step_bias, rate
):
    embedded = incoming.astype(jnp.float32) + jnp.dot(one_hot(bases), table, precision=HIGH)
    inv_scale = lax.rsqrt(jnp.mean(embedded * embedded, axis=1, keepdims=True) + EPS)
    normed = embedded * inv_scale
    features = (normed * gain[None, :]).astype(jnp.bfloat16)
    values = jnp.dot(features, projections[:, 0, :], preferred_element_type=jnp.float32)
    gates = jnp.dot(features, projections[:, 1, :], preferred_element_type=jnp.float32)
    mapped = jnp.dot(features, mixer_weight, preferred_element_type=jnp.float32)
    step_logit = (
        jnp.dot(features, step_weight, preferred_element_type=jnp.float32) + step_bias[None, :]
    )
    step = jax.nn.softplus(step_logit)
    log_decay = -step * rate[None, :]
    grad_gated = jnp.dot(upstream, projections[:, 2, :], preferred_element_type=jnp.float32)
    swish = jax.nn.silu(gates)
    grad_output = grad_gated * swish
    return (
        normed,
        inv_scale,
        features,
        values,
        gates,
        mapped,
        step_logit,
        step,
        log_decay,
        swish,
        grad_gated,
        grad_output,
    )


def group_ends(log_decay, step, values, inflow, readout, grad_output):
    lower = lower_ones(log_decay.shape[0])
    running = cumulative(lower, log_decay)
    final_log = running[-1]
    tail = jnp.exp(final_log[None, :] - running)
    drive = step[:, :, None] * values
    state = jnp.einsum("jn,jhp->hnp", inflow, drive * tail[:, :, None], precision=HIGH)
    grad_state = jnp.einsum(
        "in,ihp->hnp", readout, grad_output * jnp.exp(running)[:, :, None], precision=HIGH
    )
    return (jnp.exp(final_log), state, grad_state)


def group_full(log_decay, step, values, inflow, readout, grad_output, initial, later_grad, rate):
    lower = lower_ones(log_decay.shape[0])
    running = cumulative(lower, log_decay)
    final_log = running[-1]
    head = jnp.exp(running)
    tail = jnp.exp(final_log[None, :] - running)
    spread = running.T[:, :, None] - running.T[:, None, :]
    decay_grid = jnp.exp(jnp.where(lower[None] > 0, spread, -1e30))
    drive = step[:, :, None] * values
    affinity = jnp.dot(readout, inflow.T, precision=HIGH)
    mixing = decay_grid * affinity[None]
    carried = jnp.einsum("in,hnp->ihp", readout, initial, precision=HIGH) * head[:, :, None]
    output = jnp.einsum("hij,jhp->ihp", mixing, drive, precision=HIGH) + carried
    pulled = jnp.einsum("jn,hnp->jhp", inflow, later_grad, precision=HIGH) * tail[:, :, None]
    grad_drive = jnp.einsum("hkj,khp->jhp", mixing, grad_output, precision=HIGH) + pulled
    pairing = decay_grid * jnp.einsum("khp,jhp->hkj", grad_output, drive, precision=HIGH)
    grad_inflow = jnp.einsum("hkj,kn->jn", pairing, readout, precision=HIGH) + jnp.einsum(
        "hnp,jhp->jn", later_grad, drive * tail[:, :, None], precision=HIGH
    )
    grad_readout = jnp.einsum("hij,jn->in", pairing, inflow, precision=HIGH) + jnp.einsum(
        "hnp,ihp->in", initial, grad_output * head[:, :, None], precision=HIGH
    )
    weighted = pairing * affinity[None]
    column_sums = jnp.sum(weighted, axis=1).T
    row_sums = jnp.sum(weighted, axis=2).T
    inside = cumulative(lower, column_sums) - cumulative(lower, row_sums) + row_sums
    before = jnp.dot(lower.T, jnp.sum(grad_output * carried, axis=2), precision=HIGH)
    boundary = jnp.exp(final_log) * jnp.sum(initial * later_grad, axis=(1, 2))
    after = cumulative(lower, jnp.sum(pulled * drive, axis=2))
    grad_log = inside + before + boundary[None, :] + after - jnp.sum(grad_drive * drive, axis=2)
    grad_values = step[:, :, None] * grad_drive
    grad_step = jnp.sum(grad_drive * values, axis=2) - grad_log * rate[None, :]
    grad_rate = -jnp.sum(grad_log * step, axis=0)
    return (output, grad_values, grad_step, grad_rate, grad_inflow, grad_readout)


def finish(prepared, mixer_terms, projections, mixer_weight, step_weight):
    (
        normed,
        inv_scale,
        features,
        values,
        gates,
        mapped,
        step_logit,
        step,
        log_decay,
        swish,
        grad_gated,
        grad_output,
    ) = prepared
    output, grad_values, grad_step, grad_rate, grad_inflow, grad_readout = mixer_terms
    gated = (output * swish).astype(jnp.bfloat16)
    sigma = jax.nn.sigmoid(gates)
    grad_gates = (grad_gated * output * sigma * (1.0 + gates * (1.0 - sigma))).astype(jnp.bfloat16)
    grad_values_rounded = grad_values.astype(jnp.bfloat16)
    grad_mapped = jnp.concatenate([grad_inflow, grad_readout], axis=1).astype(jnp.bfloat16)
    grad_logit = grad_step * jax.nn.sigmoid(step_logit)
    grad_logit_rounded = grad_logit.astype(jnp.bfloat16)
    grad_features = times_transposed(grad_values_rounded, projections[:, 0, :]) + times_transposed(
        grad_gates, projections[:, 1, :]
    )
    grad_features = (
        grad_features
        + times_transposed(grad_mapped, mixer_weight)
        + times_transposed(grad_logit_rounded, step_weight)
    )
    return (
        features,
        gated,
        grad_values_rounded,
        grad_gates,
        grad_mapped,
        grad_logit_rounded,
        jnp.sum(grad_logit, axis=0),
        grad_features,
    )


def norm_back(grad_features, normed, inv_scale, gain, residual):
    grad_normed = grad_features * gain[None, :]
    centred = grad_normed - normed * jnp.mean(grad_normed * normed, axis=1, keepdims=True)
    return (inv_scale * centred + residual, jnp.sum(grad_features * normed, axis=0))


def table_grad(bases, grad_embedded):
    return jnp.dot(one_hot(bases).T, grad_embedded, precision=HIGH)


def group_pieces(prepared):
    log_decay, step, values, mapped, grad_output = (
        prepared[8],
        prepared[7],
        prepared[3],
        prepared[5],
        prepared[11],
    )
    heads = step.shape[1]
    values_heads = heads_view(values, heads)
    grad_heads = heads_view(grad_output, heads)
    high = GROUP
    pieces = [
        (log_decay, step, values_heads, mapped[0:high, :STATE], mapped[0:high, STATE:], grad_heads)
    ]
    return pieces


def device_ends(pieces):
    decays, states, grads = ([], [], [])
    for piece in pieces:
        decay, state, grad_state = group_ends(*piece)
        decays.append(decay)
        states.append(state)
        grads.append(grad_state)
    total_decay = decays[0]
    total_state = states[0]
    total_grad = grads[-1]
    return (decays, states, grads, total_decay, total_state, total_grad)


def link(earlier, later):
    return tuple(
        (
            (first[0] * second[0], second[0][:, None, None] * first[1] + second[1])
            for first, second in zip(earlier, later)
        )
    )


def run_groups(pieces, initial, later, rate):
    count = len(pieces)
    current = initial
    initials = current
    laters = [later] * count
    current = later
    laters[0] = current
    results = [group_full(*pieces[0], initials, laters[0], rate)]
    length = count * GROUP
    output = jnp.concatenate([item[0] for item in results], axis=0).reshape(length, -1)
    grad_values = jnp.concatenate([item[1] for item in results], axis=0).reshape(length, -1)
    grad_step = jnp.concatenate([item[2] for item in results], axis=0)
    grad_rate = jnp.sum(jnp.stack([item[3] for item in results]), axis=0)
    grad_inflow = jnp.concatenate([item[4] for item in results], axis=0)
    grad_readout = jnp.concatenate([item[5] for item in results], axis=0)
    return (output, grad_values, grad_step, grad_rate, grad_inflow, grad_readout)


def body(
    base_ids,
    stream,
    cotangent,
    table,
    gain,
    projections,
    mixer_weight,
    step_weight,
    step_bias,
    rate,
):
    bases = base_ids[0]
    incoming = stream[0]
    upstream = cotangent[0]
    mirrored = complement(bases)[::-1]
    incoming_back = incoming[::-1]
    upstream_back = upstream[::-1]
    ahead = prepare(
        bases,
        incoming,
        upstream,
        table,
        gain,
        projections,
        mixer_weight,
        step_weight,
        step_bias,
        rate,
    )
    behind = prepare(
        mirrored,
        incoming_back,
        upstream_back,
        table,
        gain,
        projections,
        mixer_weight,
        step_weight,
        step_bias,
        rate,
    )
    ahead_pieces = group_pieces(ahead)
    behind_pieces = group_pieces(behind)
    ahead_ends = device_ends(ahead_pieces)
    behind_ends = device_ends(behind_pieces)
    heads = step_weight.shape[1]
    unit = (jnp.ones((heads,), jnp.float32), jnp.zeros((heads, STATE, HEAD_DIM), jnp.float32))
    rising = entering(
        ((ahead_ends[3], ahead_ends[4]), (behind_ends[3], behind_ends[5])),
        "ctx",
        link,
        (unit, unit),
        False,
    )
    falling = entering(
        ((behind_ends[3], behind_ends[4]), (ahead_ends[3], ahead_ends[5])),
        "ctx",
        link,
        (unit, unit),
        True,
    )
    ahead_terms = run_groups(ahead_pieces, rising[0][1], falling[1][1], rate)
    behind_terms = run_groups(behind_pieces, falling[0][1], rising[1][1], rate)
    ahead_done = finish(ahead, ahead_terms, projections, mixer_weight, step_weight)
    behind_done = finish(behind, behind_terms, projections, mixer_weight, step_weight)
    features_all = jnp.concatenate([ahead_done[0], behind_done[0]], axis=0)
    gated_all = jnp.concatenate([ahead_done[1], behind_done[1]], axis=0)
    values_all = jnp.concatenate([ahead_done[2], behind_done[2]], axis=0)
    gates_all = jnp.concatenate([ahead_done[3], behind_done[3]], axis=0)
    upstream_all = jnp.concatenate([upstream, upstream_back], axis=0)
    grad_projections = lax.psum_scatter(
        jnp.stack(
            [
                outer_sum(features_all, values_all),
                outer_sum(features_all, gates_all),
                outer_sum(upstream_all, gated_all),
            ],
            axis=1,
        ),
        ("ctx", "dp"),
        scatter_dimension=0,
        tiled=True,
    )
    grad_mixer = outer_sum(features_all, jnp.concatenate([ahead_done[4], behind_done[4]], axis=0))
    grad_step_weight = outer_sum(
        features_all, jnp.concatenate([ahead_done[5], behind_done[5]], axis=0)
    )
    grad_bias = ahead_done[6] + behind_done[6]
    grad_rate = ahead_terms[3] + behind_terms[3]
    width = gain.shape[0]
    columns = width // lax.axis_size("tp")
    first = lax.axis_index("tp") * columns
    ahead_features, behind_features = lax.psum((ahead_done[7], behind_done[7]), "tp")
    ahead_embedded, ahead_gain = norm_back(
        ahead_features, ahead[0], ahead[1], gain, upstream.astype(jnp.float32)
    )
    behind_embedded, behind_gain = norm_back(
        behind_features, behind[0], behind[1], gain, upstream_back.astype(jnp.float32)
    )
    whole_stream = ahead_embedded + behind_embedded[::-1]
    grad_stream = lax.dynamic_slice_in_dim(whole_stream, first, columns, 1)[None]
    grad_table = table_grad(bases, ahead_embedded) + table_grad(mirrored, behind_embedded)
    grad_gain = ahead_gain + behind_gain
    grad_mixer = lax.psum(grad_mixer, ("ctx", "tp", "dp"))
    grad_step_weight, grad_bias, grad_rate, grad_table, grad_gain = lax.psum(
        (grad_step_weight, grad_bias, grad_rate, grad_table, grad_gain), ("ctx", "dp")
    )
    return (
        grad_projections,
        grad_mixer,
        grad_step_weight,
        grad_bias,
        grad_rate,
        grad_table,
        grad_gain,
        grad_stream,
    )


def solution(mesh):
    return jax.shard_map(
        body,
        mesh=mesh,
        in_specs=(
            P("dp", "ctx"),
            P("dp", "ctx", None),
            P("dp", "ctx", None),
            P(),
            P(),
            P(None, None, "tp"),
            P(),
            P(None, "tp"),
            P("tp"),
            P("tp"),
        ),
        out_specs=(
            P(("ctx", "dp"), None, "tp"),
            P(),
            P(None, "tp"),
            P("tp"),
            P("tp"),
            P(),
            P(),
            P("dp", "ctx", "tp"),
        ),
        check_vma=False,
    )
```

profile of v0, /device:TPU:1, one launch (start us, length us, event | category | flops | bytes accessed | tf_op | source)
XLA Modules:
  0.0 1678.8 jit_solution(10117843756421623330)
XLA Ops:
  8.1 6.3 rev.24
  33.8 8.3 rev.30
  71.1 25.7 %all-gather.5 = f32[32,1,16]{2,1,0:T(1,128)} all-gather(f32[1,1,16]{2,1,0:T(1,128)S(1)} %bitcast.269), channel_id=1, replica_groups=mesh['ctx'=32,'tp'=2,'dp'=2] {'ctx'}, dimensions={0}, use_global_device_ids=true | all-gather | bytes 2112 | tf_op jit(solution)/shard_map/all_gather | solution.py:17
  96.8 34.9 %all-gather.4 = f32[32,1,16]{2,1,0:T(1,128)} all-gather(f32[1,1,16]{2,1,0:T(1,128)S(1)} %bitcast.270), channel_id=1, replica_groups=mesh['ctx'=32,'tp'=2,'dp'=2] {'ctx'}, dimensions={0}, use_global_device_ids=true | all-gather | bytes 2112 | tf_op jit(solution)/shard_map/all_gather | solution.py:17
  131.7 52.8 %all-gather.17.cloned.1.call-done = f32[512,64,64]{2,1,0:T(8,128)} async-done(((f32[16,64,64]{2,1,0:T(8,128)}), f32[512,64,64]{2,1,0:T(8,128)}) %all-gather.17.cloned.1.call-update) | async-done | bytes 8388624 | tf_op jit(solution)/shard_map/all_gather | solution.py:17
  184.5 87.9 %while.33 = (s32[]{:T(128)}, f32[16,64,64]{2,1,0:T(8,128)S(1)}, f32[16,64,64]{2,1,0:T(8,128)S(1)}, s32[]{:T(128)}, f32[32,16]{1,0:T(8,128)}, /*index=5*/f32[32,1...) while((s32[]{:T(128)}, f32[16,64,64]{2,1,0:T(8,128)S(1)}, ...), condition=%wide.region_5.6_spmd.clone, body=%wide.region_4.5_spmd.clone.sunk | while | flops 524292 | bytes 1573389 | solution.py:29
  275.5 7.1 fusion.90
  284.2 4.5 multiply_convert_fusion.3
  299.6 6.3 fusion.134
  305.9 11.9 rev.27
  325.6 8.6 multiply_reduce_fusion.2
  339.3 4.5 multiply_reduce_fusion.8
  348.0 18.2 %all-gather.13.cloned.1.call-done = f32[512,64,64]{2,1,0:T(8,128)} async-done(((f32[16,64,64]{2,1,0:T(8,128)}), f32[512,64,64]{2,1,0:T(8,128)}) %all-gather.13.cloned.1.call-update) | async-done | bytes 8388624 | tf_op jit(solution)/shard_map/all_gather | solution.py:17
  366.2 11.8 rev.29
  378.0 87.1 %while.32 = (s32[]{:T(128)}, f32[16,64,64]{2,1,0:T(8,128)S(1)}, f32[16,64,64]{2,1,0:T(8,128)S(1)}, s32[]{:T(128)}, f32[32,16]{1,0:T(8,128)}, /*index=5*/f32[32,1...) while((s32[]{:T(128)}, f32[16,64,64]{2,1,0:T(8,128)S(1)}, ...), condition=%wide.region_3.4_spmd.clone, body=%wide.region_2.3_spmd.clone.sunk | while | flops 524292 | bytes 1573389 | solution.py:29
  479.0 6.5 multiply_reduce_fusion.12
  487.2 5.9 fusion.84
  519.9 6.5 pad_maximum_fusion
  526.5 49.4 %all-reduce.10.cloned.1.call-done = (f32[256,1024]{1,0:T(8,128)}, f32[256,1024]{1,0:T(8,128)}) async-done(((f32[256,1024]{1,0:T(8,128)}, f32[256,1024]{1,0:T(8,128)}), (f32[256,1024]{1,0:T(8,128)}, f32[256,1024]{1,0:T(8,128)})) %all-reduce.10.cloned.1.call-update) | async-done | bytes 2097168 | tf_op jit(solution)/shard_map/psum | solution.py:354
  579.8 5.3 rev.31
  587.7 328.0 %all-reduce = (f32[16]{0:T(128)}, f32[16]{0:T(128)}, f32[5,1024]{1,0:T(8,128)}, f32[1024]{0:T(1024)}) all-reduce(f32[16]{0:T(128)S(1)} %add.297, f32[16]{0:T(128)S(1)} %negate_add_fusion, f32[5,1024]{1,0:T(8,128)S(1)} %convolution_add_fusion.10, f32[1024]{0:T(1024)S(1)} %add.308), channel_id=1, replica_groups=mesh['ctx'=32,'tp'=2,'dp'=2] {'ctx','dp'}, use_global_device_ids=true, to_apply=%region_27.28 | all-reduce | flops 6176 | bytes 49408 | tf_op jit(solution)/shard_map/psum | solution.py:366
  917.7 226.2 %all-reduce.8.cloned.1.call-done = f32[1024,16]{0,1:T(8,128)} async-done(((f32[1024,16]{0,1:T(8,128)}), f32[1024,16]{0,1:T(8,128)}) %all-reduce.8.cloned.1.call-update) | async-done | bytes 65552 | tf_op jit(solution)/shard_map/psum | solution.py:366
  1143.9 144.4 %all-reduce.6.cloned.1.call-done = f32[1024,128]{1,0:T(8,128)} async-done(((f32[1024,128]{1,0:T(8,128)}), f32[1024,128]{1,0:T(8,128)}) %all-reduce.6.cloned.1.call-update) | async-done | bytes 524304 | tf_op jit(solution)/shard_map/psum | solution.py:365
  1288.4 380.0 %reduce-scatter.2.cloned.1.call-done = f32[16,3,1024]{2,0,1:T(8,128)} async-done(((f32[1024,3,1024]{2,0,1:T(8,128)}), f32[16,3,1024]{2,0,1:T(8,128)}) %reduce-scatter.2.cloned.1.call-update) | async-done | bytes 196624 | tf_op jit(solution)/shard_map/reduce_scatter | solution.py:332
  (497 shorter events, 307.6 us)
Async XLA Ops:
  7.2 13.8 copy-start
  7.2 11.8 copy-start.35
  7.2 11.8 copy-start.78
  7.2 12.1 copy-start.81
  7.2 124.5 %all-gather.15.cloned.1.call-start = ((), (), s32[]{:S(2)}) async-start(), calls=%async_computation.6 | async-start | bytes 17301504 | tf_op jit(solution)/shard_map/all_gather | solution.py:17
  29.1 15.5 copy-start.11
  33.7 150.8 %all-gather.17.cloned.1.call-start = ((), (), s32[]{:S(2)}) async-start(), calls=%async_computation.7 | async-start | bytes 17301504 | tf_op jit(solution)/shard_map/all_gather | solution.py:17
  60.1 245.8 %all-gather.11.cloned.1.call-start = ((), (), s32[]{:S(2)}) async-start(), calls=%async_computation.4 | async-start | bytes 17301504 | tf_op jit(solution)/shard_map/all_gather | solution.py:17
  62.0 34.9 %copy-start.77 = (f32[16]{0:T(128)S(1)}, f32[16]{0:T(128)}, u32[]{:S(2)}) copy-start(f32[16]{0:T(128)} %get-tuple-element.384) | copy-start | bytes 196
  65.8 300.4 %all-gather.13.cloned.1.call-start = ((), (), s32[]{:S(2)}) async-start(), calls=%async_computation.5 | async-start | bytes 17301504 | tf_op jit(solution)/shard_map/all_gather | solution.py:17
  184.5 91.0 %copy-start.12 = (f32[256,16,64]{0,2,1:T(8,128)S(1)}, f32[256,16,64]{0,2,1:T(8,128)}, u32[]{:S(2)}) copy-start(f32[256,16,64]{0,2,1:T(8,128)} %copy-done.11) | copy-start | bytes 3145732
  294.9 281.0 %all-reduce.10.cloned.1.call-start = ((), (), s32[]{:S(2)}) async-start(), calls=%async_computation.8 | async-start | bytes 4194304 | tf_op jit(solution)/shard_map/psum | solution.py:354
  325.5 12.7 copy-start.23
  325.6 13.7 copy-start.2
  325.6 13.7 copy-start.47
  487.2 13.5 slice-start
  507.1 636.9 %all-reduce.8.cloned.1.call-start = ((), (), s32[]{:S(2)}) async-start(), calls=%async_computation.3 | async-start | bytes 131072 | tf_op jit(solution)/shard_map/psum | solution.py:366
  515.8 772.6 %all-reduce.6.cloned.1.call-start = ((), (), s32[]{:S(2)}) async-start(), calls=%async_computation.2 | async-start | bytes 1048576 | tf_op jit(solution)/shard_map/psum | solution.py:365
  517.1 1151.3 %reduce-scatter.2.cloned.1.call-start = ((), (), s32[]{:S(2)}) async-start(), calls=%async_computation.1 | async-start | bytes 12779520 | tf_op jit(solution)/shard_map/reduce_scatter | solution.py:332
  526.4 49.5 %copy-start.5 = (f32[256,1024]{1,0:T(8,128)S(1)}, f32[256,1024]{1,0:T(8,128)}, u32[]{:S(2)}) copy-start(f32[256,1024]{1,0:T(8,128)} %copy-done.4) | copy-start | bytes 3145732
  526.4 49.5 %copy-start.62 = (f32[1024]{0:T(1024)S(1)}, f32[1024]{0:T(1024)}, u32[]{:S(2)}) copy-start(f32[1024]{0:T(1024)} %param.18) | copy-start | bytes 12292
  526.4 49.5 %copy-start.64 = (f32[256]{0:T(256)S(1)}, f32[256]{0:T(256)}, u32[]{:S(2)}) copy-start(f32[256]{0:T(256)} %copy-done.63) | copy-start | bytes 3076
  526.4 51.1 %copy-start.7 = (f32[256,1024]{1,0:T(8,128)S(1)}, f32[256,1024]{1,0:T(8,128)}, u32[]{:S(2)}) copy-start(f32[256,1024]{1,0:T(8,128)} %copy-done.6) | copy-start | bytes 3145732
  526.4 51.1 %copy-start.72 = (f32[256]{0:T(256)S(1)}, f32[256]{0:T(256)}, u32[]{:S(2)}) copy-start(f32[256]{0:T(256)} %copy-done.71) | copy-start | bytes 3076
  (79 other events, 353.3 us)
Sparse Core Ops, SparseCore 0:
  33.9 76.4 all-gather.14
  112.6 71.8 all-gather.16
  186.8 72.0 all-gather.10
  295.0 71.1 all-gather.12
  507.2 68.6 all-reduce.9
  578.9 564.9 all-reduce.7
  1149.2 139.0 all-reduce.5
  1291.5 376.8 reduce-scatter.1
where the time goes:
time: 1700 us; the launch traced here: 1680 us
  waiting for transfers between devices  871 us (51%)
  blocking collectives  389 us (23%)
  local copies, waits for them, and re-layouts  163 us (10%)
  matrix products  124 us (7%)
  other arithmetic  114 us (7%)
    reduce_scatter x1, waiting for transfers between devices, body(): lax.psum_scatter(jnp.stack([outer_sum(features_all, values_all), outer_su...  380 us
    psum x1, blocking collectives, body(): lax.psum((grad_step_weight, grad_bias, grad_rate, grad_table, grad_gain),...  328 us
    psum x1, waiting for transfers between devices, body(): lax.psum((grad_step_weight, grad_bias, grad_rate, grad_table, grad_gain),...  226 us
    psum x1, waiting for transfers between devices, body(): grad_mixer = lax.psum(grad_mixer, ('ctx', 'tp', 'dp'))  144 us
    select_n x62, other arithmetic, step(): jnp.where(position < mine, new, old)  88 us
    mul x124, local copies, waits for them, and re-layouts, link(): second[0][:, None, None] * first[1] + second[1]  85 us
    all_gather x4, waiting for transfers between devices, entering(): pieces = jax.tree.map(lambda part: lax.all_gather(part, axis), value)  71 us
    all_gather x2, blocking collectives, entering(): pieces = jax.tree.map(lambda part: lax.all_gather(part, axis), value)  60.6 us
  transfers between devices with their start and end apart: 8, of which 6 were waited for; matrix products, arithmetic and copies ran while one was open for 14% of the time, Pallas kernels for 0%

commit v1 on v0

v1 whole, which is shorter than its diff:
```python
import functools

import jax
import jax.numpy as jnp
from jax import lax
from jax.experimental import pallas as pl
from jax.experimental.pallas import tpu as pltpu
from jax.sharding import PartitionSpec as P

EPS = 1e-05
HIGH = lax.Precision.HIGHEST
F32 = jnp.float32
BF16 = jnp.bfloat16
MESH = pl.DeviceIdType.MESH
BASES = 256
WIDTH = 1024
HEADS = 16
PAIRS = 8
STATE = 64


def nt(left, right):
    return lax.dot_general(left, right, (((1,), (1,)), ((), ())), preferred_element_type=F32)


def tn(left, right):
    return lax.dot_general(left, right, (((0,), (0,)), ((), ())), preferred_element_type=F32)


def dot(left, right):
    return jnp.dot(left, right, preferred_element_type=F32)


def exact(left, right):
    return jnp.dot(left, right, preferred_element_type=F32, precision=HIGH)


def scan_kernel(src, res, recv, out, send_a, recv_a, send_b, recv_b):
    me = lax.axis_index("ctx")
    count = 32

    barrier = pltpu.get_barrier_semaphore()

    def greet(s, c):
        pl.semaphore_signal(barrier, inc=1, device_id={"ctx": lax.rem(me + s, count)}, device_id_type=MESH)
        return c

    lax.fori_loop(1, count, greet, 0)
    pl.semaphore_wait(barrier, count - 1)

    def to_owner(s):
        there = lax.rem(me + s, count)
        return pltpu.make_async_remote_copy(
            src_ref=src.at[there], dst_ref=recv.at[s], send_sem=send_a.at[s], recv_sem=recv_a.at[s],
            device_id={"ctx": there}, device_id_type=MESH)

    def back(s):
        there = lax.rem(me + s, count)
        return pltpu.make_async_remote_copy(
            src_ref=out.at[there], dst_ref=res.at[me], send_sem=send_b.at[s], recv_sem=recv_b.at[s],
            device_id={"ctx": there}, device_id_type=MESH)

    def start_a(s, c):
        to_owner(s).start()
        return c

    def wait_a(s, c):
        to_owner(s).wait()
        return c

    def start_b(s, c):
        back(s).start()
        return c

    def wait_b(s, c):
        there = lax.rem(me + s, count)
        back(s).wait_send()
        return c

    lax.fori_loop(1, count, start_a, 0)
    recv[0] = src[me]
    lax.fori_loop(1, count, wait_a, 0)
    falling = me // 16

    def step(i, carry):
        at = i + falling * (count - 1 - 2 * i)
        out[at] = carry
        slot = lax.rem(me - at + count, count)
        decay = recv[slot, 64:65, :]
        return carry * decay + recv[slot, 0:64, :]

    lax.fori_loop(0, count, step, jnp.zeros((STATE, 128), F32))
    lax.fori_loop(1, count, start_b, 0)
    res[me] = out[me]
    lax.fori_loop(1, count, wait_b, 0)

    def arrived(s, c):
        frm = lax.rem(me - s + count, count)
        pltpu.make_async_remote_copy(
            src_ref=out.at[frm], dst_ref=res.at[frm], send_sem=send_b.at[s], recv_sem=recv_b.at[s],
            device_id={"ctx": frm}, device_id_type=MESH).wait_recv()
        return c

    lax.fori_loop(1, count, arrived, 0)


def exchange_states(src):
    return pl.pallas_call(
        scan_kernel,
        out_shape=jax.ShapeDtypeStruct((32, STATE, 128), F32),
        in_specs=[pl.BlockSpec(memory_space=pltpu.VMEM)],
        out_specs=pl.BlockSpec(memory_space=pltpu.VMEM),
        scratch_shapes=[
            pltpu.VMEM((32, 72, 128), F32),
            pltpu.VMEM((32, STATE, 128), F32),
            pltpu.SemaphoreType.DMA((32,)),
            pltpu.SemaphoreType.DMA((32,)),
            pltpu.SemaphoreType.DMA((32,)),
            pltpu.SemaphoreType.DMA((32,)),
        ],
        compiler_params=pltpu.CompilerParams(collective_id=0, has_side_effects=True, vmem_limit_bytes=32 << 20),
        name="exchange_states",
    )(src)


def block_kernel(v, g, gg, run, run_t, step, logit, inflow, readout, init, later, rate,
                 gv_out, gate_out, gated_out, mapped_out, logit_out, rate_out,
                 affinity, pairs, dd, dv, kk, gin, gread):
    d, j = pl.program_id(0), pl.program_id(1)
    sign = 1 - 2 * d
    rows = lax.broadcasted_iota(jnp.int32, (BASES, BASES), 0)
    columns = lax.broadcasted_iota(jnp.int32, (BASES, BASES), 1)
    order = (rows - columns) * sign
    inflow_b = inflow[0].astype(BF16)
    readout_b = readout[0].astype(BF16)

    @pl.when(j == 0)
    def _():
        affinity[...] = nt(readout_b, inflow_b)
        pairs[...] = jnp.zeros_like(pairs)
        dd[...] = jnp.zeros_like(dd)
        dv[...] = jnp.zeros_like(dv)
        kk[...] = jnp.zeros_like(kk)
        gin[...] = jnp.zeros_like(gin)
        gread[...] = jnp.zeros_like(gread)

    lane_head = lax.broadcasted_iota(jnp.int32, (HEADS, 128), 1) // 64 + 2 * j
    spread_out = (lax.broadcasted_iota(jnp.int32, (HEADS, 128), 0) == lane_head).astype(F32)
    lane_head_t = lax.broadcasted_iota(jnp.int32, (128, HEADS), 0) // 64 + 2 * j
    gather_in = (lax.broadcasted_iota(jnp.int32, (128, HEADS), 1) == lane_head_t).astype(F32)

    run_e = exact(run[0], spread_out)
    step_e = exact(step[0], spread_out)
    last = (BASES - 1) * (1 - d)
    at_last = lax.broadcasted_iota(jnp.int32, (BASES, 128), 0) == last
    final = jnp.sum(jnp.where(at_last, run_e, 0.0), axis=0, keepdims=True)
    head = jnp.exp(run_e)
    tail = jnp.exp(final - run_e)
    values, gates, grad_gated = v[...], g[...], gg[...]
    drive = step_e * values
    sigma = jax.nn.sigmoid(gates)
    swish = gates * sigma
    go = grad_gated * swish
    drive_b = drive.astype(BF16)
    go_b = go.astype(BF16)
    drive_r = drive_b.astype(F32)
    go_r = go_b.astype(F32)
    initial, after = init[0], later[0]
    initial_b, after_b = initial.astype(BF16), after.astype(BF16)
    carried = dot(readout_b, initial_b) * head
    pulled = dot(inflow_b, after_b) * tail
    low = lax.broadcasted_iota(jnp.int32, (BASES, 128), 1) < 64
    output, grad_drive = carried, pulled
    aff = affinity[...]
    total = pairs[...]
    for half in range(2):
        mine = low if half == 0 else jnp.logical_not(low)
        column = run_e[:, 64 * half:64 * half + 1]
        row = run_t[0, pl.ds(2 * j + half, 1), :]
        decay = jnp.exp(jnp.where(order >= 0, column - row, -1e30))
        mixing = (decay * aff).astype(BF16)
        drive_h = jnp.where(mine, drive_r, 0.0).astype(BF16)
        go_h = jnp.where(mine, go_r, 0.0).astype(BF16)
        output = output + dot(mixing, drive_h)
        grad_drive = grad_drive + tn(mixing, go_h)
        total = total + decay * nt(go_h, drive_b)
    pairs[...] = total
    dd[...] += exact(grad_drive * drive_r - go_r * output, gather_in)
    dv[...] += exact(grad_drive * values, gather_in)
    boundary = jnp.sum(go_r * carried, axis=0, keepdims=True) + jnp.exp(final) * jnp.sum(
        initial * after, axis=0, keepdims=True)
    kk[...] += exact(jnp.broadcast_to(boundary, (8, 128)), gather_in)
    gin[...] += nt((drive * tail).astype(BF16), after_b)
    gread[...] += nt((go * head).astype(BF16), initial_b)
    gv_out[...] = (step_e * grad_drive).astype(BF16)
    gate_out[...] = (grad_gated * output * sigma * (1.0 + gates * (1.0 - sigma))).astype(BF16)
    gated_out[...] = (output * swish).astype(BF16)

    @pl.when(j == PAIRS - 1)
    def _():
        pairs_b = pairs[...].astype(BF16)
        grad_in = gin[...] + tn(pairs_b, readout_b)
        grad_read = gread[...] + dot(pairs_b, inflow_b)
        mapped_out[...] = jnp.concatenate([grad_in, grad_read], axis=1).astype(BF16)
        before = (order > 0).astype(F32)
        grad_log = exact(before, dd[...]) + kk[0:1, :]
        grad_step = dv[...] - grad_log * rate[...]
        logit_out[0] = grad_step * jax.nn.sigmoid(logit[0])
        rate_out[0] = jnp.broadcast_to(-jnp.sum(grad_log * step[0], axis=0, keepdims=True), (8, HEADS))


def blocks(v, g, gg, run, run_t, step, logit, inflow, readout, states, rate):
    heads_of = pl.BlockSpec((BASES, 128), lambda d, j: (d, j))
    small = pl.BlockSpec((1, BASES, HEADS), lambda d, j: (d, 0, 0))
    mapped = pl.BlockSpec((1, BASES, STATE), lambda d, j: (d, 0, 0))
    wide = jax.ShapeDtypeStruct((2 * BASES, WIDTH), BF16)
    return pl.pallas_call(
        block_kernel,
        grid=(2, PAIRS),
        in_specs=[
            heads_of, heads_of, pl.BlockSpec((BASES, 128), lambda d, j: (0, j)),
            small, pl.BlockSpec((1, HEADS, BASES), lambda d, j: (d, 0, 0)), small, small, mapped, mapped,
            pl.BlockSpec((1, STATE, 128), lambda d, j: (16 * d + j, 0, 0)),
            pl.BlockSpec((1, STATE, 128), lambda d, j: (24 - 16 * d + j, 0, 0)),
            pl.BlockSpec((1, HEADS), lambda d, j: (0, 0)),
        ],
        out_specs=[
            heads_of, heads_of, heads_of,
            pl.BlockSpec((BASES, 128), lambda d, j: (d, 0)),
            small,
            pl.BlockSpec((1, 8, HEADS), lambda d, j: (d, 0, 0)),
        ],
        out_shape=[
            wide, wide, wide,
            jax.ShapeDtypeStruct((2 * BASES, 128), BF16),
            jax.ShapeDtypeStruct((2, BASES, HEADS), F32),
            jax.ShapeDtypeStruct((2, 8, HEADS), F32),
        ],
        scratch_shapes=[
            pltpu.VMEM((BASES, BASES), F32),
            pltpu.VMEM((BASES, BASES), F32),
            pltpu.VMEM((BASES, HEADS), F32),
            pltpu.VMEM((BASES, HEADS), F32),
            pltpu.VMEM((8, HEADS), F32),
            pltpu.VMEM((BASES, STATE), F32),
            pltpu.VMEM((BASES, STATE), F32),
        ],
        compiler_params=pltpu.CompilerParams(vmem_limit_bytes=32 << 20),
        name="blocks",
    )(v, g, gg, run, run_t, step, logit, inflow, readout, states, states, rate)


SEMS = 128


def sum_kernel(p0, p1, p2, small, both, grads_out, small_out, stream_out,
               acc, core_in, ring, mid, ring2, fin, dp_in,
               acc_e, core_in_e, ring_e, mid_e, ring2_e, fin_e, dp_in_e,
               tp_in, tp_in_e, piece, row, send, recv, local):
    ctx, tp, dp = lax.axis_index("ctx"), lax.axis_index("tp"), lax.axis_index("dp")
    core, y, z = ctx % 2, (ctx // 2) % 4, ctx // 8

    def at(zz, yy, cc):
        return {"ctx": (zz * 4 + yy) * 2 + cc}

    other = at(z, y, 1 - core)
    y_dev = [at(z, (y + i) % 4, core) for i in range(4)]
    z_dev = [at((z + i) % 4, y, core) for i in range(4)]
    dp_dev, tp_dev = {"dp": 1 - dp}, {"tp": 1 - tp}

    barrier = pltpu.get_barrier_semaphore()
    partners = [other, dp_dev, tp_dev] + y_dev[1:] + z_dev[1:]
    for partner in partners:
        pl.semaphore_signal(barrier, inc=1, device_id=partner, device_id_type=MESH)
    pl.semaphore_wait(barrier, len(partners))

    started = []

    def put(src, dst, device):
        i = len(started)
        copy = pltpu.make_async_remote_copy(
            src_ref=src, dst_ref=dst, send_sem=send.at[i], recv_sem=recv.at[i], device_id=device, device_id_type=MESH)
        copy.start()
        started.append(copy)
        return copy

    half = WIDTH // 2
    here, there = pl.multiple_of(tp * half, half), pl.multiple_of((1 - tp) * half, half)
    to_tp = put(both.at[:, pl.ds(there, half)], tp_in, tp_dev)

    jobs = [dict(src=small, width=128, first=0, stream=1, acc=acc_e, core=core_in_e, ring=ring_e, mid=mid_e,
                 ring2=ring2_e, fin=fin_e, dp=dp_in_e)]
    for k, array in enumerate((p0, p1, p2)):
        for stream in range(2):
            n = 2 * k + stream
            jobs.append(dict(src=array, width=256, first=512 * stream, stream=stream, acc=acc.at[n], core=core_in.at[n],
                             ring=ring.at[n], mid=mid.at[n], ring2=ring2.at[n], fin=fin.at[n], dp=dp_in.at[n]))

    for n, job in enumerate(jobs):
        job["core_copy"], job["own_copy"] = [], []
        for h in range(2):
            lanes = pl.ds(job["first"] + h * job["width"], job["width"])
            job["core_copy"].append(put(job["src"].at[:, :, 1 - core, :, lanes], job["core"].at[h], other))
            own = pltpu.make_async_copy(job["src"].at[:, :, core, :, lanes], job["acc"].at[h], local.at[2 * n + h])
            own.start()
            job["own_copy"].append(own)

    def chunk(ref, h, c, stream, stage):
        if stream == 0 and stage == 1:
            return ref.at[h, :, c]
        return ref.at[h, c]

    def place(job, stage):
        over_y = (job["stream"] == 0) == (stage == 1)
        return (y, y_dev) if over_y else (z, z_dev)

    def ring_start(job, ref, buffer, stage):
        p, dev = place(job, stage)
        s = job["stream"]
        job["m1"] = put(chunk(ref, 0, (p + 2) % 4, s, stage), buffer.at[0], dev[1])
        job["m1p"] = put(chunk(ref, 1, (p + 2) % 4, s, stage), buffer.at[1], dev[3])
        job["m2"] = put(chunk(ref, 1, (p + 1) % 4, s, stage), buffer.at[2], dev[1])
        job["m2p"] = put(chunk(ref, 0, (p + 3) % 4, s, stage), buffer.at[3], dev[3])

    def ring_middle(job, ref, buffer, stage):
        p, dev = place(job, stage)
        s = job["stream"]
        job["m1"].wait_recv()
        up = chunk(ref, 0, (p + 1) % 4, s, stage)
        up[...] = up[...] + buffer[0]
        job["m3"] = put(up, buffer.at[4], dev[1])
        job["m1p"].wait_recv()
        down = chunk(ref, 1, (p + 3) % 4, s, stage)
        down[...] = down[...] + buffer[1]
        job["m3p"] = put(down, buffer.at[5], dev[3])

    def ring_end(job, ref, buffer, stage, into):
        p, dev = place(job, stage)
        s = job["stream"]
        for name in ("m2", "m2p", "m3", "m3p"):
            job[name].wait_recv()
        into[0] = chunk(ref, 0, p, s, stage)[...] + buffer[3] + buffer[4]
        into[1] = chunk(ref, 1, p, s, stage)[...] + buffer[2] + buffer[5]

    for job in jobs:
        for h in range(2):
            job["own_copy"][h].wait()
            job["core_copy"][h].wait_recv()
            job["acc"][h] = job["acc"][h] + job["core"][h]
        ring_start(job, job["acc"], job["ring"], 1)
    for job in jobs:
        ring_middle(job, job["acc"], job["ring"], 1)
    for job in jobs:
        ring_end(job, job["acc"], job["ring"], 1, job["mid"])
        ring_start(job, job["mid"], job["ring2"], 2)
    for job in jobs:
        ring_middle(job, job["mid"], job["ring2"], 2)
    mine = pl.ds(pl.multiple_of(16 * dp, 16), 16)
    yours = pl.ds(pl.multiple_of(16 * (1 - dp), 16), 16)
    for job in jobs:
        ring_end(job, job["mid"], job["ring2"], 2, job["fin"])
        job["dp_copy"] = put(job["fin"].at[:, yours, :], job["dp"], dp_dev)

    job = jobs[0]
    job["dp_copy"].wait_recv()
    for h in range(2):
        piece[0, mine, 128 * h:128 * h + 128] = job["fin"][h, mine, :] + job["dp"][h]
    over_tp = put(piece.at[0, mine, :], tp_in_e, tp_dev)
    for k in range(3):
        for stream in range(2):
            done = jobs[1 + 2 * k + stream]
            done["dp_copy"].wait_recv()
            for h in range(2):
                first = 512 * stream + 256 * h
                grads_out[k, :, first:first + 256] = done["fin"][h, mine, :] + done["dp"][h]
    over_tp.wait_recv()
    piece[1, mine, :] = piece[0, mine, :] + tp_in_e[...]
    put(piece.at[1, mine, :], piece.at[1, mine, :], dp_dev).wait_recv()
    row[y] = piece[1]
    for copy in [put(piece.at[1], row.at[y], dev) for dev in y_dev[1:]]:
        copy.wait_recv()
    small_out[z, :, core] = row[...]
    for copy in [put(row, small_out.at[z, :, core], dev) for dev in z_dev[1:]]:
        copy.wait_recv()
    put(small_out.at[:, :, core], small_out.at[:, :, core], other).wait_recv()

    to_tp.wait_recv()
    stream_out[...] = both[:, pl.ds(here, half)] + tp_in[...]
    for copy in started:
        copy.wait_send()


def sum_all(p0, p1, p2, small, both):
    def cut(array):
        return array.reshape(4, 4, 2, 32, array.shape[1])

    vmem, anywhere = pl.BlockSpec(memory_space=pltpu.VMEM), pl.BlockSpec(memory_space=pl.ANY)

    def buffers(lead, width):
        return [pltpu.VMEM(lead + shape + (32, width), F32) for shape in ((2, 4, 4), (2, 4, 4), (6, 4), (2, 4), (6,), (2,))
                ] + [pltpu.VMEM(lead + (2, 16, width), F32)]

    return pl.pallas_call(
        sum_kernel,
        out_shape=[
            jax.ShapeDtypeStruct((3, 16, WIDTH), F32),
            jax.ShapeDtypeStruct((4, 4, 2, 32, 256), F32),
            jax.ShapeDtypeStruct((BASES, WIDTH // 2), F32),
        ],
        in_specs=[anywhere] * 4 + [vmem],
        out_specs=[vmem] * 3,
        scratch_shapes=buffers((6,), 256) + buffers((), 128) + [
            pltpu.VMEM((BASES, WIDTH // 2), F32),
            pltpu.VMEM((16, 256), F32),
            pltpu.VMEM((2, 32, 256), F32),
            pltpu.VMEM((4, 32, 256), F32),
            pltpu.SemaphoreType.DMA((SEMS,)),
            pltpu.SemaphoreType.DMA((SEMS,)),
            pltpu.SemaphoreType.DMA((14,)),
        ],
        compiler_params=pltpu.CompilerParams(collective_id=1, has_side_effects=True, vmem_limit_bytes=48 << 20),
        name="sum_all",
    )(cut(p0), cut(p1), cut(p2), cut(small), both)


def body(base_ids, stream, cotangent, table, gain, projections, mixer_weight, step_weight, step_bias, rate):
    bases = base_ids[0]
    letters = jnp.arange(5, dtype=jnp.int32)
    own = bases[:, None] == letters[None, :]
    paired = jnp.where(bases == 4, 4, 3 - bases)[:, None] == letters[None, :]
    incoming = stream[0].astype(F32)
    upstream = cotangent[0]
    w = jnp.transpose(projections, (1, 0, 2))

    def picked(hot):
        return sum(jnp.where(hot[:, k:k + 1], table[k][None, :], 0.0) for k in range(5))

    embedded = jnp.concatenate([incoming + picked(own), incoming + picked(paired)], axis=0)
    inv_scale = lax.rsqrt(jnp.mean(embedded * embedded, axis=1, keepdims=True) + EPS)
    normed = embedded * inv_scale
    features = (normed * gain[None, :]).astype(BF16)
    v = dot(features, w[0])
    g = dot(features, w[1])
    gg = dot(upstream, w[2])
    mapped = dot(features, mixer_weight)
    logit = (dot(features, step_weight) + step_bias[None, :]).reshape(2, BASES, HEADS)
    step = jax.nn.softplus(logit)
    log_decay = -step * rate
    index = lax.broadcasted_iota(jnp.int32, (BASES, BASES), 0) - lax.broadcasted_iota(jnp.int32, (BASES, BASES), 1)
    run = jnp.stack([exact((index >= 0).astype(F32), log_decay[0]), exact((index <= 0).astype(F32), log_decay[1])])
    final = jnp.stack([run[0, BASES - 1], run[1, 0]])
    tail = jnp.exp(final[:, None, :] - run)
    head = jnp.exp(run)
    inflow, readout = mapped[:, :STATE].reshape(2, BASES, STATE), mapped[:, STATE:].reshape(2, BASES, STATE)

    def wide(small):
        return jnp.repeat(small, 64, axis=1)

    def pieces(d):
        rows = slice(BASES * d, BASES * (d + 1))
        decay = jnp.broadcast_to(wide(jnp.exp(final[d])[None]).reshape(PAIRS, 1, 128), (PAIRS, 8, 128))
        state = tn(inflow[d].astype(BF16), (v[rows] * wide(step[d] * tail[d])).astype(BF16))
        grad = tn(readout[d].astype(BF16), (gg * jax.nn.silu(g[rows]) * wide(head[d])).astype(BF16))
        return [jnp.concatenate([a.reshape(STATE, PAIRS, 128).transpose(1, 0, 2), decay], axis=1) for a in (state, grad)]

    (s0, g0), (s1, g1) = pieces(0), pieces(1)
    states = exchange_states(jnp.concatenate([s0, g1, s1, g0], axis=0))
    gv, gate, gated, gm, glogit, grate = blocks(
        v, g, gg, run, jnp.transpose(run, (0, 2, 1)), step, logit, inflow, readout, states, rate[None])

    glogit_b = glogit.reshape(2 * BASES, HEADS).astype(BF16)
    gf = nt(gv, w[0]) + nt(gate, w[1]) + nt(gm, mixer_weight) + nt(glogit_b, step_weight)
    gn = gf * gain[None, :]
    ge = inv_scale * (gn - normed * jnp.mean(gn * normed, axis=1, keepdims=True))
    ge = ge + 0.5 * jnp.concatenate([upstream, upstream], axis=0).astype(F32)
    both = ge[:BASES] + ge[BASES:]
    ggain = jnp.sum(gf * normed, axis=0)
    hot = jnp.concatenate([own, paired], axis=0).astype(F32)
    gtable = lax.dot_general(ge, hot, (((0,), (0,)), ((), ())), preferred_element_type=F32, precision=HIGH)
    tp = lax.axis_index("tp")
    gstep = tn(features, glogit_b)
    heads_at = HEADS * tp
    gbias = jnp.sum(glogit, axis=(0, 1))
    grate = grate[0, 0] + grate[1, 0]
    rest = jnp.concatenate([ggain[:, None], gtable, jnp.zeros((WIDTH, 128 - 38), F32)], axis=1)
    scalars = jnp.zeros((32, 2), F32)
    scalars = lax.dynamic_update_slice(scalars, jnp.stack([gbias, grate], axis=1), (heads_at, 0))
    steps = lax.dynamic_update_slice(jnp.zeros((WIDTH, 32), F32), gstep, (0, heads_at))
    rest = jnp.concatenate([
        steps, ggain[:, None], gtable, jnp.pad(scalars, ((0, WIDTH - 32), (0, 0))), jnp.zeros((WIDTH, 88), F32)], axis=1)
    small = jnp.concatenate([tn(features, gm), rest], axis=1)
    up2 = jnp.concatenate([upstream, upstream], axis=0)
    grads, small, stream_grad = sum_all(tn(features, gv), tn(features, gate), tn(up2, gated), small, both)
    small = small.reshape(WIDTH, 256)
    heads = lax.dynamic_slice(small, (0, 128 + heads_at), (WIDTH, HEADS))
    pair = lax.dynamic_slice(small, (heads_at, 128 + 38), (HEADS, 2))
    return (
        jnp.transpose(grads, (1, 0, 2)),
        small[:, :128],
        heads,
        pair[:, 0],
        pair[:, 1],
        jnp.transpose(small[:, 161:166]),
        small[:, 160],
        stream_grad[None],
    )


def solution(mesh):
    return jax.shard_map(
        body,
        mesh=mesh,
        in_specs=(
            P("dp", "ctx"),
            P("dp", "ctx", None),
            P("dp", "ctx", None),
            P(),
            P(),
            P(None, None, "tp"),
            P(),
            P(None, "tp"),
            P("tp"),
            P("tp"),
        ),
        out_specs=(
            P(("ctx", "dp"), None, "tp"),
            P(),
            P(None, "tp"),
            P("tp"),
            P("tp"),
            P(),
            P(),
            P("dp", "ctx", "tp"),
        ),
        check_vma=False,
    )
```

time: 1700 us -> 233 us (0.14); the launches traced: 1680 us -> 232 us
  waiting for transfers between devices: 871 us -> 0 us
  blocking collectives: 389 us -> 0 us
  Pallas kernels: 0 us -> 135 us
  local copies, waits for them, and re-layouts: 163 us -> 49.8 us
  other arithmetic: 114 us -> 9.65 us
  matrix products: 124 us -> 36.5 us
    psum x3 -> x0, waiting for transfers between devices: 420 us -> none  [the longest x1 226 us: body(): lax.psum((grad_step_weight, grad_bias, grad_rate, grad_table, grad_gain),...]
    reduce_scatter x1 -> x0, waiting for transfers between devices: 380 us -> none  [body(): lax.psum_scatter(jnp.stack([outer_sum(features_all, values_all), outer_su...]
    psum x1 -> x0, blocking collectives: 328 us -> none  [body(): lax.psum((grad_step_weight, grad_bias, grad_rate, grad_table, grad_gain),...]
    pallas_call x0 -> x3, Pallas kernels: none -> 135 us  [the longest x1 68.4 us: sum_all(): pl.pallas_call(sum_kernel, out_shape=[jax.ShapeDtypeStruct((3, 16, WIDTH)...]
    mul x126 -> x2, local copies, waits for them, and re-layouts: 88.1 us -> 0.12 us  [pieces(): step[d] * tail[d]]
    select_n x63 -> x2, other arithmetic: 88.7 us -> 0.89 us  [the longest x1 0.73 us: body(): paired = jnp.where(bases == 4, 4, 3 - bases)[:, None] == letters[None, :]]
    dot_general x57 -> x21, matrix products: 117 us -> 36.5 us  [the longest x9 15.8 us: tn(): lax.dot_general(left, right, (((0,), (0,)), ((), ())), preferred_element_...]
    all_gather x4 -> x0, waiting for transfers between devices: 71 us -> none  [entering(): pieces = jax.tree.map(lambda part: lax.all_gather(part, axis), value)]
  transfers between devices with their start and end apart: 8 -> 0, of which waited for: 6 -> 0; matrix products, arithmetic and copies ran while one was open for 14% -> 0% of each run, Pallas kernels for 0% -> 0%
where the time goes in v1:
time: 233 us; the launch traced here: 232 us
  Pallas kernels  135 us (58%)
  local copies, waits for them, and re-layouts  49.8 us (21%)
  matrix products  36.5 us (16%)
  other arithmetic  9.65 us (4%)
    pallas_call x1, Pallas kernels, sum_all(): pl.pallas_call(sum_kernel, out_shape=[jax.ShapeDtypeStruct((3, 16, WIDTH)...  68.4 us
    pallas_call x1, Pallas kernels, exchange_states(): pl.pallas_call(scan_kernel, out_shape=jax.ShapeDtypeStruct((32, STATE, 12...  41.9 us
    pallas_call x1, Pallas kernels, blocks(): pl.pallas_call(block_kernel, grid=(2, PAIRS), in_specs=[heads_of, heads_o...  24.7 us
    unnamed x94, local copies, waits for them, and re-layouts  19 us
    dot_general x9, matrix products, tn(): lax.dot_general(left, right, (((0,), (0,)), ((), ())), preferred_element_...  15.8 us
    dot_general x5, matrix products, dot(): return jnp.dot(left, right, preferred_element_type=F32)  9.89 us
    dot_general x4, matrix products, nt(): lax.dot_general(left, right, (((1,), (1,)), ((), ())), preferred_element_...  7.68 us
    reshape x4, local copies, waits for them, and re-layouts, wide(): return jnp.repeat(small, 64, axis=1)  6.83 us

profile of v1, /device:TPU:1, one launch (start us, length us, event | category | flops | bytes accessed | tf_op | source)
XLA Modules:
  0.0 232.1 jit_solution(6435770953142078247)
XLA Ops:
  3.1 2.1 convert_add_fusion.1
  11.1 1.6 copy.85
  13.9 2.6 %copy.90 = f32[256,1024]{1,0:T(8,128)} copy(f32[256,1024]{0,1:T(8,128)} %bitcast.144) | data formatting | bytes 2097152 | tf_op jit(solution)/shard_map/reshape | solution.py:457
  16.5 2.9 %fusion.2.v = f32[512,1024]{1,0:T(8,128)S(1)} fusion(bf16[512,1024]{1,0:T(8,128)(2,1)S(1)} %multiply_convert_fusion, bf16[3,1024,1024]{2,1,0:T(8,128)(2,1)} %bitcast.170), kind=kOutput, calls=%fused_computation.12 | convolution fusion | flops 1073741824 | bytes 5242880 | tf_op jit(solution)/shard_map/dot_general | solution.py:31
  24.5 1.3 copy.87
  27.3 2.9 %fusion.4.g = f32[512,1024]{1,0:T(8,128)S(1)} fusion(bf16[512,1024]{1,0:T(8,128)(2,1)S(1)} %copy-done.22, bf16[3,1024,1024]{2,1,0:T(8,128)(2,1)} %bitcast.171), kind=kOutput, calls=%fused_computation.14 | convolution fusion | flops 1073741824 | bytes 5242880 | tf_op jit(solution)/shard_map/dot_general | solution.py:31
  30.2 2.5 %fusion.gg = f32[256,1024]{1,0:T(8,128)S(1)} fusion(bf16[3,1024,1024]{2,1,0:T(8,128)(2,1)} %bitcast.172, bf16[1,256,1024]{2,1,0:T(8,128)(2,1)S(1)} %copy-done.35), kind=kOutput, calls=%fused_computation.1 | convolution fusion | flops 536870912 | bytes 3670016 | tf_op jit(solution)/shard_map/dot_general | solution.py:31
  34.8 2.0 convolution_bitcast_fusion.2
  40.3 41.9 %exchange_states.1.init.later = f32[32,64,128]{2,1,0:T(8,128)S(1)} custom-call(f32[32,72,128]{2,1,0:T(8,128)S(1)} %maximum_maximum_fusion.src), custom_call_target="tpu_custom_call" | custom-call | tf_op jit(solution)/shard_map/exchange_states/pallas_call | solution.py:108
  83.1 1.6 fusion.33
  84.7 1.8 copy.80
  87.3 1.6 copy-done.3
  95.7 24.7 %blocks.1 = (bf16[512,1024]{1,0:T(8,128)(2,1)S(1)}, bf16[512,1024]{1,0:T(8,128)(2,1)S(1)}, bf16[512,1024]{1,0:T(8,128)(2,1)S(1)}, bf16[512,128]{1,0:T(8,128)(2,1...) custom-call(f32[512,1024]{1,0:T(8,128)S(1)} %copy-done.3, f32[512,1024]{1,0:T(8,128)S(1)} %fusion.4.g, ...), custom_call_target="tpu_custom_call" | custom-call | tf_op jit(solution)/shard_map/blocks/pallas_call | solution.py:217
  124.5 3.3 %fusion.1 = f32[512,1024]{1,0:T(8,128)S(1)} fusion(bf16[512,1024]{1,0:T(8,128)(2,1)} %copy-done.13, bf16[3,1024,1024]{2,1,0:T(8,128)(2,1)} %bitcast.173), kind=kOutput, calls=%fused_computation.11 | convolution fusion | flops 1073741824 | bytes 5242880 | tf_op jit(solution)/shard_map/dot_general | solution.py:23
  127.8 2.9 %fusion.3 = f32[512,1024]{1,0:T(8,128)S(1)} fusion(bf16[512,1024]{1,0:T(8,128)(2,1)S(1)} %copy-done.16, bf16[3,1024,1024]{2,1,0:T(8,128)(2,1)} %bitcast.174), kind=kOutput, calls=%fused_computation.13 | convolution fusion | flops 1073741824 | bytes 5242880 | tf_op jit(solution)/shard_map/dot_general | solution.py:23
  133.9 1.3 copy-done.28
  135.3 2.6 %fusion.21 = f32[1024,5]{1,0:T(8,128)} fusion(f32[512,1024]{1,0:T(8,128)S(1)} %multiply_add_fusion, pred[256,5]{0,1:T(8,128)(4,1)S(1)} %iota_compare_fusion, pred[256,5]{0,1:T(8,128)(4,1)S(1)} %iota_compare_fusion.1), kind=kOutput, calls=%fused_computation.61 | convolution fusion | flops 31459840 | bytes 2120192 | tf_op jit(solution)/shard_map/dot_general | solution.py:479
  139.5 2.3 dynamic_update_slice.6
  144.0 2.2 concatenate.52.small
  146.2 1.7 slice_add_fusion.both
  147.9 3.2 %fusion.37 = f32[1024,1024]{1,0:T(8,128)} fusion(bf16[512,1024]{1,0:T(8,128)(2,1)S(1)} %copy-done.23, bf16[512,1024]{1,0:T(8,128)(2,1)S(1)} %copy-done.16), kind=kOutput, calls=%fused_computation.103 | convolution fusion | flops 1073741824 | bytes 6291456 | tf_op jit(solution)/shard_map/dot_general | solution.py:27
  151.2 3.3 %fusion.36 = f32[1024,1024]{1,0:T(8,128)} fusion(bf16[512,1024]{1,0:T(8,128)(2,1)S(1)} %copy-done.23, bf16[512,1024]{1,0:T(8,128)(2,1)S(1)} %copy-done.14), kind=kOutput, calls=%fused_computation.102 | convolution fusion | flops 1073741824 | bytes 6291456 | tf_op jit(solution)/shard_map/dot_general | solution.py:27
  154.5 3.3 %fusion.8 = f32[1024,1024]{1,0:T(8,128)} fusion(bf16[512,1024]{1,0:T(8,128)(2,1)S(1)} %copy-done.20, bf16[256,1024]{1,0:T(8,128)(2,1)S(1)} %bitcast.158), kind=kOutput, calls=%fused_computation.34 | convolution fusion | flops 1075838976 | bytes 5767168 | tf_op jit(solution)/shard_map/dot_general | solution.py:27
  157.7 68.4 %sum_all.1 = (f32[3,16,1024]{2,1,0:T(8,128)S(1)}, f32[4,4,2,32,256]{4,3,2,1,0:T(8,128)S(1)}, f32[256,512]{1,0:T(8,128)S(1)}) custom-call(f32[4,4,2,32,1024]{4,3,2,1,0:T(8,128)} %bitcast.141, f32[4,4,2,32,1024]{4,3,2,1,0:T(8,128)} %bitcast.140, f32[4,4,2,32,1024]{4,3,2,1,0:T(8,128)} %bitcast.142, f32[4,4,2,32,256]{4,3,2,1,0:T(8,128)S(1)} %concatenate.52.small, ...), custom_call_target="tpu_custom_call" | custom-call | tf_op jit(solution)/shard_map/sum_all/pallas_call | solution.py:403
  (162 shorter events, 46.9 us)
Async XLA Ops:
  0.6 20.4 %copy-start = (bf16[1024,128]{1,0:T(8,128)(2,1)S(1)}, bf16[1024,128]{1,0:T(8,128)(2,1)}, u32[]{:S(2)}) copy-start(bf16[1024,128]{1,0:T(8,128)(2,1)} %param.16) | copy-start | bytes 786436
  3.1 2.4 %copy-start.41 = (f32[1024]{0:T(1024)S(1)}, f32[1024]{0:T(1024)}, u32[]{:S(2)}) copy-start(f32[1024]{0:T(1024)} %param.14) | copy-start | bytes 12292
  5.5 1.6 copy-start.18
  6.5 14.4 %copy-start.21 = (bf16[512,1024]{1,0:T(8,128)(2,1)}, bf16[512,1024]{1,0:T(8,128)(2,1)S(1)}, u32[]{:S(2)}) copy-start(bf16[512,1024]{1,0:T(8,128)(2,1)S(1)} %multiply_convert_fusion) | copy-start | bytes 3145732
  7.1 5.6 %copy-start.8 = (f32[512,16]{1,0:T(8,128)}, f32[512,16]{1,0:T(8,128)S(1)}, u32[]{:S(2)}) copy-start(f32[512,16]{1,0:T(8,128)S(1)} %copy.79) | copy-start | bytes 98308
  7.3 5.5 %copy-start.6 = (f32[2,256,16]{2,1,0:T(8,128)}, f32[2,256,16]{2,1,0:T(8,128)S(1)}, u32[]{:S(2)}) copy-start(f32[2,256,16]{2,1,0:T(8,128)S(1)} %get-tuple-element.56.step) | copy-start | bytes 98308
  16.5 3.0 %copy-start.29 = (f32[256,1024]{1,0:T(8,128)S(1)}, f32[256,1024]{1,0:T(8,128)}, u32[]{:S(2)}) copy-start(f32[256,1024]{1,0:T(8,128)} %copy.90) | copy-start | bytes 3145732
  22.2 3.7 %copy-start.33 = (bf16[512,128]{0,1:T(8,128)(2,1)}, bf16[512,128]{0,1:T(8,128)(2,1)S(1)}, u32[]{:S(2)}) copy-start(bf16[512,128]{0,1:T(8,128)(2,1)S(1)} %get-tuple-element.69) | copy-start | bytes 393220
  25.8 1.4 copy-start.22
  27.3 2.9 %copy-start.35 = (bf16[1,256,1024]{2,1,0:T(8,128)(2,1)S(1)}, bf16[1,256,1024]{2,1,0:T(8,128)(2,1)}, u32[]{:S(2)}) copy-start(bf16[1,256,1024]{2,1,0:T(8,128)(2,1)} %param.12) | copy-start | bytes 1572868
  30.2 2.5 %copy-start.30 = (f32[256,1024]{1,0:T(8,128)S(1)}, f32[256,1024]{1,0:T(8,128)}, u32[]{:S(2)}) copy-start(f32[256,1024]{1,0:T(8,128)} %copy.87) | copy-start | bytes 3145732
  30.2 2.5 %copy-start.31 = (f32[256,1024]{1,0:T(8,128)S(1)}, f32[256,1024]{1,0:T(8,128)}, u32[]{:S(2)}) copy-start(f32[256,1024]{1,0:T(8,128)} %copy.92) | copy-start | bytes 3145732
  32.7 2.1 copy-start.34
  39.1 43.2 %copy-start.40 = (f32[2,256,16]{1,2,0:T(8,128)S(1)}, f32[2,256,16]{1,2,0:T(8,128)}, u32[]{:S(2)}) copy-start(f32[2,256,16]{1,2,0:T(8,128)} %get-tuple-element.63) | copy-start | bytes 98308
  87.3 1.6 copy-start.3
  124.5 3.3 %copy-start.16 = (bf16[512,1024]{1,0:T(8,128)(2,1)S(1)}, bf16[512,1024]{1,0:T(8,128)(2,1)}, u32[]{:S(2)}) copy-start(bf16[512,1024]{1,0:T(8,128)(2,1)} %copy-done.15) | copy-start | bytes 3145732
  130.7 1.5 copy-start.27
  130.7 1.5 copy-start.39
  130.7 1.5 copy-start.43
  135.3 3.8 %copy-start.23 = (bf16[512,1024]{1,0:T(8,128)(2,1)S(1)}, bf16[512,1024]{1,0:T(8,128)(2,1)}, u32[]{:S(2)}) copy-start(bf16[512,1024]{1,0:T(8,128)(2,1)} %copy-done.21) | copy-start | bytes 3145732
  147.9 3.2 %copy-start.14 = (bf16[512,1024]{1,0:T(8,128)(2,1)S(1)}, bf16[512,1024]{1,0:T(8,128)(2,1)}, u32[]{:S(2)}) copy-start(bf16[512,1024]{1,0:T(8,128)(2,1)} %copy-done.13) | copy-start | bytes 3145732
  151.2 3.3 %copy-start.20 = (bf16[512,1024]{1,0:T(8,128)(2,1)S(1)}, bf16[512,1024]{1,0:T(8,128)(2,1)}, u32[]{:S(2)}) copy-start(bf16[512,1024]{1,0:T(8,128)(2,1)} %copy-done.19) | copy-start | bytes 3145732
  151.2 3.3 %copy-start.37 = (bf16[1,256,1024]{2,1,0:T(8,128)(2,1)S(1)}, bf16[1,256,1024]{2,1,0:T(8,128)(2,1)}, u32[]{:S(2)}) copy-start(bf16[1,256,1024]{2,1,0:T(8,128)(2,1)} %param.12) | copy-start | bytes 1572868
  226.3 5.8 %copy-start.1 = (bf16[1024,128]{1,0:T(8,128)(2,1)S(1)}, bf16[1024,128]{1,0:T(8,128)(2,1)}, u32[]{:S(2)}) copy-start(bf16[1024,128]{1,0:T(8,128)(2,1)} %param.16) | copy-start | bytes 786436
  (21 other events, 22.8 us)

commit v2 on v1

v2 whole, which is shorter than its diff:
```python
import functools

import jax
import jax.numpy as jnp
from jax import lax
from jax.experimental import pallas as pl
from jax.experimental.pallas import tpu as pltpu
from jax.sharding import PartitionSpec as P

EPS = 1e-05
HIGH = lax.Precision.HIGHEST
F32 = jnp.float32
BF16 = jnp.bfloat16
MESH = pl.DeviceIdType.MESH
BASES = 256
WIDTH = 1024
HEADS = 16
PAIRS = 8
STATE = 64


def nt(left, right):
    return lax.dot_general(left, right, (((1,), (1,)), ((), ())), preferred_element_type=F32)


def tn(left, right):
    return lax.dot_general(left, right, (((0,), (0,)), ((), ())), preferred_element_type=F32)


def dot(left, right):
    return jnp.dot(left, right, preferred_element_type=F32)


def exact(left, right):
    return jnp.dot(left, right, preferred_element_type=F32, precision=HIGH)


def split3(x):
    a = x.astype(BF16).astype(F32)
    b = (x - a).astype(BF16).astype(F32)
    return a, b, x - a - b


def split2(x):
    a = x.astype(BF16)
    return a, (x - a.astype(F32)).astype(BF16)


def summed3(x, ones):
    r = dot(jnp.concatenate(split3(x), axis=0).astype(BF16), ones)
    n = x.shape[0]
    return r[0:n] + r[n:2 * n] + r[2 * n:3 * n]


def iota(shape, dim):
    return lax.broadcasted_iota(jnp.int32, shape, dim)


def spreads(j):
    r, c = iota((128, 256), 0), iota((128, 256), 1)
    kind = (r >= 48).astype(jnp.int32) + (r >= 96).astype(jnp.int32)
    return jnp.logical_and(kind == c // 128, (r & 15) == 2 * j + (c & 127) // 64).astype(F32).astype(BF16)


def gathers(j, base):
    r, c = iota((128, 128), 0), iota((128, 128), 1)
    return (c == base + 2 * j + r // 64).astype(F32).astype(BF16)


def front_kernel(base, x, up, table, gain, w, mw, swt, bias, rate,
                 f_out, normed_out, inv_out, gv_out, gate_out, gated_out, mapped_out, logit_out, rate_out,
                 wv, tab, v, g, gg, quant, maps, maps_t, logit_t, step_t, drive_b, go_b, out, gd, pairs, acc, kk,
                 src, recv, scanned, res, wsem, send_a, recv_a, send_b, recv_b):
    me = lax.axis_index("ctx")
    count = 32
    barrier = pltpu.get_barrier_semaphore()

    def greet(s, c):
        pl.semaphore_signal(barrier, inc=1, device_id={"ctx": lax.rem(me + s, count)}, device_id_type=MESH)
        return c

    lax.fori_loop(1, count, greet, 0)
    copies = [pltpu.make_async_copy(w.at[k], wv.at[k], wsem.at[k]) for k in range(3)]
    for copy in copies:
        copy.start()

    tab[...] = jnp.zeros_like(tab)
    tab[0:5, :] = table[...]
    pieces = jnp.concatenate(split3(tab[...]), axis=0).astype(BF16)
    incoming = x[0].astype(F32)
    for d in range(2):
        ids = base[...]
        if d:
            ids = jnp.where(ids == 4, 4, 3 - ids)
        hot = (iota((8, BASES), 0) == ids).astype(F32)
        embedded = incoming + tn(jnp.concatenate([hot, hot, hot], axis=0).astype(BF16), pieces)
        inv = lax.rsqrt(jnp.mean(embedded * embedded, axis=1, keepdims=True) + EPS)
        normed = embedded * inv
        rows = slice(BASES * d, BASES * (d + 1))
        normed_out[rows, :] = normed
        inv_out[rows, :] = inv
        f_out[rows, :] = (normed * gain[...]).astype(BF16)

    mapped = dot(f_out[...], mw[...])
    for d in range(2):
        maps[d] = mapped[BASES * d:BASES * (d + 1)].astype(BF16)
        maps_t[d] = jnp.transpose(mapped[BASES * d:BASES * (d + 1)]).astype(BF16)
    logits = nt(swt[...], f_out[...]) + bias[...]
    rows_i, cols_i = iota((BASES, BASES), 0), iota((BASES, BASES), 1)
    for d in range(2):
        logit = logits[:, BASES * d:BASES * (d + 1)]
        step = jnp.maximum(logit, 0.0) + jnp.log1p(jnp.exp(-jnp.abs(logit)))
        logit_t[d] = logit
        step_t[d] = step
        upto = (rows_i <= cols_i) if d == 0 else (rows_i >= cols_i)
        run = summed3(-step * rate[...], upto.astype(F32).astype(BF16))
        whole = jnp.concatenate(split3(run) + split3(step) + (jnp.zeros((32, BASES), F32),), axis=0)
        quant[d] = jnp.transpose(whole).astype(BF16)
        pairs[d] = jnp.zeros((BASES, BASES), F32)
        acc[d] = jnp.zeros((BASES, 128), F32)
        kk[d] = jnp.zeros((8, 128), F32)
        src_rows = run
        logit_out[:, BASES * d:BASES * (d + 1)] = src_rows
    for k, target in ((0, v), (1, g)):
        copies[k].wait()
        for c in range(4):
            block = dot(f_out[...], wv[k, :, 256 * c:256 * c + 256])
            for d in range(2):
                for i in range(2):
                    target[d, 2 * c + i] = block[BASES * d:BASES * (d + 1), 128 * i:128 * i + 128]
    copies[2].wait()
    for c in range(4):
        block = dot(up[0], wv[2, :, 256 * c:256 * c + 256])
        for i in range(2):
            gg[2 * c + i] = block[:, 128 * i:128 * i + 128]

    def expand(d, j):
        both = dot(quant[d], spreads(j))
        run_e, step_e = both[:, 0:128], both[:, 128:256]
        final = run_e[BASES - 1:BASES] if d == 0 else run_e[0:1]
        return run_e, step_e, final

    def to_owner(t):
        return pltpu.make_async_remote_copy(
            src_ref=src.at[t], dst_ref=recv.at[me], send_sem=send_a.at[t], recv_sem=recv_a.at[me],
            device_id={"ctx": t}, device_id_type=MESH)

    def from_device(t):
        return pltpu.make_async_remote_copy(
            src_ref=src.at[t], dst_ref=recv.at[t], send_sem=send_a.at[t], recv_sem=recv_a.at[t],
            device_id={"ctx": t}, device_id_type=MESH)

    def back(t):
        return pltpu.make_async_remote_copy(
            src_ref=scanned.at[t], dst_ref=res.at[me], send_sem=send_b.at[t], recv_sem=recv_b.at[me],
            device_id={"ctx": t}, device_id_type=MESH)

    def from_owner(t):
        return pltpu.make_async_remote_copy(
            src_ref=scanned.at[t], dst_ref=res.at[t], send_sem=send_b.at[t], recv_sem=recv_b.at[t],
            device_id={"ctx": t}, device_id_type=MESH)

    pl.semaphore_wait(barrier, count - 1)
    for d in range(2):
        def ends(j, c, d=d):
            run_e, step_e, final = expand(d, j)
            drive = step_e * v[d, j]
            gates = g[d, j]
            go = gg[j] * (gates * jax.nn.sigmoid(gates))
            drive_b[d, j] = drive.astype(BF16)
            go_b[d, j] = go.astype(BF16)
            state = dot(maps_t[d, 0:64, :], (drive * jnp.exp(final - run_e)).astype(BF16))
            grad = dot(maps_t[d, 64:128, :], (go * jnp.exp(run_e)).astype(BF16))
            decay = jnp.broadcast_to(jnp.exp(final), (8, 128))
            for t, value in ((16 * d + j, state), (24 - 16 * d + j, grad)):
                src[t, 0:64, :] = value
                src[t, 64:72, :] = decay

                @pl.when(t != me)
                def _():
                    to_owner(t).start()
            return c

        lax.fori_loop(0, PAIRS, ends, 0)

    low = iota((BASES, 128), 1) < 64

    def inside(d):
        seen = (rows_i >= cols_i) if d == 0 else (rows_i <= cols_i)
        inflow_b, readout_b = maps[d, :, 0:64], maps[d, :, 64:128]
        affinity = nt(readout_b, inflow_b)

        def step(j, c):
            run_e, _, _ = expand(d, j)
            drive, go = drive_b[d, j], go_b[d, j]
            zero = jnp.zeros_like(drive)
            output = grad_drive = total = None
            for half in range(2):
                mine = low if half == 0 else jnp.logical_not(low)
                row = logit_out[pl.ds(2 * j + half, 1), BASES * d:BASES * (d + 1)]
                column = run_e[:, 64 * half:64 * half + 1]
                decay = jnp.exp(jnp.where(seen, column - row, -1e30))
                mixing = (decay * affinity).astype(BF16)
                drive_h = jnp.where(mine, drive, zero)
                go_h = jnp.where(mine, go, zero)
                a, b, e = dot(mixing, drive_h), tn(mixing, go_h), decay * nt(go_h, drive)
                output = a if output is None else output + a
                grad_drive = b if grad_drive is None else grad_drive + b
                total = e if total is None else total + e
            out[d, j] = output
            gd[d, j] = grad_drive
            pairs[d] += total
            return c

        lax.fori_loop(0, PAIRS, step, 0)

    inside(0)

    def wait_a(s, c):
        t = lax.rem(me + s, count)
        from_device(t).wait_recv()
        return c

    recv[me] = src[me]
    lax.fori_loop(1, count, wait_a, 0)
    falling = me // 16

    def scan(i, carry):
        t = i + falling * (count - 1 - 2 * i)
        scanned[t] = carry

        @pl.when(t != me)
        def _():
            back(t).start()
        return carry * recv[t, 64:65, :] + recv[t, 0:64, :]

    lax.fori_loop(0, count, scan, jnp.zeros((STATE, 128), F32))
    res[me] = scanned[me]

    inside(1)

    def wait_b(s, c):
        t = lax.rem(me + s, count)
        from_owner(t).wait_recv()
        return c

    lax.fori_loop(1, count, wait_b, 0)

    for d in range(2):
        rows = slice(BASES * d, BASES * (d + 1))
        inflow_b, readout_b = maps[d, :, 0:64], maps[d, :, 64:128]

        def outside(j, c, d=d, rows=rows, inflow_b=inflow_b, readout_b=readout_b):
            gin, gread = c
            run_e, step_e, final = expand(d, j)
            initial, after = res[16 * d + j], res[24 - 16 * d + j]
            initial_b, after_b = initial.astype(BF16), after.astype(BF16)
            head, tail = jnp.exp(run_e), jnp.exp(final - run_e)
            drive_r, go_r = drive_b[d, j].astype(F32), go_b[d, j].astype(F32)
            carried = dot(readout_b, initial_b) * head
            output = out[d, j] + carried
            grad_drive = gd[d, j] + dot(inflow_b, after_b) * tail
            values, gates, grad_gated = v[d, j], g[d, j], gg[j]
            sigma = jax.nn.sigmoid(gates)
            swish = gates * sigma
            a, b = split2(grad_drive * drive_r - go_r * output)
            p, q = split2(grad_drive * values)
            acc[d] += dot(a, gathers(j, 0)) + dot(b, gathers(j, 0)) + dot(p, gathers(j, 16)) + dot(q, gathers(j, 16))
            boundary = jnp.sum(go_r * carried, axis=0, keepdims=True) + jnp.exp(final) * jnp.sum(
                initial * after, axis=0, keepdims=True)
            a, b = split2(jnp.broadcast_to(boundary, (16, 128)))
            kk[d] += (dot(a, gathers(j, 32)) + dot(b, gathers(j, 32)))[0:8]
            gin = gin + nt((drive_r * tail).astype(BF16), after_b)
            gread = gread + nt((go_r * head).astype(BF16), initial_b)
            lanes = pl.ds(pl.multiple_of(128 * j, 128), 128)
            gv_out[rows, lanes] = (step_e * grad_drive).astype(BF16)
            gate_out[rows, lanes] = (grad_gated * output * sigma * (1.0 + gates * (1.0 - sigma))).astype(BF16)
            gated_out[rows, lanes] = (output * swish).astype(BF16)
            return gin, gread

        zeros = jnp.zeros((BASES, STATE), F32)
        gin, gread = lax.fori_loop(0, PAIRS, outside, (zeros, zeros))
        pairs_b = pairs[d].astype(BF16)
        gin = gin + tn(pairs_b, readout_b)
        gread = gread + dot(pairs_b, inflow_b)
        mapped_out[rows, :] = jnp.concatenate([gin, gread], axis=1).astype(BF16)
        per_head = jnp.transpose(acc[d] + kk[d, 0:1, :])
        earlier = (rows_i < cols_i) if d == 0 else (rows_i > cols_i)
        grad_log = summed3(per_head[0:16], earlier.astype(F32).astype(BF16)) + per_head[32:48]
        grad_step = per_head[16:32] - grad_log * rate[...]
        logit_out[:, rows] = grad_step * jax.nn.sigmoid(logit_t[d])
        rate_out[:, d:d + 1] = -jnp.sum(grad_log * step_t[d], axis=1, keepdims=True)

    def wait_sent(s, c):
        t = lax.rem(me + s, count)
        to_owner(t).wait_send()
        back(t).wait_send()
        return c

    lax.fori_loop(1, count, wait_sent, 0)


def front(base, stream, cotangent, table, gain, w, mw, swt, bias, rate):
    vmem, anywhere = pl.BlockSpec(memory_space=pltpu.VMEM), pl.BlockSpec(memory_space=pl.ANY)
    rows = 2 * BASES

    def shape(*dims, kind=F32):
        return jax.ShapeDtypeStruct(dims, kind)

    return pl.pallas_call(
        front_kernel,
        out_shape=[
            shape(rows, WIDTH, kind=BF16), shape(rows, WIDTH), shape(rows, 1),
            shape(rows, WIDTH, kind=BF16), shape(rows, WIDTH, kind=BF16), shape(rows, WIDTH, kind=BF16),
            shape(rows, 128, kind=BF16), shape(HEADS, rows), shape(HEADS, 2),
        ],
        in_specs=[vmem] * 5 + [anywhere] + [vmem] * 4,
        out_specs=[vmem] * 9,
        scratch_shapes=[
            pltpu.VMEM((3, WIDTH, WIDTH), BF16),
            pltpu.VMEM((8, WIDTH), F32),
            pltpu.VMEM((2, PAIRS, BASES, 128), F32),
            pltpu.VMEM((2, PAIRS, BASES, 128), F32),
            pltpu.VMEM((PAIRS, BASES, 128), F32),
            pltpu.VMEM((2, BASES, 128), BF16),
            pltpu.VMEM((2, BASES, 128), BF16),
            pltpu.VMEM((2, 128, BASES), BF16),
            pltpu.VMEM((2, HEADS, BASES), F32),
            pltpu.VMEM((2, HEADS, BASES), F32),
            pltpu.VMEM((2, PAIRS, BASES, 128), BF16),
            pltpu.VMEM((2, PAIRS, BASES, 128), BF16),
            pltpu.VMEM((2, PAIRS, BASES, 128), F32),
            pltpu.VMEM((2, PAIRS, BASES, 128), F32),
            pltpu.VMEM((2, BASES, BASES), F32),
            pltpu.VMEM((2, BASES, 128), F32),
            pltpu.VMEM((2, 8, 128), F32),
            pltpu.VMEM((32, 72, 128), F32),
            pltpu.VMEM((32, 72, 128), F32),
            pltpu.VMEM((32, STATE, 128), F32),
            pltpu.VMEM((32, STATE, 128), F32),
            pltpu.SemaphoreType.DMA((3,)),
            pltpu.SemaphoreType.DMA((32,)),
            pltpu.SemaphoreType.DMA((32,)),
            pltpu.SemaphoreType.DMA((32,)),
            pltpu.SemaphoreType.DMA((32,)),
        ],
        compiler_params=pltpu.CompilerParams(collective_id=0, has_side_effects=True, vmem_limit_bytes=56 << 20),
        name="front",
    )(base, stream, cotangent, table, gain, w, mw, swt, bias, rate)


SEMS = 128


def sum_kernel(p0, p1, p2, small, both, grads_out, small_out, stream_out,
               acc, core_in, ring, mid, ring2, fin, dp_in,
               acc_e, core_in_e, ring_e, mid_e, ring2_e, fin_e, dp_in_e,
               tp_in, tp_in_e, piece, row, send, recv, local):
    ctx, tp, dp = lax.axis_index("ctx"), lax.axis_index("tp"), lax.axis_index("dp")
    core, y, z = ctx % 2, (ctx // 2) % 4, ctx // 8

    def at(zz, yy, cc):
        return {"ctx": (zz * 4 + yy) * 2 + cc}

    other = at(z, y, 1 - core)
    y_dev = [at(z, (y + i) % 4, core) for i in range(4)]
    z_dev = [at((z + i) % 4, y, core) for i in range(4)]
    dp_dev, tp_dev = {"dp": 1 - dp}, {"tp": 1 - tp}

    barrier = pltpu.get_barrier_semaphore()
    partners = [other, dp_dev, tp_dev] + y_dev[1:] + z_dev[1:]
    for partner in partners:
        pl.semaphore_signal(barrier, inc=1, device_id=partner, device_id_type=MESH)
    pl.semaphore_wait(barrier, len(partners))

    started = []

    def put(src, dst, device):
        i = len(started)
        copy = pltpu.make_async_remote_copy(
            src_ref=src, dst_ref=dst, send_sem=send.at[i], recv_sem=recv.at[i], device_id=device, device_id_type=MESH)
        copy.start()
        started.append(copy)
        return copy

    half = WIDTH // 2
    here, there = pl.multiple_of(tp * half, half), pl.multiple_of((1 - tp) * half, half)
    to_tp = put(both.at[:, pl.ds(there, half)], tp_in, tp_dev)

    jobs = [dict(src=small, width=128, first=0, stream=1, acc=acc_e, core=core_in_e, ring=ring_e, mid=mid_e,
                 ring2=ring2_e, fin=fin_e, dp=dp_in_e)]
    for k, array in enumerate((p0, p1, p2)):
        for stream in range(2):
            n = 2 * k + stream
            jobs.append(dict(src=array, width=256, first=512 * stream, stream=stream, acc=acc.at[n], core=core_in.at[n],
                             ring=ring.at[n], mid=mid.at[n], ring2=ring2.at[n], fin=fin.at[n], dp=dp_in.at[n]))

    for n, job in enumerate(jobs):
        job["core_copy"], job["own_copy"] = [], []
        for h in range(2):
            lanes = pl.ds(job["first"] + h * job["width"], job["width"])
            job["core_copy"].append(put(job["src"].at[:, :, 1 - core, :, lanes], job["core"].at[h], other))
            own = pltpu.make_async_copy(job["src"].at[:, :, core, :, lanes], job["acc"].at[h], local.at[2 * n + h])
            own.start()
            job["own_copy"].append(own)

    def chunk(ref, h, c, stream, stage):
        if stream == 0 and stage == 1:
            return ref.at[h, :, c]
        return ref.at[h, c]

    def place(job, stage):
        over_y = (job["stream"] == 0) == (stage == 1)
        return (y, y_dev) if over_y else (z, z_dev)

    def ring_start(job, ref, buffer, stage):
        p, dev = place(job, stage)
        s = job["stream"]
        job["m1"] = put(chunk(ref, 0, (p + 2) % 4, s, stage), buffer.at[0], dev[1])
        job["m1p"] = put(chunk(ref, 1, (p + 2) % 4, s, stage), buffer.at[1], dev[3])
        job["m2"] = put(chunk(ref, 1, (p + 1) % 4, s, stage), buffer.at[2], dev[1])
        job["m2p"] = put(chunk(ref, 0, (p + 3) % 4, s, stage), buffer.at[3], dev[3])

    def ring_middle(job, ref, buffer, stage):
        p, dev = place(job, stage)
        s = job["stream"]
        job["m1"].wait_recv()
        up = chunk(ref, 0, (p + 1) % 4, s, stage)
        up[...] = up[...] + buffer[0]
        job["m3"] = put(up, buffer.at[4], dev[1])
        job["m1p"].wait_recv()
        down = chunk(ref, 1, (p + 3) % 4, s, stage)
        down[...] = down[...] + buffer[1]
        job["m3p"] = put(down, buffer.at[5], dev[3])

    def ring_end(job, ref, buffer, stage, into):
        p, dev = place(job, stage)
        s = job["stream"]
        for name in ("m2", "m2p", "m3", "m3p"):
            job[name].wait_recv()
        into[0] = chunk(ref, 0, p, s, stage)[...] + buffer[3] + buffer[4]
        into[1] = chunk(ref, 1, p, s, stage)[...] + buffer[2] + buffer[5]

    for job in jobs:
        for h in range(2):
            job["own_copy"][h].wait()
            job["core_copy"][h].wait_recv()
            job["acc"][h] = job["acc"][h] + job["core"][h]
        ring_start(job, job["acc"], job["ring"], 1)
    for job in jobs:
        ring_middle(job, job["acc"], job["ring"], 1)
    for job in jobs:
        ring_end(job, job["acc"], job["ring"], 1, job["mid"])
        ring_start(job, job["mid"], job["ring2"], 2)
    for job in jobs:
        ring_middle(job, job["mid"], job["ring2"], 2)
    mine = pl.ds(pl.multiple_of(16 * dp, 16), 16)
    yours = pl.ds(pl.multiple_of(16 * (1 - dp), 16), 16)
    for job in jobs:
        ring_end(job, job["mid"], job["ring2"], 2, job["fin"])
        job["dp_copy"] = put(job["fin"].at[:, yours, :], job["dp"], dp_dev)

    job = jobs[0]
    job["dp_copy"].wait_recv()
    for h in range(2):
        piece[0, mine, 128 * h:128 * h + 128] = job["fin"][h, mine, :] + job["dp"][h]
    over_tp = put(piece.at[0, mine, :], tp_in_e, tp_dev)
    for k in range(3):
        for stream in range(2):
            done = jobs[1 + 2 * k + stream]
            done["dp_copy"].wait_recv()
            for h in range(2):
                first = 512 * stream + 256 * h
                grads_out[k, :, first:first + 256] = done["fin"][h, mine, :] + done["dp"][h]
    over_tp.wait_recv()
    piece[1, mine, :] = piece[0, mine, :] + tp_in_e[...]
    put(piece.at[1, mine, :], piece.at[1, mine, :], dp_dev).wait_recv()
    row[y] = piece[1]
    for copy in [put(piece.at[1], row.at[y], dev) for dev in y_dev[1:]]:
        copy.wait_recv()
    small_out[z, :, core] = row[...]
    for copy in [put(row, small_out.at[z, :, core], dev) for dev in z_dev[1:]]:
        copy.wait_recv()
    put(small_out.at[:, :, core], small_out.at[:, :, core], other).wait_recv()

    to_tp.wait_recv()
    stream_out[...] = both[:, pl.ds(here, half)] + tp_in[...]
    for copy in started:
        copy.wait_send()


def sum_all(p0, p1, p2, small, both):
    def cut(array):
        return array.reshape(4, 4, 2, 32, array.shape[1])

    vmem, anywhere = pl.BlockSpec(memory_space=pltpu.VMEM), pl.BlockSpec(memory_space=pl.ANY)

    def buffers(lead, width):
        return [pltpu.VMEM(lead + shape + (32, width), F32) for shape in ((2, 4, 4), (2, 4, 4), (6, 4), (2, 4), (6,), (2,))
                ] + [pltpu.VMEM(lead + (2, 16, width), F32)]

    return pl.pallas_call(
        sum_kernel,
        out_shape=[
            jax.ShapeDtypeStruct((3, 16, WIDTH), F32),
            jax.ShapeDtypeStruct((4, 4, 2, 32, 256), F32),
            jax.ShapeDtypeStruct((BASES, WIDTH // 2), F32),
        ],
        in_specs=[anywhere] * 4 + [vmem],
        out_specs=[vmem] * 3,
        scratch_shapes=buffers((6,), 256) + buffers((), 128) + [
            pltpu.VMEM((BASES, WIDTH // 2), F32),
            pltpu.VMEM((16, 256), F32),
            pltpu.VMEM((2, 32, 256), F32),
            pltpu.VMEM((4, 32, 256), F32),
            pltpu.SemaphoreType.DMA((SEMS,)),
            pltpu.SemaphoreType.DMA((SEMS,)),
            pltpu.SemaphoreType.DMA((14,)),
        ],
        compiler_params=pltpu.CompilerParams(collective_id=1, has_side_effects=True, vmem_limit_bytes=48 << 20),
        name="sum_all",
    )(cut(p0), cut(p1), cut(p2), cut(small), both)


def body(base_ids, stream, cotangent, table, gain, projections, mixer_weight, step_weight, step_bias, rate):
    bases = base_ids[0]
    letters = jnp.arange(5, dtype=jnp.int32)
    own = bases[:, None] == letters[None, :]
    paired = jnp.where(bases == 4, 4, 3 - bases)[:, None] == letters[None, :]
    upstream = cotangent[0]
    w = jnp.transpose(projections, (1, 0, 2))
    features, normed, inv_scale, gv, gate, gated, gm, glogit, grate = front(
        base_ids, stream, cotangent, table, gain[None], w, mixer_weight, jnp.transpose(step_weight),
        step_bias[:, None], rate[:, None])

    glogit_b = jnp.transpose(glogit).astype(BF16)
    gf = nt(gv, w[0]) + nt(gate, w[1]) + nt(gm, mixer_weight) + nt(glogit_b, step_weight)
    gn = gf * gain[None, :]
    ge = inv_scale * (gn - normed * jnp.mean(gn * normed, axis=1, keepdims=True))
    ge = ge + 0.5 * jnp.concatenate([upstream, upstream], axis=0).astype(F32)
    both = ge[:BASES] + ge[BASES:]
    ggain = jnp.sum(gf * normed, axis=0)
    hot = jnp.concatenate([own, paired], axis=0).astype(F32)
    gtable = lax.dot_general(ge, hot, (((0,), (0,)), ((), ())), preferred_element_type=F32, precision=HIGH)
    tp = lax.axis_index("tp")
    gstep = tn(features, glogit_b)
    heads_at = HEADS * tp
    gbias = jnp.sum(glogit, axis=1)
    grate = jnp.sum(grate, axis=1)
    scalars = jnp.zeros((32, 2), F32)
    scalars = lax.dynamic_update_slice(scalars, jnp.stack([gbias, grate], axis=1), (heads_at, 0))
    steps = lax.dynamic_update_slice(jnp.zeros((WIDTH, 32), F32), gstep, (0, heads_at))
    rest = jnp.concatenate([
        steps, ggain[:, None], gtable, jnp.pad(scalars, ((0, WIDTH - 32), (0, 0))), jnp.zeros((WIDTH, 88), F32)], axis=1)
    small = jnp.concatenate([tn(features, gm), rest], axis=1)
    up2 = jnp.concatenate([upstream, upstream], axis=0)
    grads, small, stream_grad = sum_all(tn(features, gv), tn(features, gate), tn(up2, gated), small, both)
    small = small.reshape(WIDTH, 256)
    heads = lax.dynamic_slice(small, (0, 128 + heads_at), (WIDTH, HEADS))
    pair = lax.dynamic_slice(small, (heads_at, 128 + 38), (HEADS, 2))
    return (
        jnp.transpose(grads, (1, 0, 2)),
        small[:, :128],
        heads,
        pair[:, 0],
        pair[:, 1],
        jnp.transpose(small[:, 161:166]),
        small[:, 160],
        stream_grad[None],
    )


def solution(mesh):
    return jax.shard_map(
        body,
        mesh=mesh,
        in_specs=(
            P("dp", "ctx"),
            P("dp", "ctx", None),
            P("dp", "ctx", None),
            P(),
            P(),
            P(None, None, "tp"),
            P(),
            P(None, "tp"),
            P("tp"),
            P("tp"),
        ),
        out_specs=(
            P(("ctx", "dp"), None, "tp"),
            P(),
            P(None, "tp"),
            P("tp"),
            P("tp"),
            P(),
            P(),
            P("dp", "ctx", "tp"),
        ),
        check_vma=False,
    )
```

time: 233 us -> 176 us (0.76)
  local copies, waits for them, and re-layouts: 49.8 us -> 18.4 us
  matrix products: 36.5 us -> 19.8 us
  other arithmetic: 9.65 us -> 4.33 us
  Pallas kernels: 135 us -> 132 us
    unnamed x94 -> x40, local copies, waits for them, and re-layouts: 19 us -> 5.57 us
    dot_general x7 -> x0, matrix products: 10.4 us -> none  [the longest x5 9.89 us: dot(): return jnp.dot(left, right, preferred_element_type=F32)]
    reshape x4 -> x0, local copies, waits for them, and re-layouts: 6.83 us -> none  [wide(): return jnp.repeat(small, 64, axis=1)]
    slice x7 -> x0, local copies, waits for them, and re-layouts: 6.62 us -> none  [the longest x2 2.47 us: body(): mapped[:, STATE:].reshape(2, BASES, STATE)]
    dot_general x9 -> x5, matrix products: 15.8 us -> 11.5 us  [tn(): lax.dot_general(left, right, (((0,), (0,)), ((), ())), preferred_element_...]
    pallas_call x2 -> x1, Pallas kernels: 66.6 us -> 63.8 us  [front(): pl.pallas_call(front_kernel, out_shape=[shape(rows, WIDTH, kind=BF16), sh...]
where the time goes in v2:
time: 176 us
  Pallas kernels  132 us (75%)
  matrix products  19.8 us (11%)
  local copies, waits for them, and re-layouts  18.4 us (10%)
  other arithmetic  4.33 us (2%)
    pallas_call x1, Pallas kernels, sum_all(): pl.pallas_call(sum_kernel, out_shape=[jax.ShapeDtypeStruct((3, 16, WIDTH)...  68.3 us
    pallas_call x1, Pallas kernels, front(): pl.pallas_call(front_kernel, out_shape=[shape(rows, WIDTH, kind=BF16), sh...  63.8 us
    dot_general x5, matrix products, tn(): lax.dot_general(left, right, (((0,), (0,)), ((), ())), preferred_element_...  11.5 us
    dot_general x4, matrix products, nt(): lax.dot_general(left, right, (((1,), (1,)), ((), ())), preferred_element_...  6.52 us
    unnamed x40, local copies, waits for them, and re-layouts  5.57 us

profile of v2, /device:TPU:1, one launch (start us, length us, event | category | flops | bytes accessed | tf_op | source)
XLA Modules:
  0.0 175.6 jit_solution(6838479295752562440)
XLA Ops:
  0.6 1.3 copy.33.bias
  2.0 1.3 copy.34.rate
  3.3 63.8 %front.1 = (bf16[512,1024]{1,0:T(8,128)(2,1)}, f32[512,1024]{1,0:T(8,128)}, f32[512,1]{1,0:T(8,128)}, bf16[512,1024]{1,0:T(8,128)(2,1)}, bf16[512,1024]{1,0:T(8,...) custom-call(s32[1,256]{1,0:T(1,128)} %base.1, ...), custom_call_target="tpu_custom_call" | custom-call | tf_op jit(solution)/shard_map/front/pallas_call | solution.py:310
  67.1 2.6 %fusion = f32[512,1024]{1,0:T(8,128)S(1)} fusion(bf16[512,1024]{1,0:T(8,128)(2,1)} %get-tuple-element.22, bf16[3,1024,1024]{2,1,0:T(8,128)(2,1)S(1)} %bitcast.50), kind=kOutput, calls=%fused_computation.1 | convolution fusion | flops 1073741824 | bytes 5242880 | tf_op jit(solution)/shard_map/dot_general | solution.py:23
  69.7 1.3 fusion.1
  71.5 1.1 copy-done.2
  72.6 2.2 %multiply_reduce_fusion = (f32[512]{0:T(512)S(1)}, f32[1024]{0:T(1024)S(1)}, f32[512,1024]{1,0:T(8,128)}) fusion(f32[512,1024]{1,0:T(8,128)S(1)} %copy-done.2, f32[1024]{0:T(1024)S(1)} %copy-done.14, bf16[1024,16]{0,1:T(8,128)(2,1)S(1)} %copy-done.13, f32[16,512]{1,0:T(8,128)S(1)} %copy-done.11, f32[512,1024]{1,0:T(8,128)S(1)} %fusion.15, ...), kind=kOutput, calls=%fused_computation.5 | convolution fusion | flops 20978176 | bytes 10561536 | tf_op jit(solution)/shard_map/dot_general | solution.py:23
  75.0 2.1 %multiply_add_fusion = f32[512,1024]{1,0:T(8,128)S(1)} fusion(f32[512,1024]{1,0:T(8,128)S(1)} %copy-done.2, f32[512,1024]{1,0:T(8,128)} %get-tuple-element.36, f32[512]{0:T(512)S(1)} %broadcast_multiply_fusion, f32[1024]{0:T(1024)S(1)} %copy-done.14, f32[512]{0:T(512)S(1)} %reduce, bf16[256,1024]{1,0:T(8,128)(2,1)S(1)} %bitcast.53), kind=kLoop, calls=%fused_computation.4 | loop fusion | flops 5242880 | bytes 6823936 | tf_op jit(solution)/shard_map/add | solution.py:540
  77.2 1.3 copy-done.1
  78.5 1.8 %fusion.3 = f32[1024,5]{1,0:T(8,128)S(1)} fusion(f32[512,1024]{1,0:T(8,128)S(1)} %multiply_add_fusion, pred[256,5]{0,1:T(8,128)(4,1)S(1)} %get-tuple-element.37, pred[256,5]{0,1:T(8,128)(4,1)S(1)} %get-tuple-element.38), kind=kOutput, calls=%fused_computation.12 | convolution fusion | flops 31459840 | bytes 2120192 | tf_op jit(solution)/shard_map/dot_general | solution.py:544
  80.3 1.1 concatenate.29
  82.0 2.3 %dynamic_update_slice.6 = f32[1024,32]{1,0:T(8,128)S(1)} dynamic-update-slice(f32[1024,32]{1,0:T(8,128)S(1)} %broadcast_in_dim.32, f32[1024,16]{1,0:T(8,128)S(1)} %fusion.8, s32[]{:T(128)} %constant.14.clone.1, s32[]{:T(128)S(6)} %select_n.18) | dynamic-update-slice | bytes 131076 | tf_op jit(solution)/shard_map/dynamic_update_slice | solution.py:552
  84.6 0.8 pad.4
  85.5 1.3 fusion.14
  86.7 0.9 broadcast_in_dim.34
  87.6 2.1 %concatenate.28.small = f32[4,4,2,32,256]{4,3,2,1,0:T(8,128)S(1)} concatenate(f32[4,4,2,32,128]{4,3,2,1,0:T(8,128)} %bitcast.57, f32[4,4,2,32,32]{4,3,2,1,0:T(8,128)} %bitcast.58, f32[4,4,2,32,1]{4,3,2,1,0:T(8,128)} %concatenate.29, f32[4,4,2,32,5]{4,3,2,1,0:T(8,128)S(1)} %bitcast.55, f32[4,4,2,32,2]{4,3,2,1,0:T(8,128)} %bitcast.56, f32[4,4,2,32,88]{4,3,2,1,0:T(8,128)} %broadcast_in_dim.34), dimensions={4} | concatenate | bytes 2097152 | tf_op jit(solution)/shard_map/concatenate | solution.py:555
  89.7 1.8 %slice_add_fusion.both = f32[256,1024]{1,0:T(8,128)S(1)} fusion(f32[512,1024]{1,0:T(8,128)} %copy-done.1), kind=kLoop, calls=%fused_computation.8 | loop fusion | flops 262144 | bytes 3145728 | tf_op jit(solution)/shard_map/add | solution.py:541
  91.5 3.2 %fusion.13 = f32[1024,1024]{1,0:T(8,128)} fusion(bf16[512,1024]{1,0:T(8,128)(2,1)S(1)} %copy-done, bf16[512,1024]{1,0:T(8,128)(2,1)S(1)} %copy-done.9), kind=kOutput, calls=%fused_computation.31 | convolution fusion | flops 1073741824 | bytes 6291456 | tf_op jit(solution)/shard_map/dot_general | solution.py:27
  94.7 3.3 %fusion.12 = f32[1024,1024]{1,0:T(8,128)} fusion(bf16[512,1024]{1,0:T(8,128)(2,1)S(1)} %copy-done, bf16[512,1024]{1,0:T(8,128)(2,1)S(1)} %copy-done.8), kind=kOutput, calls=%fused_computation.30 | convolution fusion | flops 1073741824 | bytes 6291456 | tf_op jit(solution)/shard_map/dot_general | solution.py:27
  98.0 3.3 %fusion.2 = f32[1024,1024]{1,0:T(8,128)} fusion(bf16[512,1024]{1,0:T(8,128)(2,1)S(1)} %copy-done.17, bf16[256,1024]{1,0:T(8,128)(2,1)S(1)} %bitcast.54), kind=kOutput, calls=%fused_computation.10 | convolution fusion | flops 1075838976 | bytes 5767168 | tf_op jit(solution)/shard_map/dot_general | solution.py:27
  101.3 68.3 %sum_all.1 = (f32[3,16,1024]{2,1,0:T(8,128)S(1)}, f32[4,4,2,32,256]{4,3,2,1,0:T(8,128)S(1)}, f32[256,512]{1,0:T(8,128)S(1)}) custom-call(f32[4,4,2,32,1024]{4,3,2,1,0:T(8,128)} %bitcast.48, f32[4,4,2,32,1024]{4,3,2,1,0:T(8,128)} %bitcast.47, f32[4,4,2,32,1024]{4,3,2,1,0:T(8,128)} %bitcast.52, f32[4,4,2,32,256]{4,3,2,1,0:T(8,128)S(1)} %concatenate.28.small, ...), custom_call_target="tpu_custom_call" | custom-call | tf_op jit(solution)/shard_map/sum_all/pallas_call | solution.py:502
  170.8 0.8 copy.44
  171.6 0.8 slice.40
  173.1 1.0 slice_reduce_fusion
  (53 shorter events, 4.9 us)
Async XLA Ops:
  3.3 63.8 %copy-start.3 = (bf16[1024,3,1024]{2,0,1:T(8,128)(2,1)S(1)}, bf16[1024,3,1024]{2,0,1:T(8,128)(2,1)}, u32[]{:S(2)}) copy-start(bf16[1024,3,1024]{2,0,1:T(8,128)(2,1)} %param.15) | copy-start | bytes 18874372
  67.1 2.6 %copy-start.7 = (bf16[512,1024]{1,0:T(8,128)(2,1)S(1)}, bf16[512,1024]{1,0:T(8,128)(2,1)}, u32[]{:S(2)}) copy-start(bf16[512,1024]{1,0:T(8,128)(2,1)} %get-tuple-element.21) | copy-start | bytes 3145732
  69.7 1.4 copy-start.6
  69.7 1.4 copy-start.10
  71.0 1.6 copy-start.2
  71.0 1.6 copy-start.11
  71.0 1.6 copy-start.13
  71.0 1.6 copy-start.14
  72.6 2.2 %copy-start.12 = (f32[512,1]{1,0:T(8,128)S(1)}, f32[512,1]{1,0:T(8,128)}, u32[]{:S(2)}) copy-start(f32[512,1]{1,0:T(8,128)} %get-tuple-element.27) | copy-start | bytes 6148
  72.6 2.4 %copy-start.4 = (bf16[1,256,1024]{2,1,0:T(8,128)(2,1)S(1)}, bf16[1,256,1024]{2,1,0:T(8,128)(2,1)}, u32[]{:S(2)}) copy-start(bf16[1,256,1024]{2,1,0:T(8,128)(2,1)} %up.1) | copy-start | bytes 1572868
  75.0 2.2 %copy-start.15 = (s32[1,256]{1,0:T(1,128)S(1)}, s32[1,256]{1,0:T(1,128)}, u32[]{:S(2)}) copy-start(s32[1,256]{1,0:T(1,128)} %base.1) | copy-start | bytes 3076
  77.1 1.4 copy-start.1
  77.1 4.3 %copy-start = (bf16[512,1024]{1,0:T(8,128)(2,1)S(1)}, bf16[512,1024]{1,0:T(8,128)(2,1)}, u32[]{:S(2)}) copy-start(bf16[512,1024]{1,0:T(8,128)(2,1)} %get-tuple-element.20) | copy-start | bytes 3145732
  80.3 4.1 %copy-start.16 = (f32[16,2]{1,0:T(8,128)S(1)}, f32[16,2]{1,0:T(8,128)}, u32[]{:S(2)}) copy-start(f32[16,2]{1,0:T(8,128)} %get-tuple-element.28) | copy-start | bytes 388
  84.3 2.4 %copy-start.5 = (f32[1024,32]{1,0:T(8,128)}, f32[1024,32]{1,0:T(8,128)S(1)}, u32[]{:S(2)}) copy-start(f32[1024,32]{1,0:T(8,128)S(1)} %dynamic_update_slice.6) | copy-start | bytes 393220
  89.7 1.9 %copy-start.9 = (bf16[512,1024]{1,0:T(8,128)(2,1)S(1)}, bf16[512,1024]{1,0:T(8,128)(2,1)}, u32[]{:S(2)}) copy-start(bf16[512,1024]{1,0:T(8,128)(2,1)} %get-tuple-element.22) | copy-start | bytes 3145732
  91.5 3.2 %copy-start.8 = (bf16[512,1024]{1,0:T(8,128)(2,1)S(1)}, bf16[512,1024]{1,0:T(8,128)(2,1)}, u32[]{:S(2)}) copy-start(bf16[512,1024]{1,0:T(8,128)(2,1)} %get-tuple-element.21) | copy-start | bytes 3145732
  94.7 3.3 %copy-start.17 = (bf16[512,1024]{1,0:T(8,128)(2,1)S(1)}, bf16[512,1024]{1,0:T(8,128)(2,1)}, u32[]{:S(2)}) copy-start(bf16[512,1024]{1,0:T(8,128)(2,1)} %get-tuple-element.23) | copy-start | bytes 3145732

commit v3 on v2

v3 whole, which is shorter than its diff:
```python
import functools

import jax
import jax.numpy as jnp
from jax import lax
from jax.experimental import pallas as pl
from jax.experimental.pallas import tpu as pltpu
from jax.sharding import PartitionSpec as P

EPS = 1e-05
HIGH = lax.Precision.HIGHEST
F32 = jnp.float32
BF16 = jnp.bfloat16
MESH = pl.DeviceIdType.MESH
BASES = 256
WIDTH = 1024
HEADS = 16
PAIRS = 8
STATE = 64


def nt(left, right):
    return lax.dot_general(left, right, (((1,), (1,)), ((), ())), preferred_element_type=F32)


def tn(left, right):
    return lax.dot_general(left, right, (((0,), (0,)), ((), ())), preferred_element_type=F32)


def dot(left, right):
    return jnp.dot(left, right, preferred_element_type=F32)


def exact(left, right):
    return jnp.dot(left, right, preferred_element_type=F32, precision=HIGH)


def split3(x):
    a = x.astype(BF16).astype(F32)
    b = (x - a).astype(BF16).astype(F32)
    return a, b, x - a - b


def split2(x):
    a = x.astype(BF16)
    return a, (x - a.astype(F32)).astype(BF16)


def summed3(x, ones):
    r = dot(jnp.concatenate(split3(x), axis=0).astype(BF16), ones)
    n = x.shape[0]
    return r[0:n] + r[n:2 * n] + r[2 * n:3 * n]


def iota(shape, dim):
    return lax.broadcasted_iota(jnp.int32, shape, dim)


def spreads(j):
    r, c = iota((128, 256), 0), iota((128, 256), 1)
    kind = (r >= 48).astype(jnp.int32) + (r >= 96).astype(jnp.int32)
    return jnp.logical_and(kind == c // 128, (r & 15) == 2 * j + (c & 127) // 64).astype(F32).astype(BF16)


def gathers(j, base):
    r, c = iota((128, 128), 0), iota((128, 128), 1)
    return (c == base + 2 * j + r // 64).astype(F32).astype(BF16)


CHIPS = 16
SEMS = 216
ORDER = [(q, k) for q in range(4) for k in (2, 1, 0)]


def main_kernel(base, x, up, table, gain, w, mw, swt, bias, rate,
                grads_out, mixer_out, step_out, table_out, gain_out, scalars_out, stream_out,
                wv, tab, f, normed_s, inv_s, v, g, gg, quant, run_t, maps, maps_t, logit_t, step_t, drive_b, go_b, out, gd, pairs,
                acc, kk, gins, greads, src, from_core, totals, recv, scanned, res, ent, ent_out,
                gv, gate, gated, gm, glt, rates, ft, upt, rt, prod, core_in, ring, mid, ring2, fin, dp_in,
                prod_e, core_e, parts, mine_e, x_in, all_e, tp_in,
                wsem, send_c, recv_c, send_a, recv_a, send_b, recv_b, send_d, recv_d, send, receive):
    ctx, tp, dp = lax.axis_index("ctx"), lax.axis_index("tp"), lax.axis_index("dp")
    core, chip = ctx % 2, ctx // 2
    y, z = chip % 4, chip // 4

    def on(c):
        return {"ctx": c * 2 + core}

    other = {"ctx": chip * 2 + 1 - core}
    tp_dev, dp_dev, far_dev = {"tp": 1 - tp}, {"dp": 1 - dp}, {"tp": 1 - tp, "dp": 1 - dp}
    y_dev = [on(z * 4 + (y + i) % 4) for i in range(4)]
    z_dev = [on(((z + i) % 4) * 4 + y) for i in range(4)]

    barrier = pltpu.get_barrier_semaphore()

    def greet(i, c):
        pl.semaphore_signal(barrier, inc=1, device_id=on(lax.rem(chip + i, CHIPS)), device_id_type=MESH)
        return c

    lax.fori_loop(1, CHIPS, greet, 0)
    for device in (other, tp_dev, dp_dev, far_dev):
        pl.semaphore_signal(barrier, inc=1, device_id=device, device_id_type=MESH)
    copies = [pltpu.make_async_copy(w.at[k], wv.at[k], wsem.at[k]) for k in range(3)]
    for copy in copies:
        copy.start()

    tab[...] = jnp.zeros_like(tab)
    tab[0:5, :] = table[...]
    pieces = jnp.concatenate(split3(tab[...]), axis=0).astype(BF16)
    incoming = x[0].astype(F32)
    hots = []
    for d in range(2):
        ids = base[...]
        if d:
            ids = jnp.where(ids == 4, 4, 3 - ids)
        hot = (iota((8, BASES), 0) == ids).astype(F32)
        hots.append(hot.astype(BF16))
        embedded = incoming + tn(jnp.concatenate([hot, hot, hot], axis=0).astype(BF16), pieces)
        inv = lax.rsqrt(jnp.mean(embedded * embedded, axis=1, keepdims=True) + EPS)
        normed = embedded * inv
        rows = slice(BASES * d, BASES * (d + 1))
        normed_s[rows, :] = normed
        inv_s[rows, :] = inv
        f[rows, :] = (normed * gain[...]).astype(BF16)

    def column(row):
        square = jnp.broadcast_to(row, (HEADS, HEADS))
        return jnp.sum(jnp.where(iota((HEADS, HEADS), 0) == iota((HEADS, HEADS), 1), square, 0.0), axis=1, keepdims=True)

    rate_c = column(rate[...])
    mapped = dot(f[...], mw[...])
    for d in range(2):
        maps[d] = mapped[BASES * d:BASES * (d + 1)].astype(BF16)
        maps_t[d] = jnp.transpose(mapped[BASES * d:BASES * (d + 1)]).astype(BF16)
    logits = nt(swt[...], f[...]) + column(bias[...])
    rows_i, cols_i = iota((BASES, BASES), 0), iota((BASES, BASES), 1)
    for d in range(2):
        logit = logits[:, BASES * d:BASES * (d + 1)]
        step = jnp.maximum(logit, 0.0) + jnp.log1p(jnp.exp(-jnp.abs(logit)))
        logit_t[d] = logit
        step_t[d] = step
        upto = (rows_i <= cols_i) if d == 0 else (rows_i >= cols_i)
        run = summed3(-step * rate_c, upto.astype(F32).astype(BF16))
        run_t[d] = run
        whole = jnp.concatenate(split3(run) + split3(step) + (jnp.zeros((32, BASES), F32),), axis=0)
        quant[d] = jnp.transpose(whole).astype(BF16)
        pairs[d] = jnp.zeros((BASES, BASES), F32)
        acc[d] = jnp.zeros((BASES, 128), F32)
        kk[d] = jnp.zeros((8, 128), F32)
        gins[d] = jnp.zeros((BASES, STATE), F32)
        greads[d] = jnp.zeros((BASES, STATE), F32)
    for k, target in ((0, v), (1, g)):
        copies[k].wait()
        for c in range(4):
            block = dot(f[...], wv[k, :, 256 * c:256 * c + 256])
            for d in range(2):
                for i in range(2):
                    target[d, 2 * c + i] = block[BASES * d:BASES * (d + 1), 128 * i:128 * i + 128]
    copies[2].wait()
    for c in range(4):
        block = dot(up[0], wv[2, :, 256 * c:256 * c + 256])
        for i in range(2):
            gg[2 * c + i] = block[:, 128 * i:128 * i + 128]

    def expand(d, j):
        both = dot(quant[d], spreads(j))
        run_e, step_e = both[:, 0:128], both[:, 128:256]
        final = run_e[BASES - 1:BASES] if d == 0 else run_e[0:1]
        return run_e, step_e, final

    def to_core(i):
        return pltpu.make_async_remote_copy(
            src_ref=src.at[CHIPS * (1 - core) + i], dst_ref=from_core.at[i], send_sem=send_c.at[i], recv_sem=recv_c.at[i],
            device_id=other, device_id_type=MESH)

    def to_owner(i):
        return pltpu.make_async_remote_copy(
            src_ref=totals.at[i], dst_ref=recv.at[chip], send_sem=send_a.at[i], recv_sem=recv_a.at[chip],
            device_id=on(i), device_id_type=MESH)

    def from_chip(i):
        return pltpu.make_async_remote_copy(
            src_ref=totals.at[i], dst_ref=recv.at[i], send_sem=send_a.at[i], recv_sem=recv_a.at[i],
            device_id=on(i), device_id_type=MESH)

    def to_chip(i):
        return pltpu.make_async_remote_copy(
            src_ref=scanned.at[i], dst_ref=res.at[chip], send_sem=send_b.at[i], recv_sem=recv_b.at[chip],
            device_id=on(i), device_id_type=MESH)

    def from_owner(i):
        return pltpu.make_async_remote_copy(
            src_ref=scanned.at[i], dst_ref=res.at[i], send_sem=send_b.at[i], recv_sem=recv_b.at[i],
            device_id=on(i), device_id_type=MESH)

    def entering(i):
        return pltpu.make_async_remote_copy(
            src_ref=ent_out.at[i], dst_ref=ent.at[CHIPS * core + i], send_sem=send_d.at[i], recv_sem=recv_d.at[i],
            device_id=other, device_id_type=MESH)

    def entered(i):
        return pltpu.make_async_remote_copy(
            src_ref=ent_out.at[i], dst_ref=ent.at[CHIPS * (1 - core) + i], send_sem=send_d.at[i], recv_sem=recv_d.at[i],
            device_id=other, device_id_type=MESH)

    pl.semaphore_wait(barrier, CHIPS + 3)
    for d in range(2):
        def ends(j, c, d=d):
            run_e, step_e, final = expand(d, j)
            drive = step_e * v[d, j]
            gates = g[d, j]
            go = gg[j] * (gates * jax.nn.sigmoid(gates))
            drive_b[d, j] = drive.astype(BF16)
            go_b[d, j] = go.astype(BF16)
            state = dot(maps_t[d, 0:64, :], (drive * jnp.exp(final - run_e)).astype(BF16))
            grad = dot(maps_t[d, 64:128, :], (go * jnp.exp(run_e)).astype(BF16))
            decay = jnp.broadcast_to(jnp.exp(final), (8, 128))
            for t, value in ((16 * d + j, state), (24 - 16 * d + j, grad)):
                src[t, 0:64, :] = value
                src[t, 64:72, :] = decay
            to_core(j + 8 * (1 - core) if d == 0 else j + 8 * core).start()
            return c

        lax.fori_loop(0, PAIRS, ends, 0)

    def combine(i, c):
        to_core(i).wait_recv()
        here, there = src[CHIPS * core + i], from_core[i]
        totals[i, 0:64, :] = here[0:64] * there[64:65] + there[0:64]
        totals[i, 64:72, :] = here[64:72] * there[64:72]

        @pl.when(i != chip)
        def _():
            to_owner(i).start()
        return c

    lax.fori_loop(0, CHIPS, combine, 0)

    low = iota((BASES, 128), 1) < 64

    def inside(d):
        seen = (rows_i >= cols_i) if d == 0 else (rows_i <= cols_i)
        inflow_b, readout_b = maps[d, :, 0:64], maps[d, :, 64:128]
        affinity = nt(readout_b, inflow_b)

        def step(j, c):
            run_e, _, _ = expand(d, j)
            drive, go = drive_b[d, j], go_b[d, j]
            zero = jnp.zeros_like(drive)
            output = grad_drive = total = None
            for half in range(2):
                mine = low if half == 0 else jnp.logical_not(low)
                row = run_t[d, pl.ds(2 * j + half, 1), :]
                col = run_e[:, 64 * half:64 * half + 1]
                decay = jnp.exp(jnp.where(seen, col - row, -1e30))
                mixing = (decay * affinity).astype(BF16)
                drive_h = jnp.where(mine, drive, zero)
                go_h = jnp.where(mine, go, zero)
                a, b, e = dot(mixing, drive_h), tn(mixing, go_h), decay * nt(go_h, drive)
                output = a if output is None else output + a
                grad_drive = b if grad_drive is None else grad_drive + b
                total = e if total is None else total + e
            out[d, j] = output
            gd[d, j] = grad_drive
            pairs[d] += total
            return c

        lax.fori_loop(0, PAIRS, step, 0)

    inside(0)

    def others(act):
        def step(i, c):
            act(lax.rem(chip + i, CHIPS))
            return c

        lax.fori_loop(1, CHIPS, step, 0)

    recv[chip] = totals[chip]
    others(lambda i: from_chip(i).wait_recv())

    def scan(i, carry):
        t = i + core * (CHIPS - 1 - 2 * i)
        scanned[t] = carry

        @pl.when(t != chip)
        def _():
            to_chip(t).start()
        return carry * recv[t, 64:65, :] + recv[t, 0:64, :]

    lax.fori_loop(0, CHIPS, scan, jnp.zeros((STATE, 128), F32))
    res[chip] = scanned[chip]

    inside(1)
    for c in range(4):
        ft[256 * c:256 * c + 256, :] = jnp.transpose(f[:, 256 * c:256 * c + 256])
        upt[256 * c:256 * c + 256, :] = jnp.transpose(up[0, :, 256 * c:256 * c + 256])
    others(lambda i: from_owner(i).wait_recv())

    def hand_on(i, c):
        first = res[i]
        here = src[CHIPS * core + i]
        ent_out[i] = first * here[64:65] + here[0:64]
        entering(i).start()
        ent[CHIPS * core + i] = first
        return c

    lax.fori_loop(0, CHIPS, hand_on, 0)

    def wait_entered(i, c):
        entered(i).wait_recv()
        return c

    lax.fori_loop(0, CHIPS, wait_entered, 0)

    started = []

    def put(source, target, device):
        i = len(started)
        copy = pltpu.make_async_remote_copy(
            src_ref=source, dst_ref=target, send_sem=send.at[i], recv_sem=receive.at[i], device_id=device,
            device_id_type=MESH)
        copy.start()
        started.append(copy)
        return copy

    jobs = []
    for n, (q, k) in enumerate(ORDER):
        jobs.append(dict(stream=n % 2, prod=prod.at[n % 6], acc=core_in.at[n], ring=ring.at[n], mid=mid.at[n],
                         ring2=ring2.at[n], fin=fin.at[n], dp=dp_in.at[n]))

    def core_start(job):
        job["core"] = put(job["prod"].at[:, :, :, 1 - core], job["acc"], other)

    def core_end(job):
        job["core"].wait_recv()
        job["acc"][...] = job["acc"][...] + job["prod"][:, :, :, core]

    def chunk(ref, h, c, stream, stage):
        if stream == 0 and stage == 1:
            return ref.at[h, :, c]
        return ref.at[h, c]

    def place(job, stage):
        over_y = (job["stream"] == 0) == (stage == 1)
        return (y, y_dev) if over_y else (z, z_dev)

    def refs(job, stage):
        return (job["acc"], job["ring"], job["mid"]) if stage == 1 else (job["mid"], job["ring2"], job["fin"])

    def ring_start(job, stage):
        p, dev = place(job, stage)
        s = job["stream"]
        ref, buffer, _ = refs(job, stage)
        job["m1"] = put(chunk(ref, 0, (p + 2) % 4, s, stage), buffer.at[0], dev[1])
        job["m1p"] = put(chunk(ref, 1, (p + 2) % 4, s, stage), buffer.at[1], dev[3])
        job["m2"] = put(chunk(ref, 1, (p + 1) % 4, s, stage), buffer.at[2], dev[1])
        job["m2p"] = put(chunk(ref, 0, (p + 3) % 4, s, stage), buffer.at[3], dev[3])

    def ring_middle(job, stage):
        p, dev = place(job, stage)
        s = job["stream"]
        ref, buffer, _ = refs(job, stage)
        job["m1"].wait_recv()
        ahead = chunk(ref, 0, (p + 1) % 4, s, stage)
        ahead[...] = ahead[...] + buffer[0]
        job["m3"] = put(ahead, buffer.at[4], dev[1])
        job["m1p"].wait_recv()
        behind = chunk(ref, 1, (p + 3) % 4, s, stage)
        behind[...] = behind[...] + buffer[1]
        job["m3p"] = put(behind, buffer.at[5], dev[3])

    def ring_end(job, stage):
        p, dev = place(job, stage)
        s = job["stream"]
        ref, buffer, into = refs(job, stage)
        for name in ("m2", "m2p", "m3", "m3p"):
            job[name].wait_recv()
        into[0] = chunk(ref, 0, p, s, stage)[...] + buffer[3] + buffer[4]
        into[1] = chunk(ref, 1, p, s, stage)[...] + buffer[2] + buffer[5]

    mine = pl.ds(pl.multiple_of(16 * dp, 16), 16)
    yours = pl.ds(pl.multiple_of(16 * (1 - dp), 16), 16)

    def go_on(n):
        job = jobs[n]
        at = job.get("at", 0)
        job["at"] = at + 1
        if at == 0:
            core_end(job)
            ring_start(job, 1)
        elif at == 1:
            ring_middle(job, 1)
        elif at == 2:
            ring_end(job, 1)
            ring_start(job, 2)
        elif at == 3:
            ring_middle(job, 2)
        elif at == 4:
            ring_end(job, 2)
            job["over_dp"] = put(job["fin"].at[:, yours, :], job["dp"], dp_dev)
        else:
            q, k = ORDER[n]
            job["over_dp"].wait_recv()
            for h in range(2):
                first = 256 * q + 128 * h
                grads_out[k, :, first:first + 128] = job["fin"][h, mine, :] + job["dp"][h]

    def outside(d, q):
        rows = slice(BASES * d, BASES * (d + 1))
        inflow_b, readout_b = maps[d, :, 0:64], maps[d, :, 64:128]

        def step(j, c):
            run_e, step_e, final = expand(d, j)
            initial, after = ent[16 * d + j], ent[24 - 16 * d + j]
            initial_b, after_b = initial.astype(BF16), after.astype(BF16)
            head, tail = jnp.exp(run_e), jnp.exp(final - run_e)
            drive_r, go_r = drive_b[d, j].astype(F32), go_b[d, j].astype(F32)
            carried = dot(readout_b, initial_b) * head
            output = out[d, j] + carried
            grad_drive = gd[d, j] + dot(inflow_b, after_b) * tail
            values, gates, grad_gated = v[d, j], g[d, j], gg[j]
            sigma = jax.nn.sigmoid(gates)
            swish = gates * sigma
            a, b = split2(grad_drive * drive_r - go_r * output)
            p, r = split2(grad_drive * values)
            acc[d] += dot(a, gathers(j, 0)) + dot(b, gathers(j, 0)) + dot(p, gathers(j, 16)) + dot(r, gathers(j, 16))
            boundary = jnp.sum(go_r * carried, axis=0, keepdims=True) + jnp.exp(final) * jnp.sum(
                initial * after, axis=0, keepdims=True)
            a, b = split2(jnp.broadcast_to(boundary, (16, 128)))
            kk[d] += (dot(a, gathers(j, 32)) + dot(b, gathers(j, 32)))[0:8]
            gins[d] += nt((drive_r * tail).astype(BF16), after_b)
            greads[d] += nt((go_r * head).astype(BF16), initial_b)
            lanes = pl.ds(pl.multiple_of(128 * j, 128), 128)
            gv[rows, lanes] = (step_e * grad_drive).astype(BF16)
            gate[rows, lanes] = (grad_gated * output * sigma * (1.0 + gates * (1.0 - sigma))).astype(BF16)
            gated[rows, lanes] = (output * swish).astype(BF16)
            return c

        lax.fori_loop(2 * q, 2 * q + 2, step, 0)

    def product(n):
        q, k = ORDER[n]
        result = (gv, gate, gated)[k]
        lanes = slice(256 * q, 256 * q + 256)
        if n >= 6:
            jobs[n - 6]["core"].wait_send()

        def step(i, c):
            rows = pl.ds(pl.multiple_of(256 * i, 256), 256)
            if k == 2:
                block = dot(upt[rows, :], result[0:BASES, lanes]) + dot(upt[rows, :], result[BASES:, lanes])
            else:
                block = dot(ft[rows, :], result[:, lanes])
            for h in range(2):
                prod[n % 6, h, i] = block[:, 128 * h:128 * h + 128].reshape(4, 2, 32, 128)
            return c

        lax.fori_loop(0, 4, step, 0)
        core_start(jobs[n])

    for q in range(4):
        outside(0, q)
        if q:
            go_on(3 * q - 1)
        outside(1, q)
        for n in range(3 * q, 3 * q + 3):
            product(n)
            if n > 3 * q:
                go_on(n - 1)
            if n >= 5:
                go_on(n - 5)

    for d in range(2):
        rows = slice(BASES * d, BASES * (d + 1))
        inflow_b, readout_b = maps[d, :, 0:64], maps[d, :, 64:128]
        pairs_b = pairs[d].astype(BF16)
        gin = gins[d] + tn(pairs_b, readout_b)
        gread = greads[d] + dot(pairs_b, inflow_b)
        gm[rows, :] = jnp.concatenate([gin, gread], axis=1).astype(BF16)
        per_head = jnp.transpose(acc[d] + kk[d, 0:1, :])
        earlier = (rows_i < cols_i) if d == 0 else (rows_i > cols_i)
        grad_log = summed3(per_head[0:16], earlier.astype(F32).astype(BF16)) + per_head[32:48]
        grad_step = per_head[16:32] - grad_log * rate_c
        glt[:, rows] = grad_step * jax.nn.sigmoid(logit_t[d])
        rates[:, d:d + 1] = -jnp.sum(grad_log * step_t[d], axis=1, keepdims=True)
    go_on(11)

    glb = glt[...].astype(BF16)
    mean = [jnp.zeros((BASES, 1), F32)] * 2
    for c in range(4):
        lanes = slice(256 * c, 256 * c + 256)
        by_gain = jnp.zeros((1, 256), F32)
        for d in range(2):
            rows = slice(BASES * d, BASES * (d + 1))
            gf = (nt(gv[rows, :], wv[0, lanes, :]) + nt(gate[rows, :], wv[1, lanes, :]) + nt(gm[rows, :], mw[lanes, :])
                  + tn(glb[:, rows], swt[:, lanes]))
            nrm = normed_s[rows, lanes]
            scaled = gf * gain[:, lanes]
            for i in range(2):
                v[d, 2 * c + i] = scaled[:, 128 * i:128 * i + 128]
            mean[d] = mean[d] + jnp.sum(scaled * nrm, axis=1, keepdims=True)
            by_gain = by_gain + jnp.sum(gf * nrm, axis=0, keepdims=True)
        rt[32:40, lanes] = jnp.broadcast_to(by_gain, (8, 256))
    go_on(7)
    for c in range(8):
        lanes = slice(128 * c, 128 * c + 128)
        residual = 0.5 * up[0, :, lanes].astype(F32)
        by_base = jnp.zeros((8, 128), F32)
        whole = None
        for d in range(2):
            rows = slice(BASES * d, BASES * (d + 1))
            ge = inv_s[rows, :] * (v[d, c] - normed_s[rows, lanes] * (mean[d] * (1.0 / WIDTH))) + residual
            whole = ge if whole is None else whole + ge
            for part in split3(ge):
                by_base = by_base + dot(hots[d], part.astype(BF16))
        gg[c] = whole
        rt[40:48, lanes] = by_base
    to_tp = put(gg.at[pl.ds(4 * (1 - tp), 4)], tp_in, tp_dev)

    rt[0:32, :] = jnp.zeros((32, WIDTH), F32)
    rt[48:128, :] = jnp.zeros((80, WIDTH), F32)
    heads_at = pl.multiple_of(16 * tp, 16)
    scalars_at = pl.multiple_of(48 + 16 * tp, 16)
    rt[pl.ds(heads_at, 16), :] = dot(glb, f[...])
    rt[pl.ds(scalars_at, 16), 0:128] = jnp.broadcast_to(jnp.sum(glt[...], axis=1, keepdims=True), (HEADS, 128))
    rt[pl.ds(scalars_at, 16), 128:256] = jnp.broadcast_to(rates[:, 0:1] + rates[:, 1:2], (HEADS, 128))
    for i in range(4):
        prod_e[i, :, :, :, 0:128] = dot(ft[256 * i:256 * i + 256, :], gm[...]).reshape(4, 2, 32, 128)
    for i in range(8):
        prod_e[i // 2, 2 * (i % 2):2 * (i % 2) + 2, :, :, 128:256] = rt[:, 128 * i:128 * i + 128].reshape(2, 2, 32, 128)
    small_core = put(prod_e.at[:, :, 1 - core], core_e, other)
    for n in (0, 1):
        go_on(n)
    small_core.wait_recv()
    core_e[...] = core_e[...] + prod_e[:, :, core]
    offsets = [(dz, dy) for dz in range(4) for dy in range(4)][1:]
    small_in = [put(core_e.at[(z + dz) % 4, (y + dy) % 4], parts.at[4 * dz + dy], on(((z + dz) % 4) * 4 + (y + dy) % 4))
                for dz, dy in offsets]
    for n in (8, 2, 3, 4, 0, 1):
        go_on(n)
    total = core_e[z, y]
    for i, copy in enumerate(small_in):
        copy.wait_recv()
        total = total + parts[i + 1]
    mine_e[0] = total
    over_x = [put(mine_e.at[0], x_in.at[i], device) for i, device in enumerate((tp_dev, dp_dev, far_dev))]
    for n in (9, 5, 6, 2, 3):
        go_on(n)
    for copy in over_x:
        copy.wait_recv()
    mine_e[1] = (mine_e[0] + x_in[0]) + (x_in[1] + x_in[2])
    all_e[z, y, core] = mine_e[1]
    small_back = [put(mine_e.at[1], all_e.at[z, y, core], on(((z + dz) % 4) * 4 + (y + dy) % 4)) for dz, dy in offsets]
    for n in (10, 11, 7, 8, 4, 0, 1, 5, 2, 6, 3):
        go_on(n)
    for copy in small_back:
        copy.wait_recv()
    back_core = put(all_e.at[:, :, core], all_e.at[:, :, core], other)
    for n in (9, 10, 11, 7, 8, 4, 5):
        go_on(n)
    to_tp.wait_recv()
    for i in range(4):
        stream_out[:, 128 * i:128 * i + 128] = gg[4 * tp + i] + tp_in[i]
    back_core.wait_recv()
    mixer_out[...] = all_e[:, :, :, :, 0:128].reshape(WIDTH, 128)
    for i in range(8):
        rt[:, 128 * i:128 * i + 128] = all_e[i // 2, 2 * (i % 2):2 * (i % 2) + 2, :, :, 128:256].reshape(128, 128)
    step_out[...] = rt[pl.ds(heads_at, 16), :]
    gain_out[...] = rt[32:33, :]
    table_out[...] = rt[40:45, :]
    scalars_out[...] = rt[pl.ds(scalars_at, 16), 0:256]
    while any(job["at"] < 6 for job in jobs):
        low_at = min(job["at"] for job in jobs)
        for n, job in enumerate(jobs):
            if job["at"] == low_at:
                go_on(n)
    for n, copy in enumerate(started):
        if not any(copy is job["core"] for job in jobs[:6]):
            copy.wait_send()

    def wait_sent(i, c):
        to_core(i).wait_send()
        entering(i).wait_send()
        return c

    lax.fori_loop(0, CHIPS, wait_sent, 0)
    others(lambda i: to_owner(i).wait_send())
    others(lambda i: to_chip(i).wait_send())


def main(base, stream, cotangent, table, gain, w, mw, swt, bias, rate):
    vmem, anywhere = pl.BlockSpec(memory_space=pltpu.VMEM), pl.BlockSpec(memory_space=pl.ANY)
    rows = 2 * BASES

    def shape(*dims):
        return jax.ShapeDtypeStruct(dims, F32)

    def f32(*dims):
        return pltpu.VMEM(dims, F32)

    def bf16(*dims):
        return pltpu.VMEM(dims, BF16)

    def sems(n):
        return pltpu.SemaphoreType.DMA((n,))

    jobs = len(ORDER)
    return pl.pallas_call(
        main_kernel,
        out_shape=[
            shape(3, 16, WIDTH), shape(WIDTH, 128), shape(HEADS, WIDTH), shape(5, WIDTH), shape(1, WIDTH),
            shape(HEADS, 256), shape(BASES, WIDTH // 2),
        ],
        in_specs=[vmem] * 5 + [anywhere] + [vmem] * 4,
        out_specs=[vmem] * 7,
        scratch_shapes=[
            bf16(3, WIDTH, WIDTH), f32(8, WIDTH), bf16(rows, WIDTH), f32(rows, WIDTH), f32(rows, 1),
            f32(2, PAIRS, BASES, 128), f32(2, PAIRS, BASES, 128), f32(PAIRS, BASES, 128),
            bf16(2, BASES, 128), f32(2, HEADS, BASES), bf16(2, BASES, 128), bf16(2, 128, BASES), f32(2, HEADS, BASES),
            f32(2, HEADS, BASES), bf16(2, PAIRS, BASES, 128), bf16(2, PAIRS, BASES, 128),
            f32(2, PAIRS, BASES, 128), f32(2, PAIRS, BASES, 128), f32(2, BASES, BASES),
            f32(2, BASES, 128), f32(2, 8, 128), f32(2, BASES, STATE), f32(2, BASES, STATE),
            f32(2 * CHIPS, 72, 128), f32(CHIPS, 72, 128), f32(CHIPS, 72, 128), f32(CHIPS, 72, 128),
            f32(CHIPS, STATE, 128), f32(CHIPS, STATE, 128), f32(2 * CHIPS, STATE, 128), f32(CHIPS, STATE, 128),
            bf16(rows, WIDTH), bf16(rows, WIDTH), bf16(rows, WIDTH), bf16(rows, 128), f32(HEADS, rows), f32(HEADS, 2),
            bf16(WIDTH, rows), bf16(WIDTH, BASES), f32(128, WIDTH),
            f32(6, 2, 4, 4, 2, 32, 128), f32(jobs, 2, 4, 4, 32, 128), f32(jobs, 6, 4, 32, 128), f32(jobs, 2, 4, 32, 128),
            f32(jobs, 6, 32, 128), f32(jobs, 2, 32, 128), f32(jobs, 2, 16, 128),
            f32(4, 4, 2, 32, 256), f32(4, 4, 32, 256), f32(16, 32, 256), f32(2, 32, 256), f32(3, 32, 256),
            f32(4, 4, 2, 32, 256), f32(4, BASES, 128),
            sems(3), sems(CHIPS), sems(CHIPS), sems(CHIPS), sems(CHIPS), sems(CHIPS), sems(CHIPS), sems(CHIPS), sems(CHIPS),
            sems(SEMS), sems(SEMS),
        ],
        compiler_params=pltpu.CompilerParams(collective_id=0, has_side_effects=True, vmem_limit_bytes=61 << 20),
        name="main",
    )(base, stream, cotangent, table, gain, w, mw, swt, bias, rate)


def emit_kernel(grads, mixer, steps, by_base, by_gain, scalars, stream,
                grads_out, mixer_out, steps_out, base_out, gain_out, bias_out, rate_out, stream_out):
    for source, target in ((grads, grads_out), (mixer, mixer_out), (steps, steps_out), (by_base, base_out),
                           (by_gain, gain_out), (stream, stream_out)):
        target[...] = source[...]
    same = iota((HEADS, HEADS), 0) == iota((HEADS, HEADS), 1)
    for first, target in ((0, bias_out), (128, rate_out)):
        target[...] = jnp.sum(jnp.where(same, scalars[:, first:first + HEADS], 0.0), axis=0, keepdims=True)


def emit(*results):
    vmem = pl.BlockSpec(memory_space=pltpu.VMEM)
    like = [jax.ShapeDtypeStruct(r.shape, F32) for r in results]
    row = jax.ShapeDtypeStruct((1, HEADS), F32)
    return pl.pallas_call(
        emit_kernel,
        out_shape=like[:5] + [row, row] + like[6:],
        in_specs=[vmem] * 7,
        out_specs=[vmem] * 8,
        name="emit",
    )(*results)


def body(base_ids, stream, cotangent, table, gain, projections, mixer_weight, step_weight, step_bias, rate):
    results = main(
        base_ids, stream, cotangent, table, gain[None], jnp.transpose(projections, (1, 0, 2)), mixer_weight,
        jnp.transpose(step_weight), step_bias[None], rate[None])
    grads, mixer, steps, by_base, by_gain, by_bias, by_rate, stream_grad = emit(*results)
    return (
        jnp.transpose(grads, (1, 0, 2)),
        mixer,
        jnp.transpose(steps),
        by_bias[0],
        by_rate[0],
        by_base,
        by_gain[0],
        stream_grad[None],
    )


def solution(mesh):
    return jax.shard_map(
        body,
        mesh=mesh,
        in_specs=(
            P("dp", "ctx"),
            P("dp", "ctx", None),
            P("dp", "ctx", None),
            P(),
            P(),
            P(None, None, "tp"),
            P(),
            P(None, "tp"),
            P("tp"),
            P("tp"),
        ),
        out_specs=(
            P(("ctx", "dp"), None, "tp"),
            P(),
            P(None, "tp"),
            P("tp"),
            P("tp"),
            P(),
            P(),
            P("dp", "ctx", "tp"),
        ),
        check_vma=False,
    )
```

time: 176 us -> 113 us (0.64)
  Pallas kernels: 132 us -> 111 us
  matrix products: 19.8 us -> 0 us
  local copies, waits for them, and re-layouts: 18.4 us -> 0 us
  other arithmetic: 4.33 us -> 0 us
    pallas_call x2, Pallas kernels: 132 us -> 111 us  [the longest x1 108 us: main(): pl.pallas_call(main_kernel, out_shape=[shape(3, 16, WIDTH), shape(WIDTH,...]
    dot_general x10 -> x0, matrix products: 19.8 us -> none  [the longest x5 11.5 us: tn(): lax.dot_general(left, right, (((0,), (0,)), ((), ())), preferred_element_...]
    unnamed x40 -> x0, local copies, waits for them, and re-layouts: 5.57 us -> none
    add x2 -> x0, other arithmetic: 3.93 us -> none  [the longest x1 2.12 us: body(): ge = ge + 0.5 * jnp.concatenate([upstream, upstream], axis=0).astype(F32)]
    broadcast_in_dim x5 -> x0, local copies, waits for them, and re-layouts: 3.57 us -> none  [the longest x1 1.33 us: body(): step_bias[:, None]]
    concatenate x2 -> x0, local copies, waits for them, and re-layouts: 3.21 us -> none  [body(): small = jnp.concatenate([tn(features, gm), rest], axis=1)]
    slice x4 -> x0, local copies, waits for them, and re-layouts: 2.68 us -> none  [the longest x1 0.96 us: body(): small[:, 160]]
    dynamic_update_slice x2 -> x0, local copies, waits for them, and re-layouts: 2.29 us -> none  [the longest x1 2.29 us: body(): lax.dynamic_update_slice(jnp.zeros((WIDTH, 32), F32), gstep, (0, heads_at))]
where the time goes in v3:
time: 113 us; the launch traced here: 111 us
  Pallas kernels  111 us (98%)
    pallas_call x1, Pallas kernels, main(): pl.pallas_call(main_kernel, out_shape=[shape(3, 16, WIDTH), shape(WIDTH,...  108 us
    pallas_call x1, Pallas kernels, emit(): pl.pallas_call(emit_kernel, out_shape=like[:5] + [row, row] + like[6:], i...  2.43 us

profile of v3, /device:TPU:1, one launch (start us, length us, event | category | flops | bytes accessed | tf_op | source)
XLA Modules:
  0.0 111.3 jit_solution(1359125816484494573)
XLA Ops:
  0.6 108.3 %main.1 = (f32[3,16,1024]{2,1,0:T(8,128)}, f32[1024,128]{1,0:T(8,128)}, f32[16,1024]{1,0:T(8,128)}, f32[5,1024]{1,0:T(8,128)}, f32[1,1024]{1,0:T(1,128)}, /*index=5*/f32[16,256]{1,0:T(8,128)}, f32[256,512]{1,0:T(8,128)}) custom-call(s32[1,256]{1,0:T(1,128)} %base.1, bf16[1,256,1024]{2,1,0:T(8,128)(2,1)} %x.1, bf16[1,256,1024]{2,1,0:T(8,128)(2,1)} %up.1, ...), custom_call_target="tpu_custom_call" | custom-call | tf_op jit(solution)/shard_map/main/pallas_call | solution.py:609
  108.9 2.4 %emit.1 = (f32[3,16,1024]{2,1,0:T(8,128)}, f32[1024,128]{1,0:T(8,128)}, f32[16,1024]{1,0:T(8,128)}, f32[5,1024]{1,0:T(8,128)}, f32[1,1024]{1,0:T(1,128)}, /*inde...) custom-call(f32[3,16,1024]{2,1,0:T(8,128)} %get-tuple-element.23.grads, f32[1024,128]{1,0:T(8,128)} %get-tuple-element.24.mixer, ...), custom_call_target="tpu_custom_call" | custom-call | tf_op jit(solution)/shard_map/emit/pallas_call | solution.py:654

commit v4 on v3

--- a/solution.py
+++ b/solution.py
@@ -2,6 +2,7 @@
 
 import jax
 import jax.numpy as jnp
+import numpy as np
 from jax import lax
 from jax.experimental import pallas as pl
 from jax.experimental.pallas import tpu as pltpu
@@ -56,29 +57,22 @@
     return lax.broadcasted_iota(jnp.int32, shape, dim)
 
 
-def spreads(j):
-    r, c = iota((128, 256), 0), iota((128, 256), 1)
-    kind = (r >= 48).astype(jnp.int32) + (r >= 96).astype(jnp.int32)
-    return jnp.logical_and(kind == c // 128, (r & 15) == 2 * j + (c & 127) // 64).astype(F32).astype(BF16)
-
-
-def gathers(j, base):
-    r, c = iota((128, 128), 0), iota((128, 128), 1)
-    return (c == base + 2 * j + r // 64).astype(F32).astype(BF16)
+def spreads():
+    j, r, c = np.indices((PAIRS, 128, 256))
+    return np.logical_and(r // 48 == c // 128, r % 16 == 2 * j + c % 128 // 64).astype(np.float32)
 
 
 CHIPS = 16
-SEMS = 216
 ORDER = [(q, k) for q in range(4) for k in (2, 1, 0)]
 
 
-def main_kernel(base, x, up, table, gain, w, mw, swt, bias, rate,
+def main_kernel(base, x, up, table, gain, w, mw, swt, bias, rate, spread,
                 grads_out, mixer_out, step_out, table_out, gain_out, scalars_out, stream_out,
                 wv, tab, f, normed_s, inv_s, v, g, gg, quant, run_t, maps, maps_t, logit_t, step_t, drive_b, go_b, out, gd, pairs,
-                acc, kk, gins, greads, src, from_core, totals, recv, scanned, res, ent, ent_out,
-                gv, gate, gated, gm, glt, rates, ft, upt, rt, prod, core_in, ring, mid, ring2, fin, dp_in,
+                acc, acc_v, kk, gins, greads, swish_s, src, from_core, totals, recv, scanned, res, ent,
+                gv, gate, gm, glt, rates, ft, upt, rt, prod, core_in, ring, mid, ring2, fin, dp_in,
                 prod_e, core_e, parts, mine_e, x_in, all_e, tp_in,
-                wsem, send_c, recv_c, send_a, recv_a, send_b, recv_b, send_d, recv_d, send, receive):
+                wsem, core_sem, state_sem, job_recv, job_core, job_send, small_sem):
     ctx, tp, dp = lax.axis_index("ctx"), lax.axis_index("tp"), lax.axis_index("dp")
     core, chip = ctx % 2, ctx // 2
     y, z = chip % 4, chip // 4
@@ -146,6 +140,7 @@
         quant[d] = jnp.transpose(whole).astype(BF16)
         pairs[d] = jnp.zeros((BASES, BASES), F32)
         acc[d] = jnp.zeros((BASES, 128), F32)
+        acc_v[d] = jnp.zeros((BASES, 128), F32)
         kk[d] = jnp.zeros((8, 128), F32)
         gins[d] = jnp.zeros((BASES, STATE), F32)
         greads[d] = jnp.zeros((BASES, STATE), F32)
@@ -163,45 +158,34 @@
             gg[2 * c + i] = block[:, 128 * i:128 * i + 128]
 
     def expand(d, j):
-        both = dot(quant[d], spreads(j))
+        both = dot(quant[d], spread[j])
         run_e, step_e = both[:, 0:128], both[:, 128:256]
         final = run_e[BASES - 1:BASES] if d == 0 else run_e[0:1]
         return run_e, step_e, final
 
-    def to_core(i):
+    def remote(source, target, sent, arrived, device):
         return pltpu.make_async_remote_copy(
-            src_ref=src.at[CHIPS * (1 - core) + i], dst_ref=from_core.at[i], send_sem=send_c.at[i], recv_sem=recv_c.at[i],
-            device_id=other, device_id_type=MESH)
+            src_ref=source, dst_ref=target, send_sem=sent, recv_sem=arrived, device_id=device, device_id_type=MESH)
+
+    def to_core(i, half, n=1):
+        source = src.at[CHIPS * (1 - core) + i] if n == 1 else src.at[pl.ds(0, n)]
+        target = from_core.at[i] if n == 1 else from_core.at[pl.ds(i, n)]
+        return remote(source, target, core_sem.at[2], core_sem.at[half], other)
 
     def to_owner(i):
-        return pltpu.make_async_remote_copy(
-            src_ref=totals.at[i], dst_ref=recv.at[chip], send_sem=send_a.at[i], recv_sem=recv_a.at[chip],
-            device_id=on(i), device_id_type=MESH)
-
-    def from_chip(i):
-        return pltpu.make_async_remote_copy(
-            src_ref=totals.at[i], dst_ref=recv.at[i], send_sem=send_a.at[i], recv_sem=recv_a.at[i],
-            device_id=on(i), device_id_type=MESH)
+        return remote(totals.at[i], recv.at[chip], state_sem.at[0], state_sem.at[1], on(i))
+
+    all_to_owners = remote(totals.at[pl.ds(0, 15)], recv.at[pl.ds(0, 15)], state_sem.at[0], state_sem.at[1], other)
 
     def to_chip(i):
-        return pltpu.make_async_remote_copy(
-            src_ref=scanned.at[i], dst_ref=res.at[chip], send_sem=send_b.at[i], recv_sem=recv_b.at[chip],
-            device_id=on(i), device_id_type=MESH)
-
-    def from_owner(i):
-        return pltpu.make_async_remote_copy(
-            src_ref=scanned.at[i], dst_ref=res.at[i], send_sem=send_b.at[i], recv_sem=recv_b.at[i],
-            device_id=on(i), device_id_type=MESH)
+        return remote(scanned.at[i], res.at[chip], state_sem.at[2], state_sem.at[3], on(i))
+
+    all_to_chips = remote(scanned.at[pl.ds(0, 15)], res.at[pl.ds(0, 15)], state_sem.at[2], state_sem.at[3], other)
 
     def entering(i):
-        return pltpu.make_async_remote_copy(
-            src_ref=ent_out.at[i], dst_ref=ent.at[CHIPS * core + i], send_sem=send_d.at[i], recv_sem=recv_d.at[i],
-            device_id=other, device_id_type=MESH)
-
-    def entered(i):
-        return pltpu.make_async_remote_copy(
-            src_ref=ent_out.at[i], dst_ref=ent.at[CHIPS * (1 - core) + i], send_sem=send_d.at[i], recv_sem=recv_d.at[i],
-            device_id=other, device_id_type=MESH)
+        return remote(from_core.at[i, pl.ds(0, 64)], ent.at[CHIPS * core + i], state_sem.at[4], state_sem.at[5], other)
+
+    all_entering = remote(ent.at[pl.ds(CHIPS * core, CHIPS)], ent.at[pl.ds(CHIPS * (1 - core), CHIPS)], state_sem.at[4], state_sem.at[5], other)
 
     pl.semaphore_wait(barrier, CHIPS + 3)
     for d in range(2):
@@ -209,22 +193,30 @@
             run_e, step_e, final = expand(d, j)
             drive = step_e * v[d, j]
             gates = g[d, j]
-            go = gg[j] * (gates * jax.nn.sigmoid(gates))
+            sigma = jax.nn.sigmoid(gates)
+            swish = gates * sigma
+            go = gg[j] * swish
             drive_b[d, j] = drive.astype(BF16)
             go_b[d, j] = go.astype(BF16)
-            state = dot(maps_t[d, 0:64, :], (drive * jnp.exp(final - run_e)).astype(BF16))
-            grad = dot(maps_t[d, 64:128, :], (go * jnp.exp(run_e)).astype(BF16))
+            swish_s[d, j] = swish
+            late_drive = (drive * jnp.exp(final - run_e)).astype(BF16)
+            late_go = (go * jnp.exp(run_e)).astype(BF16)
+            lanes = pl.ds(pl.multiple_of(128 * j, 128), 128)
+            wv[2, BASES * d:BASES * (d + 1), lanes] = late_drive
+            wv[2, BASES * (d + 2):BASES * (d + 3), lanes] = late_go
+            state = dot(maps_t[d, 0:64, :], late_drive)
+            grad = dot(maps_t[d, 64:128, :], late_go)
             decay = jnp.broadcast_to(jnp.exp(final), (8, 128))
             for t, value in ((16 * d + j, state), (24 - 16 * d + j, grad)):
                 src[t, 0:64, :] = value
                 src[t, 64:72, :] = decay
-            to_core(j + 8 * (1 - core) if d == 0 else j + 8 * core).start()
+            half = (1 - core) if d == 0 else core
+            to_core(j + 8 * half, half).start()
             return c
 
         lax.fori_loop(0, PAIRS, ends, 0)
 
     def combine(i, c):
-        to_core(i).wait_recv()
         here, there = src[CHIPS * core + i], from_core[i]
         totals[i, 0:64, :] = here[0:64] * there[64:65] + there[0:64]
         totals[i, 64:72, :] = here[64:72] * there[64:72]
@@ -234,7 +226,10 @@
             to_owner(i).start()
         return c
 
-    lax.fori_loop(0, CHIPS, combine, 0)
+    for part in range(2):
+        half = (core + part) % 2
+        to_core(8 * half, half, 8).wait_recv()
+        lax.fori_loop(8 * half, 8 * half + 8, combine, 0)
 
     low = iota((BASES, 128), 1) < 64
 
@@ -269,15 +264,8 @@
 
     inside(0)
 
-    def others(act):
-        def step(i, c):
-            act(lax.rem(chip + i, CHIPS))
-            return c
-
-        lax.fori_loop(1, CHIPS, step, 0)
-
     recv[chip] = totals[chip]
-    others(lambda i: from_chip(i).wait_recv())
+    all_to_owners.wait_recv()
 
     def scan(i, carry):
         t = i + core * (CHIPS - 1 - 2 * i)
@@ -295,42 +283,42 @@
     for c in range(4):
         ft[256 * c:256 * c + 256, :] = jnp.transpose(f[:, 256 * c:256 * c + 256])
         upt[256 * c:256 * c + 256, :] = jnp.transpose(up[0, :, 256 * c:256 * c + 256])
-    others(lambda i: from_owner(i).wait_recv())
+    gated = f
+    for d in range(2):
+        def prepare(j, c, d=d):
+            gates, swish = g[d, j], swish_s[d, j]
+            sigma = jax.nn.sigmoid(gates)
+            g[d, j] = gg[j] * (sigma + swish * (1.0 - sigma))
+            return c
+
+        lax.fori_loop(0, PAIRS, prepare, 0)
+    all_to_chips.wait_recv()
 
     def hand_on(i, c):
         first = res[i]
         here = src[CHIPS * core + i]
-        ent_out[i] = first * here[64:65] + here[0:64]
+        from_core[i, 0:64, :] = first * here[64:65] + here[0:64]
         entering(i).start()
         ent[CHIPS * core + i] = first
         return c
 
     lax.fori_loop(0, CHIPS, hand_on, 0)
 
-    def wait_entered(i, c):
-        entered(i).wait_recv()
-        return c
-
-    lax.fori_loop(0, CHIPS, wait_entered, 0)
-
-    started = []
-
-    def put(source, target, device):
-        i = len(started)
-        copy = pltpu.make_async_remote_copy(
-            src_ref=source, dst_ref=target, send_sem=send.at[i], recv_sem=receive.at[i], device_id=device,
-            device_id_type=MESH)
+    all_entering.wait_recv()
+
+    def put(source, target, sent, arrived, device):
+        copy = remote(source, target, sent, arrived, device)
         copy.start()
-        started.append(copy)
         return copy
 
     jobs = []
     for n, (q, k) in enumerate(ORDER):
-        jobs.append(dict(stream=n % 2, prod=prod.at[n % 6], acc=core_in.at[n], ring=ring.at[n], mid=mid.at[n],
+        jobs.append(dict(n=n, stream=n % 2, prod=prod.at[n % 6], acc=core_in.at[n], ring=ring.at[n], mid=mid.at[n],
                          ring2=ring2.at[n], fin=fin.at[n], dp=dp_in.at[n]))
 
     def core_start(job):
-        job["core"] = put(job["prod"].at[:, :, :, 1 - core], job["acc"], other)
+        n = job["n"]
+        job["core"] = put(job["prod"].at[:, :, :, 1 - core], job["acc"], job_core.at[n], job_recv.at[6 * n], other)
 
     def core_end(job):
         job["core"].wait_recv()
@@ -352,30 +340,31 @@
         p, dev = place(job, stage)
         s = job["stream"]
         ref, buffer, _ = refs(job, stage)
-        job["m1"] = put(chunk(ref, 0, (p + 2) % 4, s, stage), buffer.at[0], dev[1])
-        job["m1p"] = put(chunk(ref, 1, (p + 2) % 4, s, stage), buffer.at[1], dev[3])
-        job["m2"] = put(chunk(ref, 1, (p + 1) % 4, s, stage), buffer.at[2], dev[1])
-        job["m2p"] = put(chunk(ref, 0, (p + 3) % 4, s, stage), buffer.at[3], dev[3])
+        sent, first, second = job_send.at[stage - 1], job_recv.at[6 * job["n"] + 2 * stage - 1], job_recv.at[6 * job["n"] + 2 * stage]
+        put(chunk(ref, 0, (p + 2) % 4, s, stage), buffer.at[0], sent, first, dev[1])
+        put(chunk(ref, 1, (p + 2) % 4, s, stage), buffer.at[1], sent, first, dev[3])
+        put(chunk(ref, 1, (p + 1) % 4, s, stage), buffer.at[2], sent, second, dev[1])
+        put(chunk(ref, 0, (p + 3) % 4, s, stage), buffer.at[3], sent, second, dev[3])
 
     def ring_middle(job, stage):
         p, dev = place(job, stage)
         s = job["stream"]
         ref, buffer, _ = refs(job, stage)
-        job["m1"].wait_recv()
+        sent, first, second = job_send.at[stage - 1], job_recv.at[6 * job["n"] + 2 * stage - 1], job_recv.at[6 * job["n"] + 2 * stage]
+        remote(buffer.at[pl.ds(0, 2)], buffer.at[pl.ds(0, 2)], sent, first, other).wait_recv()
         ahead = chunk(ref, 0, (p + 1) % 4, s, stage)
         ahead[...] = ahead[...] + buffer[0]
-        job["m3"] = put(ahead, buffer.at[4], dev[1])
-        job["m1p"].wait_recv()
+        put(ahead, buffer.at[4], sent, second, dev[1])
         behind = chunk(ref, 1, (p + 3) % 4, s, stage)
         behind[...] = behind[...] + buffer[1]
-        job["m3p"] = put(behind, buffer.at[5], dev[3])
+        put(behind, buffer.at[5], sent, second, dev[3])
 
     def ring_end(job, stage):
         p, dev = place(job, stage)
         s = job["stream"]
         ref, buffer, into = refs(job, stage)
-        for name in ("m2", "m2p", "m3", "m3p"):
-            job[name].wait_recv()
+        sent, second = job_send.at[stage - 1], job_recv.at[6 * job["n"] + 2 * stage]
+        remote(buffer.at[pl.ds(2, 4)], buffer.at[pl.ds(2, 4)], sent, second, other).wait_recv()
         into[0] = chunk(ref, 0, p, s, stage)[...] + buffer[3] + buffer[4]
         into[1] = chunk(ref, 1, p, s, stage)[...] + buffer[2] + buffer[5]
 
@@ -398,7 +387,8 @@
             ring_middle(job, 2)
         elif at == 4:
             ring_end(job, 2)
-            job["over_dp"] = put(job["fin"].at[:, yours, :], job["dp"], dp_dev)
+            job["over_dp"] = put(
+                job["fin"].at[:, yours, :], job["dp"], job_send.at[2], job_recv.at[6 * n + 5], dp_dev)
         else:
             q, k = ORDER[n]
             job["over_dp"].wait_recv()
@@ -419,22 +409,20 @@
             carried = dot(readout_b, initial_b) * head
             output = out[d, j] + carried
             grad_drive = gd[d, j] + dot(inflow_b, after_b) * tail
-            values, gates, grad_gated = v[d, j], g[d, j], gg[j]
-            sigma = jax.nn.sigmoid(gates)
-            swish = gates * sigma
+            values, to_heads = v[d, j], spread[j, :, 0:128]
             a, b = split2(grad_drive * drive_r - go_r * output)
-            p, r = split2(grad_drive * values)
-            acc[d] += dot(a, gathers(j, 0)) + dot(b, gathers(j, 0)) + dot(p, gathers(j, 16)) + dot(r, gathers(j, 16))
+            acc[d] += nt(a, to_heads) + nt(b, to_heads)
+            acc_v[d] += nt((grad_drive * values).astype(BF16), to_heads)
             boundary = jnp.sum(go_r * carried, axis=0, keepdims=True) + jnp.exp(final) * jnp.sum(
                 initial * after, axis=0, keepdims=True)
             a, b = split2(jnp.broadcast_to(boundary, (16, 128)))
-            kk[d] += (dot(a, gathers(j, 32)) + dot(b, gathers(j, 32)))[0:8]
-            gins[d] += nt((drive_r * tail).astype(BF16), after_b)
-            greads[d] += nt((go_r * head).astype(BF16), initial_b)
+            kk[d] += (nt(a, to_heads) + nt(b, to_heads))[0:8]
             lanes = pl.ds(pl.multiple_of(128 * j, 128), 128)
+            gins[d] += nt(wv[2, BASES * d:BASES * (d + 1), lanes], after_b)
+            greads[d] += nt(wv[2, BASES * (d + 2):BASES * (d + 3), lanes], initial_b)
             gv[rows, lanes] = (step_e * grad_drive).astype(BF16)
-            gate[rows, lanes] = (grad_gated * output * sigma * (1.0 + gates * (1.0 - sigma))).astype(BF16)
-            gated[rows, lanes] = (output * swish).astype(BF16)
+            gate[rows, lanes] = (g[d, j] * output).astype(BF16)
+            gated[rows, lanes] = (output * swish_s[d, j]).astype(BF16)
             return c
 
         lax.fori_loop(2 * q, 2 * q + 2, step, 0)
@@ -446,30 +434,34 @@
         if n >= 6:
             jobs[n - 6]["core"].wait_send()
 
-        def step(i, c):
-            rows = pl.ds(pl.multiple_of(256 * i, 256), 256)
+        for i in range(2):
+            rows = slice(512 * i, 512 * i + 512)
             if k == 2:
                 block = dot(upt[rows, :], result[0:BASES, lanes]) + dot(upt[rows, :], result[BASES:, lanes])
             else:
                 block = dot(ft[rows, :], result[:, lanes])
             for h in range(2):
-                prod[n % 6, h, i] = block[:, 128 * h:128 * h + 128].reshape(4, 2, 32, 128)
-            return c
-
-        lax.fori_loop(0, 4, step, 0)
+                prod[n % 6, h, 2 * i:2 * i + 2] = block[:, 128 * h:128 * h + 128].reshape(2, 4, 2, 32, 128)
         core_start(jobs[n])
 
-    for q in range(4):
-        outside(0, q)
-        if q:
-            go_on(3 * q - 1)
-        outside(1, q)
-        for n in range(3 * q, 3 * q + 3):
-            product(n)
-            if n > 3 * q:
-                go_on(n - 1)
-            if n >= 5:
-                go_on(n - 5)
+    outside(0, 0)
+    outside(1, 0)
+    for n in range(3):
+        product(n)
+    outside(0, 1)
+    for n in range(3):
+        go_on(n)
+    outside(1, 1)
+    for n in range(3, 6):
+        product(n)
+    outside(0, 2)
+    for n in range(3, 6):
+        go_on(n)
+    outside(1, 2)
+    outside(0, 3)
+    go_on(0)
+    go_on(1)
+    outside(1, 3)
 
     for d in range(2):
         rows = slice(BASES * d, BASES * (d + 1))
@@ -478,13 +470,14 @@
         gin = gins[d] + tn(pairs_b, readout_b)
         gread = greads[d] + dot(pairs_b, inflow_b)
         gm[rows, :] = jnp.concatenate([gin, gread], axis=1).astype(BF16)
-        per_head = jnp.transpose(acc[d] + kk[d, 0:1, :])
+        per_head = jnp.transpose(acc[d])
+        boundary = jnp.transpose(jnp.broadcast_to(kk[d, 0:1, :], (128, 128)))[0:16, 0:1]
         earlier = (rows_i < cols_i) if d == 0 else (rows_i > cols_i)
-        grad_log = summed3(per_head[0:16], earlier.astype(F32).astype(BF16)) + per_head[32:48]
-        grad_step = per_head[16:32] - grad_log * rate_c
+        grad_log = summed3(per_head[0:16], earlier.astype(F32).astype(BF16)) + boundary
+        grad_step = jnp.transpose(acc_v[d])[0:16] - grad_log * rate_c
         glt[:, rows] = grad_step * jax.nn.sigmoid(logit_t[d])
         rates[:, d:d + 1] = -jnp.sum(grad_log * step_t[d], axis=1, keepdims=True)
-    go_on(11)
+    go_on(2)
 
     glb = glt[...].astype(BF16)
     mean = [jnp.zeros((BASES, 1), F32)] * 2
@@ -502,7 +495,8 @@
             mean[d] = mean[d] + jnp.sum(scaled * nrm, axis=1, keepdims=True)
             by_gain = by_gain + jnp.sum(gf * nrm, axis=0, keepdims=True)
         rt[32:40, lanes] = jnp.broadcast_to(by_gain, (8, 256))
-    go_on(7)
+        if c in (1, 3):
+            go_on(3 + c // 2)
     for c in range(8):
         lanes = slice(128 * c, 128 * c + 128)
         residual = 0.5 * up[0, :, lanes].astype(F32)
@@ -516,48 +510,65 @@
                 by_base = by_base + dot(hots[d], part.astype(BF16))
         gg[c] = whole
         rt[40:48, lanes] = by_base
-    to_tp = put(gg.at[pl.ds(4 * (1 - tp), 4)], tp_in, tp_dev)
+    to_tp = put(gg.at[pl.ds(4 * (1 - tp), 4)], tp_in, small_sem.at[0], small_sem.at[1], tp_dev)
+    go_on(5)
 
     rt[0:32, :] = jnp.zeros((32, WIDTH), F32)
     rt[48:128, :] = jnp.zeros((80, WIDTH), F32)
     heads_at = pl.multiple_of(16 * tp, 16)
     scalars_at = pl.multiple_of(48 + 16 * tp, 16)
-    rt[pl.ds(heads_at, 16), :] = dot(glb, f[...])
+    rt[pl.ds(heads_at, 16), :] = nt(glb, ft[...])
     rt[pl.ds(scalars_at, 16), 0:128] = jnp.broadcast_to(jnp.sum(glt[...], axis=1, keepdims=True), (HEADS, 128))
     rt[pl.ds(scalars_at, 16), 128:256] = jnp.broadcast_to(rates[:, 0:1] + rates[:, 1:2], (HEADS, 128))
     for i in range(4):
         prod_e[i, :, :, :, 0:128] = dot(ft[256 * i:256 * i + 256, :], gm[...]).reshape(4, 2, 32, 128)
     for i in range(8):
         prod_e[i // 2, 2 * (i % 2):2 * (i % 2) + 2, :, :, 128:256] = rt[:, 128 * i:128 * i + 128].reshape(2, 2, 32, 128)
-    small_core = put(prod_e.at[:, :, 1 - core], core_e, other)
-    for n in (0, 1):
-        go_on(n)
+    small_core = put(prod_e.at[:, :, 1 - core], core_e, small_sem.at[2], small_sem.at[3], other)
+    product(6)
+    product(7)
     small_core.wait_recv()
     core_e[...] = core_e[...] + prod_e[:, :, core]
     offsets = [(dz, dy) for dz in range(4) for dy in range(4)][1:]
-    small_in = [put(core_e.at[(z + dz) % 4, (y + dy) % 4], parts.at[4 * dz + dy], on(((z + dz) % 4) * 4 + (y + dy) % 4))
-                for dz, dy in offsets]
-    for n in (8, 2, 3, 4, 0, 1):
+
+    def to_all(source, place_of, sent, arrived):
+        for dz, dy in offsets:
+            zz, yy = (z + dz) % 4, (y + dy) % 4
+            mine_of, theirs = source(zz, yy), place_of(4 * dz + dy)
+            put(mine_of, theirs, sent, arrived, on(zz * 4 + yy))
+        return remote(parts.at[pl.ds(1, 15)], parts.at[pl.ds(1, 15)], sent, arrived, other)
+
+    small_in = to_all(lambda zz, yy: core_e.at[zz, yy], lambda i: parts.at[i], small_sem.at[4], small_sem.at[5])
+    go_on(6)
+    product(8)
+    go_on(7)
+    product(9)
+    go_on(8)
+    product(10)
+    for n in (9, 0, 1):
         go_on(n)
+    product(11)
+    for n in (10, 2, 3, 11):
+        go_on(n)
+    small_in.wait_recv()
     total = core_e[z, y]
-    for i, copy in enumerate(small_in):
-        copy.wait_recv()
+    for i in range(15):
         total = total + parts[i + 1]
     mine_e[0] = total
-    over_x = [put(mine_e.at[0], x_in.at[i], device) for i, device in enumerate((tp_dev, dp_dev, far_dev))]
-    for n in (9, 5, 6, 2, 3):
+    for i, device in enumerate((tp_dev, dp_dev, far_dev)):
+        put(mine_e.at[0], x_in.at[i], small_sem.at[6], small_sem.at[7], device)
+    over_x = remote(x_in, x_in, small_sem.at[6], small_sem.at[7], other)
+    for n in (4, 5, 0, 1, 6, 7):
         go_on(n)
-    for copy in over_x:
-        copy.wait_recv()
+    over_x.wait_recv()
     mine_e[1] = (mine_e[0] + x_in[0]) + (x_in[1] + x_in[2])
     all_e[z, y, core] = mine_e[1]
-    small_back = [put(mine_e.at[1], all_e.at[z, y, core], on(((z + dz) % 4) * 4 + (y + dy) % 4)) for dz, dy in offsets]
-    for n in (10, 11, 7, 8, 4, 0, 1, 5, 2, 6, 3):
+    small_back = to_all(lambda zz, yy: mine_e.at[1], lambda i: all_e.at[z, y, core], small_sem.at[8], small_sem.at[9])
+    for n in (2, 3, 8, 9, 0, 1, 4, 5, 10, 11):
         go_on(n)
-    for copy in small_back:
-        copy.wait_recv()
-    back_core = put(all_e.at[:, :, core], all_e.at[:, :, core], other)
-    for n in (9, 10, 11, 7, 8, 4, 5):
+    small_back.wait_recv()
+    back_core = put(all_e.at[:, :, core], all_e.at[:, :, core], small_sem.at[10], small_sem.at[11], other)
+    for n in (2, 3, 6, 7, 4, 5, 8, 9):
         go_on(n)
     to_tp.wait_recv()
     for i in range(4):
@@ -575,21 +586,19 @@
         for n, job in enumerate(jobs):
             if job["at"] == low_at:
                 go_on(n)
-    for n, copy in enumerate(started):
-        if not any(copy is job["core"] for job in jobs[:6]):
-            copy.wait_send()
-
-    def wait_sent(i, c):
-        to_core(i).wait_send()
-        entering(i).wait_send()
-        return c
-
-    lax.fori_loop(0, CHIPS, wait_sent, 0)
-    others(lambda i: to_owner(i).wait_send())
-    others(lambda i: to_chip(i).wait_send())
-
-
-def main(base, stream, cotangent, table, gain, w, mw, swt, bias, rate):
+    for n in range(6, 12):
+        jobs[n]["core"].wait_send()
+    remote(ring, ring, job_send.at[0], job_recv.at[0], other).wait_send()
+    remote(ring2, ring2, job_send.at[1], job_recv.at[0], other).wait_send()
+    remote(dp_in, dp_in, job_send.at[2], job_recv.at[0], other).wait_send()
+    for copy in (to_tp, small_core, small_in, over_x, small_back, back_core):
+        copy.wait_send()
+    to_core(0, 0, 16).wait_send()
+    for copy in (all_to_owners, all_to_chips, all_entering):
+        copy.wait_send()
+
+
+def main(base, stream, cotangent, table, gain, w, mw, swt, bias, rate, spread):
     vmem, anywhere = pl.BlockSpec(memory_space=pltpu.VMEM), pl.BlockSpec(memory_space=pl.ANY)
     rows = 2 * BASES
 
@@ -612,7 +621,7 @@
             shape(3, 16, WIDTH), shape(WIDTH, 128), shape(HEADS, WIDTH), shape(5, WIDTH), shape(1, WIDTH),
             shape(HEADS, 256), shape(BASES, WIDTH // 2),
         ],
-        in_specs=[vmem] * 5 + [anywhere] + [vmem] * 4,
+        in_specs=[vmem] * 5 + [anywhere] + [vmem] * 5,
         out_specs=[vmem] * 7,
         scratch_shapes=[
             bf16(3, WIDTH, WIDTH), f32(8, WIDTH), bf16(rows, WIDTH), f32(rows, WIDTH), f32(rows, 1),
@@ -620,21 +629,21 @@
             bf16(2, BASES, 128), f32(2, HEADS, BASES), bf16(2, BASES, 128), bf16(2, 128, BASES), f32(2, HEADS, BASES),
             f32(2, HEADS, BASES), bf16(2, PAIRS, BASES, 128), bf16(2, PAIRS, BASES, 128),
             f32(2, PAIRS, BASES, 128), f32(2, PAIRS, BASES, 128), f32(2, BASES, BASES),
-            f32(2, BASES, 128), f32(2, 8, 128), f32(2, BASES, STATE), f32(2, BASES, STATE),
+            f32(2, BASES, 128), f32(2, BASES, 128), f32(2, 8, 128), f32(2, BASES, STATE), f32(2, BASES, STATE),
+            f32(2, PAIRS, BASES, 128),
             f32(2 * CHIPS, 72, 128), f32(CHIPS, 72, 128), f32(CHIPS, 72, 128), f32(CHIPS, 72, 128),
-            f32(CHIPS, STATE, 128), f32(CHIPS, STATE, 128), f32(2 * CHIPS, STATE, 128), f32(CHIPS, STATE, 128),
-            bf16(rows, WIDTH), bf16(rows, WIDTH), bf16(rows, WIDTH), bf16(rows, 128), f32(HEADS, rows), f32(HEADS, 2),
+            f32(CHIPS, STATE, 128), f32(CHIPS, STATE, 128), f32(2 * CHIPS, STATE, 128),
+            bf16(rows, WIDTH), bf16(rows, WIDTH), bf16(rows, 128), f32(HEADS, rows), f32(HEADS, 2),
             bf16(WIDTH, rows), bf16(WIDTH, BASES), f32(128, WIDTH),
             f32(6, 2, 4, 4, 2, 32, 128), f32(jobs, 2, 4, 4, 32, 128), f32(jobs, 6, 4, 32, 128), f32(jobs, 2, 4, 32, 128),
             f32(jobs, 6, 32, 128), f32(jobs, 2, 32, 128), f32(jobs, 2, 16, 128),
             f32(4, 4, 2, 32, 256), f32(4, 4, 32, 256), f32(16, 32, 256), f32(2, 32, 256), f32(3, 32, 256),
             f32(4, 4, 2, 32, 256), f32(4, BASES, 128),
-            sems(3), sems(CHIPS), sems(CHIPS), sems(CHIPS), sems(CHIPS), sems(CHIPS), sems(CHIPS), sems(CHIPS), sems(CHIPS),
-            sems(SEMS), sems(SEMS),
+            sems(3), sems(3), sems(6), sems(6 * jobs), sems(jobs), sems(3), sems(12),
         ],
-        compiler_params=pltpu.CompilerParams(collective_id=0, has_side_effects=True, vmem_limit_bytes=61 << 20),
+        compiler_params=pltpu.CompilerParams(collective_id=0, has_side_effects=True, vmem_limit_bytes=62 << 20),
         name="main",
-    )(base, stream, cotangent, table, gain, w, mw, swt, bias, rate)
+    )(base, stream, cotangent, table, gain, w, mw, swt, bias, rate, spread)
 
 
 def emit_kernel(grads, mixer, steps, by_base, by_gain, scalars, stream,
@@ -663,7 +672,7 @@
 def body(base_ids, stream, cotangent, table, gain, projections, mixer_weight, step_weight, step_bias, rate):
     results = main(
         base_ids, stream, cotangent, table, gain[None], jnp.transpose(projections, (1, 0, 2)), mixer_weight,
-        jnp.transpose(step_weight), step_bias[None], rate[None])
+        jnp.transpose(step_weight), step_bias[None], rate[None], jnp.asarray(spreads(), BF16))
     grads, mixer, steps, by_base, by_gain, by_bias, by_rate, stream_grad = emit(*results)
     return (
         jnp.transpose(grads, (1, 0, 2)),

time: 113 us -> 104 us (0.920)
  Pallas kernels: 111 us -> 102 us
    pallas_call x1, Pallas kernels: 108 us -> 99.3 us  [main(): pl.pallas_call(main_kernel, out_shape=[shape(3, 16, WIDTH), shape(WIDTH,...]
where the time goes in v4:
time: 104 us; the launch traced here: 102 us
  Pallas kernels  102 us (98%)
    pallas_call x1, Pallas kernels, main(): pl.pallas_call(main_kernel, out_shape=[shape(3, 16, WIDTH), shape(WIDTH,...  99.3 us
    pallas_call x1, Pallas kernels, emit(): pl.pallas_call(emit_kernel, out_shape=like[:5] + [row, row] + like[6:], i...  2.43 us

profile of v4, /device:TPU:1, one launch (start us, length us, event | category | flops | bytes accessed | tf_op | source)
XLA Modules:
  0.0 102.4 jit_solution(4711381416877111111)
XLA Ops:
  0.6 99.3 %main.1 = (f32[3,16,1024]{2,1,0:T(8,128)}, f32[1024,128]{1,0:T(8,128)}, f32[16,1024]{1,0:T(8,128)}, f32[5,1024]{1,0:T(8,128)}, f32[1,1024]{1,0:T(1,128)}, /*index=5*/f32[16,256]{1,0:T(8,128)}, f32[256,512]{1,0:T(8,128)}) custom-call(s32[1,256]{1,0:T(1,128)} %base.1, bf16[1,256,1024]{2,1,0:T(8,128)(2,1)} %x.1, bf16[1,256,1024]{2,1,0:T(8,128)(2,1)} %up.1, ...), custom_call_target="tpu_custom_call" | custom-call | tf_op jit(solution)/shard_map/main/pallas_call | solution.py:618
  99.9 2.4 %emit.1 = (f32[3,16,1024]{2,1,0:T(8,128)}, f32[1024,128]{1,0:T(8,128)}, f32[16,1024]{1,0:T(8,128)}, f32[5,1024]{1,0:T(8,128)}, f32[1,1024]{1,0:T(1,128)}, /*inde...) custom-call(f32[3,16,1024]{2,1,0:T(8,128)} %get-tuple-element.23.grads, f32[1024,128]{1,0:T(8,128)} %get-tuple-element.24.mixer, ...), custom_call_target="tpu_custom_call" | custom-call | tf_op jit(solution)/shard_map/emit/pallas_call | solution.py:663

commit v5 on v4

--- a/solution.py
+++ b/solution.py
@@ -64,14 +64,35 @@
 
 CHIPS = 16
 ORDER = [(q, k) for q in range(4) for k in (2, 1, 0)]
+PLAN = [
+    ("outside", 0, 0), ("outside", 1, 0), ("product", 0), ("product", 1), ("product", 2), ("outside", 0, 1),
+    ("outside", 1, 1), ("job", 0), ("job", 1), ("product", 3), ("product", 4), ("job", 2),
+    ("product", 5), ("outside", 0, 2), ("job", 3), ("outside", 1, 2), ("job", 0), ("job", 4),
+    ("job", 1), ("outside", 0, 3), ("job", 5), ("outside", 1, 3), ("job", 2), ("finish",),
+    ("job", 3), ("small", 0, 0), ("features", 0), ("features", 1), ("job", 0), ("job", 1),
+    ("features", 2), ("small", 0, 1), ("job", 4), ("features", 3), ("job", 5), ("embedded",),
+    ("small", 1, 0), ("product", 6), ("job", 2), ("job", 3), ("job", 1), ("job", 0),
+    ("product", 7), ("small", 1, 1), ("job", 4), ("small", 0, 2), ("job", 5), ("job", 6),
+    ("product", 8), ("job", 2), ("job", 3), ("job", 7), ("job", 0), ("job", 1),
+    ("product", 9), ("job", 4), ("product", 10), ("job", 8), ("product", 11), ("job", 5),
+    ("job", 2), ("small", 1, 2), ("job", 9), ("job", 10), ("job", 6), ("small", 0, 3),
+    ("job", 7), ("job", 11), ("job", 3), ("job", 4), ("job", 8), ("small", 0, 4),
+    ("job", 9), ("job", 5), ("job", 7), ("job", 10), ("small", 1, 3), ("job", 11),
+    ("job", 0), ("job", 1), ("job", 2), ("job", 3), ("job", 4), ("job", 6),
+    ("job", 5), ("small", 1, 4), ("job", 8), ("job", 9), ("job", 7), ("job", 11),
+    ("job", 6), ("small", 0, 5), ("job", 10), ("job", 8), ("job", 9), ("job", 6),
+    ("job", 7), ("job", 11), ("job", 10), ("small", 1, 5), ("job", 8), ("job", 9),
+    ("small", 0, 6), ("job", 11), ("job", 10), ("job", 6), ("small", 0, 7), ("job", 7),
+    ("small", 1, 6), ("job", 8), ("small", 1, 7), ("job", 9), ("job", 11), ("job", 10),
+]
 
 
 def main_kernel(base, x, up, table, gain, w, mw, swt, bias, rate, spread,
                 grads_out, mixer_out, step_out, table_out, gain_out, scalars_out, stream_out,
-                wv, tab, f, normed_s, inv_s, v, g, gg, quant, run_t, maps, maps_t, logit_t, step_t, drive_b, go_b, out, gd, pairs,
-                acc, acc_v, kk, gins, greads, swish_s, src, from_core, totals, recv, scanned, res, ent,
+                wv, f, normed_s, inv_s, v, g, gg, quant, run_t, maps, maps_t, logit_t, step_t, drive_b, go_b, out, gd, pairs,
+                acc, acc_v, kk, gmaps, swish_s, src, from_core, totals, recv, scanned, res, ent,
                 gv, gate, gm, glt, rates, ft, upt, rt, prod, core_in, ring, mid, ring2, fin, dp_in,
-                prod_e, core_e, parts, mine_e, x_in, all_e, tp_in,
+                prod_e, core_e, parts, mine_e, far_in, tp_in_e, sum_x, gat, all_e, tp_in,
                 wsem, core_sem, state_sem, job_recv, job_core, job_send, small_sem):
     ctx, tp, dp = lax.axis_index("ctx"), lax.axis_index("tp"), lax.axis_index("dp")
     core, chip = ctx % 2, ctx // 2
@@ -98,9 +119,9 @@
     for copy in copies:
         copy.start()
 
-    tab[...] = jnp.zeros_like(tab)
-    tab[0:5, :] = table[...]
-    pieces = jnp.concatenate(split3(tab[...]), axis=0).astype(BF16)
+    rt[0:8, :] = jnp.zeros((8, WIDTH), F32)
+    rt[0:5, :] = table[...]
+    pieces = jnp.concatenate(split3(rt[0:8, :]), axis=0).astype(BF16)
     incoming = x[0].astype(F32)
     hots = []
     for d in range(2):
@@ -142,8 +163,7 @@
         acc[d] = jnp.zeros((BASES, 128), F32)
         acc_v[d] = jnp.zeros((BASES, 128), F32)
         kk[d] = jnp.zeros((8, 128), F32)
-        gins[d] = jnp.zeros((BASES, STATE), F32)
-        greads[d] = jnp.zeros((BASES, STATE), F32)
+        gmaps[d] = jnp.zeros((BASES, 128), F32)
     for k, target in ((0, v), (1, g)):
         copies[k].wait()
         for c in range(4):
@@ -188,8 +208,9 @@
     all_entering = remote(ent.at[pl.ds(CHIPS * core, CHIPS)], ent.at[pl.ds(CHIPS * (1 - core), CHIPS)], state_sem.at[4], state_sem.at[5], other)
 
     pl.semaphore_wait(barrier, CHIPS + 3)
-    for d in range(2):
-        def ends(j, c, d=d):
+
+    def ends(d, first, last):
+        def step(j, c):
             run_e, step_e, final = expand(d, j)
             drive = step_e * v[d, j]
             gates = g[d, j]
@@ -214,7 +235,7 @@
             to_core(j + 8 * half, half).start()
             return c
 
-        lax.fori_loop(0, PAIRS, ends, 0)
+        lax.fori_loop(first, last, step, 0)
 
     def combine(i, c):
         here, there = src[CHIPS * core + i], from_core[i]
@@ -226,10 +247,15 @@
             to_owner(i).start()
         return c
 
-    for part in range(2):
-        half = (core + part) % 2
+    def combine_half(half):
         to_core(8 * half, half, 8).wait_recv()
         lax.fori_loop(8 * half, 8 * half + 8, combine, 0)
+
+    ends(0, 0, PAIRS)
+    ends(1, 0, PAIRS // 2)
+    combine_half(core)
+    ends(1, PAIRS // 2, PAIRS)
+    combine_half(1 - core)
 
     low = iota((BASES, 128), 1) < 64
 
@@ -375,6 +401,7 @@
         job = jobs[n]
         at = job.get("at", 0)
         job["at"] = at + 1
+        q, k = ORDER[n]
         if at == 0:
             core_end(job)
             ring_start(job, 1)
@@ -390,7 +417,6 @@
             job["over_dp"] = put(
                 job["fin"].at[:, yours, :], job["dp"], job_send.at[2], job_recv.at[6 * n + 5], dp_dev)
         else:
-            q, k = ORDER[n]
             job["over_dp"].wait_recv()
             for h in range(2):
                 first = 256 * q + 128 * h
@@ -418,8 +444,8 @@
             a, b = split2(jnp.broadcast_to(boundary, (16, 128)))
             kk[d] += (nt(a, to_heads) + nt(b, to_heads))[0:8]
             lanes = pl.ds(pl.multiple_of(128 * j, 128), 128)
-            gins[d] += nt(wv[2, BASES * d:BASES * (d + 1), lanes], after_b)
-            greads[d] += nt(wv[2, BASES * (d + 2):BASES * (d + 3), lanes], initial_b)
+            gmaps[d, :, 0:64] += nt(wv[2, BASES * d:BASES * (d + 1), lanes], after_b)
+            gmaps[d, :, 64:128] += nt(wv[2, BASES * (d + 2):BASES * (d + 3), lanes], initial_b)
             gv[rows, lanes] = (step_e * grad_drive).astype(BF16)
             gate[rows, lanes] = (g[d, j] * output).astype(BF16)
             gated[rows, lanes] = (output * swish_s[d, j]).astype(BF16)
@@ -444,44 +470,26 @@
                 prod[n % 6, h, 2 * i:2 * i + 2] = block[:, 128 * h:128 * h + 128].reshape(2, 4, 2, 32, 128)
         core_start(jobs[n])
 
-    outside(0, 0)
-    outside(1, 0)
-    for n in range(3):
-        product(n)
-    outside(0, 1)
-    for n in range(3):
-        go_on(n)
-    outside(1, 1)
-    for n in range(3, 6):
-        product(n)
-    outside(0, 2)
-    for n in range(3, 6):
-        go_on(n)
-    outside(1, 2)
-    outside(0, 3)
-    go_on(0)
-    go_on(1)
-    outside(1, 3)
-
-    for d in range(2):
-        rows = slice(BASES * d, BASES * (d + 1))
-        inflow_b, readout_b = maps[d, :, 0:64], maps[d, :, 64:128]
-        pairs_b = pairs[d].astype(BF16)
-        gin = gins[d] + tn(pairs_b, readout_b)
-        gread = greads[d] + dot(pairs_b, inflow_b)
-        gm[rows, :] = jnp.concatenate([gin, gread], axis=1).astype(BF16)
-        per_head = jnp.transpose(acc[d])
-        boundary = jnp.transpose(jnp.broadcast_to(kk[d, 0:1, :], (128, 128)))[0:16, 0:1]
-        earlier = (rows_i < cols_i) if d == 0 else (rows_i > cols_i)
-        grad_log = summed3(per_head[0:16], earlier.astype(F32).astype(BF16)) + boundary
-        grad_step = jnp.transpose(acc_v[d])[0:16] - grad_log * rate_c
-        glt[:, rows] = grad_step * jax.nn.sigmoid(logit_t[d])
-        rates[:, d:d + 1] = -jnp.sum(grad_log * step_t[d], axis=1, keepdims=True)
-    go_on(2)
-
-    glb = glt[...].astype(BF16)
+    def finish():
+        for d in range(2):
+            rows = slice(BASES * d, BASES * (d + 1))
+            inflow_b, readout_b = maps[d, :, 0:64], maps[d, :, 64:128]
+            pairs_b = pairs[d].astype(BF16)
+            gin = gmaps[d, :, 0:64] + tn(pairs_b, readout_b)
+            gread = gmaps[d, :, 64:128] + dot(pairs_b, inflow_b)
+            gm[rows, :] = jnp.concatenate([gin, gread], axis=1).astype(BF16)
+            per_head = jnp.transpose(acc[d])
+            boundary = jnp.transpose(jnp.broadcast_to(kk[d, 0:1, :], (128, 128)))[0:16, 0:1]
+            earlier = (rows_i < cols_i) if d == 0 else (rows_i > cols_i)
+            grad_log = summed3(per_head[0:16], earlier.astype(F32).astype(BF16)) + boundary
+            grad_step = jnp.transpose(acc_v[d])[0:16] - grad_log * rate_c
+            glt[:, rows] = grad_step * jax.nn.sigmoid(logit_t[d])
+            rates[:, d:d + 1] = -jnp.sum(grad_log * step_t[d], axis=1, keepdims=True)
+
     mean = [jnp.zeros((BASES, 1), F32)] * 2
-    for c in range(4):
+
+    def features(c):
+        glb = glt[...].astype(BF16)
         lanes = slice(256 * c, 256 * c + 256)
         by_gain = jnp.zeros((1, 256), F32)
         for d in range(2):
@@ -495,104 +503,112 @@
             mean[d] = mean[d] + jnp.sum(scaled * nrm, axis=1, keepdims=True)
             by_gain = by_gain + jnp.sum(gf * nrm, axis=0, keepdims=True)
         rt[32:40, lanes] = jnp.broadcast_to(by_gain, (8, 256))
-        if c in (1, 3):
-            go_on(3 + c // 2)
-    for c in range(8):
-        lanes = slice(128 * c, 128 * c + 128)
-        residual = 0.5 * up[0, :, lanes].astype(F32)
-        by_base = jnp.zeros((8, 128), F32)
-        whole = None
-        for d in range(2):
-            rows = slice(BASES * d, BASES * (d + 1))
-            ge = inv_s[rows, :] * (v[d, c] - normed_s[rows, lanes] * (mean[d] * (1.0 / WIDTH))) + residual
-            whole = ge if whole is None else whole + ge
-            for part in split3(ge):
-                by_base = by_base + dot(hots[d], part.astype(BF16))
-        gg[c] = whole
-        rt[40:48, lanes] = by_base
-    to_tp = put(gg.at[pl.ds(4 * (1 - tp), 4)], tp_in, small_sem.at[0], small_sem.at[1], tp_dev)
-    go_on(5)
-
-    rt[0:32, :] = jnp.zeros((32, WIDTH), F32)
-    rt[48:128, :] = jnp.zeros((80, WIDTH), F32)
+
+    def embedded_grad():
+        for c in range(8):
+            lanes = slice(128 * c, 128 * c + 128)
+            residual = 0.5 * up[0, :, lanes].astype(F32)
+            by_base = jnp.zeros((8, 128), F32)
+            whole = None
+            for d in range(2):
+                rows = slice(BASES * d, BASES * (d + 1))
+                ge = inv_s[rows, :] * (v[d, c] - normed_s[rows, lanes] * (mean[d] * (1.0 / WIDTH))) + residual
+                whole = ge if whole is None else whole + ge
+                for part in split3(ge):
+                    by_base = by_base + dot(hots[d], part.astype(BF16))
+            gg[c] = whole
+            rt[40:48, lanes] = by_base
+
     heads_at = pl.multiple_of(16 * tp, 16)
     scalars_at = pl.multiple_of(48 + 16 * tp, 16)
-    rt[pl.ds(heads_at, 16), :] = nt(glb, ft[...])
-    rt[pl.ds(scalars_at, 16), 0:128] = jnp.broadcast_to(jnp.sum(glt[...], axis=1, keepdims=True), (HEADS, 128))
-    rt[pl.ds(scalars_at, 16), 128:256] = jnp.broadcast_to(rates[:, 0:1] + rates[:, 1:2], (HEADS, 128))
-    for i in range(4):
-        prod_e[i, :, :, :, 0:128] = dot(ft[256 * i:256 * i + 256, :], gm[...]).reshape(4, 2, 32, 128)
-    for i in range(8):
-        prod_e[i // 2, 2 * (i % 2):2 * (i % 2) + 2, :, :, 128:256] = rt[:, 128 * i:128 * i + 128].reshape(2, 2, 32, 128)
-    small_core = put(prod_e.at[:, :, 1 - core], core_e, small_sem.at[2], small_sem.at[3], other)
-    product(6)
-    product(7)
-    small_core.wait_recv()
-    core_e[...] = core_e[...] + prod_e[:, :, core]
     offsets = [(dz, dy) for dz in range(4) for dy in range(4)][1:]
-
-    def to_all(source, place_of, sent, arrived):
-        for dz, dy in offsets:
-            zz, yy = (z + dz) % 4, (y + dy) % 4
-            mine_of, theirs = source(zz, yy), place_of(4 * dz + dy)
-            put(mine_of, theirs, sent, arrived, on(zz * 4 + yy))
-        return remote(parts.at[pl.ds(1, 15)], parts.at[pl.ds(1, 15)], sent, arrived, other)
-
-    small_in = to_all(lambda zz, yy: core_e.at[zz, yy], lambda i: parts.at[i], small_sem.at[4], small_sem.at[5])
-    go_on(6)
-    product(8)
-    go_on(7)
-    product(9)
-    go_on(8)
-    product(10)
-    for n in (9, 0, 1):
-        go_on(n)
-    product(11)
-    for n in (10, 2, 3, 11):
-        go_on(n)
-    small_in.wait_recv()
-    total = core_e[z, y]
-    for i in range(15):
-        total = total + parts[i + 1]
-    mine_e[0] = total
-    for i, device in enumerate((tp_dev, dp_dev, far_dev)):
-        put(mine_e.at[0], x_in.at[i], small_sem.at[6], small_sem.at[7], device)
-    over_x = remote(x_in, x_in, small_sem.at[6], small_sem.at[7], other)
-    for n in (4, 5, 0, 1, 6, 7):
-        go_on(n)
-    over_x.wait_recv()
-    mine_e[1] = (mine_e[0] + x_in[0]) + (x_in[1] + x_in[2])
-    all_e[z, y, core] = mine_e[1]
-    small_back = to_all(lambda zz, yy: mine_e.at[1], lambda i: all_e.at[z, y, core], small_sem.at[8], small_sem.at[9])
-    for n in (2, 3, 8, 9, 0, 1, 4, 5, 10, 11):
-        go_on(n)
-    small_back.wait_recv()
-    back_core = put(all_e.at[:, :, core], all_e.at[:, :, core], small_sem.at[10], small_sem.at[11], other)
-    for n in (2, 3, 6, 7, 4, 5, 8, 9):
-        go_on(n)
-    to_tp.wait_recv()
+    small = [{}, {}]
+
+    def small_step(h, at):
+        now = small[h]
+
+        def pair(i):
+            return small_sem.at[2 + 12 * h + 2 * i], small_sem.at[3 + 12 * h + 2 * i]
+
+        fifteen = parts.at[h, pl.ds(1, 15)]
+        if at == 0:
+            if h == 0:
+                for i in range(4):
+                    prod_e[0, i] = dot(ft[256 * i:256 * i + 256, :], gm[...]).reshape(4, 2, 32, 128)
+            else:
+                rt[0:32, :] = jnp.zeros((32, WIDTH), F32)
+                rt[48:128, :] = jnp.zeros((80, WIDTH), F32)
+                rt[pl.ds(heads_at, 16), :] = nt(glt[...].astype(BF16), ft[...])
+                rt[pl.ds(scalars_at, 16), 0:128] = jnp.broadcast_to(
+                    jnp.sum(glt[...], axis=1, keepdims=True), (HEADS, 128))
+                rt[pl.ds(scalars_at, 16), 128:256] = jnp.broadcast_to(rates[:, 0:1] + rates[:, 1:2], (HEADS, 128))
+                for i in range(8):
+                    prod_e[1, i // 2, 2 * (i % 2):2 * (i % 2) + 2] = rt[:, 128 * i:128 * i + 128].reshape(2, 2, 32, 128)
+            now[0] = put(prod_e.at[h, :, :, 1 - core], core_e.at[h], *pair(0), other)
+        elif at == 1:
+            now[0].wait_recv()
+            core_e[h] = core_e[h] + prod_e[h, :, :, core]
+            now[1] = put(core_e.at[h, :, :, yours], far_in.at[h], *pair(1), far_dev)
+            if h == 1:
+                now["tp"] = put(gg.at[pl.ds(4 * (1 - tp), 4)], tp_in, small_sem.at[0], small_sem.at[1], tp_dev)
+        elif at == 2:
+            now[1].wait_recv()
+            sum_x[h] = core_e[h, :, :, mine] + far_in[h]
+            for dz, dy in offsets:
+                zz, yy = (z + dz) % 4, (y + dy) % 4
+                put(sum_x.at[h, zz, yy], parts.at[h, 4 * dz + dy], *pair(2), on(zz * 4 + yy))
+            now[2] = remote(fifteen, fifteen, *pair(2), other)
+        elif at == 3:
+            now[2].wait_recv()
+            total = sum_x[h, z, y]
+            for i in range(15):
+                total = total + parts[h, i + 1]
+            mine_e[h, 0] = total
+            now[3] = put(mine_e.at[h, 0], tp_in_e.at[h], *pair(3), tp_dev)
+        elif at == 4:
+            now[3].wait_recv()
+            total = mine_e[h, 0] + tp_in_e[h]
+            mine_e[h, 1] = total
+            gat[h, z, y] = total
+            for dz, dy in offsets:
+                put(mine_e.at[h, 1], gat.at[h, z, y], *pair(4), on(((z + dz) % 4) * 4 + (y + dy) % 4))
+            now[4] = remote(fifteen, fifteen, *pair(4), other)
+        elif at == 5:
+            now[4].wait_recv()
+            all_e[h, :, :, core, mine] = gat[h]
+            now[5] = put(gat.at[h], all_e.at[h, :, :, core, mine], *pair(5), far_dev)
+        elif at == 6:
+            now[5].wait_recv()
+            now[6] = put(all_e.at[h, :, :, core], all_e.at[h, :, :, core], small_sem.at[26 + 2 * h],
+                         small_sem.at[27 + 2 * h], other)
+        else:
+            now[6].wait_recv()
+            if h == 0:
+                mixer_out[...] = all_e[0].reshape(WIDTH, 128)
+            else:
+                for i in range(8):
+                    rt[:, 128 * i:128 * i + 128] = all_e[1, i // 2, 2 * (i % 2):2 * (i % 2) + 2].reshape(128, 128)
+                step_out[...] = rt[pl.ds(heads_at, 16), :]
+                gain_out[...] = rt[32:33, :]
+                table_out[...] = rt[40:45, :]
+                scalars_out[...] = rt[pl.ds(scalars_at, 16), 0:256]
+
+    acts = dict(outside=outside, product=product, finish=finish, features=features, embedded=embedded_grad,
+                small=small_step, job=go_on)
+    for name, *which in PLAN:
+        acts[name](*which)
+    small[1]["tp"].wait_recv()
     for i in range(4):
         stream_out[:, 128 * i:128 * i + 128] = gg[4 * tp + i] + tp_in[i]
-    back_core.wait_recv()
-    mixer_out[...] = all_e[:, :, :, :, 0:128].reshape(WIDTH, 128)
-    for i in range(8):
-        rt[:, 128 * i:128 * i + 128] = all_e[i // 2, 2 * (i % 2):2 * (i % 2) + 2, :, :, 128:256].reshape(128, 128)
-    step_out[...] = rt[pl.ds(heads_at, 16), :]
-    gain_out[...] = rt[32:33, :]
-    table_out[...] = rt[40:45, :]
-    scalars_out[...] = rt[pl.ds(scalars_at, 16), 0:256]
-    while any(job["at"] < 6 for job in jobs):
-        low_at = min(job["at"] for job in jobs)
-        for n, job in enumerate(jobs):
-            if job["at"] == low_at:
-                go_on(n)
+
     for n in range(6, 12):
         jobs[n]["core"].wait_send()
     remote(ring, ring, job_send.at[0], job_recv.at[0], other).wait_send()
     remote(ring2, ring2, job_send.at[1], job_recv.at[0], other).wait_send()
     remote(dp_in, dp_in, job_send.at[2], job_recv.at[0], other).wait_send()
-    for copy in (to_tp, small_core, small_in, over_x, small_back, back_core):
-        copy.wait_send()
+    for half in small:
+        for copy in half.values():
+            copy.wait_send()
     to_core(0, 0, 16).wait_send()
     for copy in (all_to_owners, all_to_chips, all_entering):
         copy.wait_send()
@@ -624,12 +640,12 @@
         in_specs=[vmem] * 5 + [anywhere] + [vmem] * 5,
         out_specs=[vmem] * 7,
         scratch_shapes=[
-            bf16(3, WIDTH, WIDTH), f32(8, WIDTH), bf16(rows, WIDTH), f32(rows, WIDTH), f32(rows, 1),
+            bf16(3, WIDTH, WIDTH), bf16(rows, WIDTH), f32(rows, WIDTH), f32(rows, 1),
             f32(2, PAIRS, BASES, 128), f32(2, PAIRS, BASES, 128), f32(PAIRS, BASES, 128),
             bf16(2, BASES, 128), f32(2, HEADS, BASES), bf16(2, BASES, 128), bf16(2, 128, BASES), f32(2, HEADS, BASES),
             f32(2, HEADS, BASES), bf16(2, PAIRS, BASES, 128), bf16(2, PAIRS, BASES, 128),
             f32(2, PAIRS, BASES, 128), f32(2, PAIRS, BASES, 128), f32(2, BASES, BASES),
-            f32(2, BASES, 128), f32(2, BASES, 128), f32(2, 8, 128), f32(2, BASES, STATE), f32(2, BASES, STATE),
+            f32(2, BASES, 128), f32(2, BASES, 128), f32(2, 8, 128), f32(2, BASES, 128),
             f32(2, PAIRS, BASES, 128),
             f32(2 * CHIPS, 72, 128), f32(CHIPS, 72, 128), f32(CHIPS, 72, 128), f32(CHIPS, 72, 128),
             f32(CHIPS, STATE, 128), f32(CHIPS, STATE, 128), f32(2 * CHIPS, STATE, 128),
@@ -637,11 +653,11 @@
             bf16(WIDTH, rows), bf16(WIDTH, BASES), f32(128, WIDTH),
             f32(6, 2, 4, 4, 2, 32, 128), f32(jobs, 2, 4, 4, 32, 128), f32(jobs, 6, 4, 32, 128), f32(jobs, 2, 4, 32, 128),
             f32(jobs, 6, 32, 128), f32(jobs, 2, 32, 128), f32(jobs, 2, 16, 128),
-            f32(4, 4, 2, 32, 256), f32(4, 4, 32, 256), f32(16, 32, 256), f32(2, 32, 256), f32(3, 32, 256),
-            f32(4, 4, 2, 32, 256), f32(4, BASES, 128),
-            sems(3), sems(3), sems(6), sems(6 * jobs), sems(jobs), sems(3), sems(12),
+            f32(2, 4, 4, 2, 32, 128), f32(2, 4, 4, 32, 128), f32(2, 16, 16, 128), f32(2, 2, 16, 128), f32(2, 4, 4, 16, 128),
+            f32(2, 16, 128), f32(2, 4, 4, 16, 128), f32(2, 4, 4, 16, 128), f32(2, 4, 4, 2, 32, 128), f32(4, BASES, 128),
+            sems(3), sems(3), sems(6), sems(6 * jobs), sems(jobs), sems(3), sems(30),
         ],
-        compiler_params=pltpu.CompilerParams(collective_id=0, has_side_effects=True, vmem_limit_bytes=62 << 20),
+        compiler_params=pltpu.CompilerParams(collective_id=0, has_side_effects=True, vmem_limit_bytes=125 << 19),
         name="main",
     )(base, stream, cotangent, table, gain, w, mw, swt, bias, rate, spread)
 

time: 104 us -> 96 us (0.923); the launches traced: 102 us -> 95.8 us
  Pallas kernels: 102 us -> 95.2 us
    pallas_call x1, Pallas kernels: 99.3 us -> 92.8 us  [main(): pl.pallas_call(main_kernel, out_shape=[shape(3, 16, WIDTH), shape(WIDTH,...]
where the time goes in v5:
time: 96 us; the launch traced here: 95.8 us
  Pallas kernels  95.2 us (99%)
    pallas_call x1, Pallas kernels, main(): pl.pallas_call(main_kernel, out_shape=[shape(3, 16, WIDTH), shape(WIDTH,...  92.8 us
    pallas_call x1, Pallas kernels, emit(): pl.pallas_call(emit_kernel, out_shape=like[:5] + [row, row] + like[6:], i...  2.43 us

profile of v5, /device:TPU:1, one launch (start us, length us, event | category | flops | bytes accessed | tf_op | source)
XLA Modules:
  0.0 95.8 jit_solution(5946692135027181351)
XLA Ops:
  0.6 92.8 %main.1 = (f32[3,16,1024]{2,1,0:T(8,128)}, f32[1024,128]{1,0:T(8,128)}, f32[16,1024]{1,0:T(8,128)}, f32[5,1024]{1,0:T(8,128)}, f32[1,1024]{1,0:T(1,128)}, /*index=5*/f32[16,256]{1,0:T(8,128)}, f32[256,512]{1,0:T(8,128)}) custom-call(s32[1,256]{1,0:T(1,128)} %base.1, bf16[1,256,1024]{2,1,0:T(8,128)(2,1)} %x.1, bf16[1,256,1024]{2,1,0:T(8,128)(2,1)} %up.1, ...), custom_call_target="tpu_custom_call" | custom-call | tf_op jit(solution)/shard_map/main/pallas_call | solution.py:634
  93.4 2.4 %emit.1 = (f32[3,16,1024]{2,1,0:T(8,128)}, f32[1024,128]{1,0:T(8,128)}, f32[16,1024]{1,0:T(8,128)}, f32[5,1024]{1,0:T(8,128)}, f32[1,1024]{1,0:T(1,128)}, /*inde...) custom-call(f32[3,16,1024]{2,1,0:T(8,128)} %get-tuple-element.23.grads, f32[1024,128]{1,0:T(8,128)} %get-tuple-element.24.mixer, ...), custom_call_target="tpu_custom_call" | custom-call | tf_op jit(solution)/shard_map/emit/pallas_call | solution.py:679

commit v6 on v5

--- a/solution.py
+++ b/solution.py
@@ -65,25 +65,25 @@
 CHIPS = 16
 ORDER = [(q, k) for q in range(4) for k in (2, 1, 0)]
 PLAN = [
-    ("outside", 0, 0), ("outside", 1, 0), ("product", 0), ("product", 1), ("product", 2), ("outside", 0, 1),
+    ("outside", 0, 0), ("outside", 1, 0), ("product", 0), ("product", 1), ("outside", 0, 1), ("product", 2),
     ("outside", 1, 1), ("job", 0), ("job", 1), ("product", 3), ("product", 4), ("job", 2),
-    ("product", 5), ("outside", 0, 2), ("job", 3), ("outside", 1, 2), ("job", 0), ("job", 4),
-    ("job", 1), ("outside", 0, 3), ("job", 5), ("outside", 1, 3), ("job", 2), ("finish",),
-    ("job", 3), ("small", 0, 0), ("features", 0), ("features", 1), ("job", 0), ("job", 1),
-    ("features", 2), ("small", 0, 1), ("job", 4), ("features", 3), ("job", 5), ("embedded",),
-    ("small", 1, 0), ("product", 6), ("job", 2), ("job", 3), ("job", 1), ("job", 0),
-    ("product", 7), ("small", 1, 1), ("job", 4), ("small", 0, 2), ("job", 5), ("job", 6),
-    ("product", 8), ("job", 2), ("job", 3), ("job", 7), ("job", 0), ("job", 1),
-    ("product", 9), ("job", 4), ("product", 10), ("job", 8), ("product", 11), ("job", 5),
-    ("job", 2), ("small", 1, 2), ("job", 9), ("job", 10), ("job", 6), ("small", 0, 3),
-    ("job", 7), ("job", 11), ("job", 3), ("job", 4), ("job", 8), ("small", 0, 4),
-    ("job", 9), ("job", 5), ("job", 7), ("job", 10), ("small", 1, 3), ("job", 11),
-    ("job", 0), ("job", 1), ("job", 2), ("job", 3), ("job", 4), ("job", 6),
-    ("job", 5), ("small", 1, 4), ("job", 8), ("job", 9), ("job", 7), ("job", 11),
-    ("job", 6), ("small", 0, 5), ("job", 10), ("job", 8), ("job", 9), ("job", 6),
-    ("job", 7), ("job", 11), ("job", 10), ("small", 1, 5), ("job", 8), ("job", 9),
-    ("small", 0, 6), ("job", 11), ("job", 10), ("job", 6), ("small", 0, 7), ("job", 7),
-    ("small", 1, 6), ("job", 8), ("small", 1, 7), ("job", 9), ("job", 11), ("job", 10),
+    ("outside", 0, 2), ("product", 5), ("job", 3), ("outside", 0, 3), ("outside", 1, 2), ("job", 1),
+    ("job", 0), ("job", 4), ("job", 5), ("outside", 1, 3), ("finish",), ("small", 0, 0),
+    ("job", 3), ("product", 6), ("job", 2), ("product", 7), ("features", 0), ("small", 0, 1),
+    ("job", 0), ("job", 1), ("job", 6), ("features", 1), ("job", 4), ("job", 7),
+    ("features", 2), ("features", 3), ("embedded",), ("small", 1, 0), ("job", 2), ("job", 5),
+    ("product", 8), ("job", 3), ("small", 0, 2), ("small", 1, 1), ("product", 9), ("job", 7),
+    ("job", 8), ("product", 10), ("job", 1), ("job", 9), ("job", 3), ("job", 6),
+    ("product", 11), ("small", 1, 2), ("job", 7), ("job", 0), ("job", 11), ("small", 0, 3),
+    ("job", 10), ("job", 3), ("job", 2), ("job", 5), ("job", 9), ("job", 0),
+    ("small", 0, 4), ("job", 6), ("small", 1, 3), ("job", 8), ("job", 4), ("job", 10),
+    ("job", 11), ("job", 7), ("job", 1), ("small", 1, 4), ("job", 2), ("job", 6),
+    ("job", 4), ("job", 5), ("job", 9), ("job", 8), ("small", 0, 5), ("job", 10),
+    ("job", 11), ("job", 0), ("job", 3), ("job", 6), ("job", 7), ("job", 5),
+    ("job", 8), ("job", 4), ("job", 9), ("job", 10), ("small", 1, 5), ("job", 11),
+    ("job", 8), ("job", 9), ("job", 10), ("job", 11), ("job", 7), ("job", 2),
+    ("small", 0, 6), ("job", 6), ("job", 1), ("small", 1, 6), ("small", 0, 7), ("job", 5),
+    ("job", 4), ("job", 8), ("small", 1, 7), ("job", 9), ("job", 10), ("job", 11),
 ]
 
 
@@ -235,7 +235,7 @@
             to_core(j + 8 * half, half).start()
             return c
 
-        lax.fori_loop(first, last, step, 0)
+        lax.fori_loop(first, last, step, 0, unroll=2)
 
     def combine(i, c):
         here, there = src[CHIPS * core + i], from_core[i]
@@ -451,7 +451,7 @@
             gated[rows, lanes] = (output * swish_s[d, j]).astype(BF16)
             return c
 
-        lax.fori_loop(2 * q, 2 * q + 2, step, 0)
+        lax.fori_loop(2 * q, 2 * q + 2, step, 0, unroll=2)
 
     def product(n):
         q, k = ORDER[n]
@@ -581,6 +581,10 @@
             now[5].wait_recv()
             now[6] = put(all_e.at[h, :, :, core], all_e.at[h, :, :, core], small_sem.at[26 + 2 * h],
                          small_sem.at[27 + 2 * h], other)
+            if h == 1:
+                now["tp"].wait_recv()
+                for i in range(4):
+                    stream_out[:, 128 * i:128 * i + 128] = gg[4 * tp + i] + tp_in[i]
         else:
             now[6].wait_recv()
             if h == 0:
@@ -597,10 +601,6 @@
                 small=small_step, job=go_on)
     for name, *which in PLAN:
         acts[name](*which)
-    small[1]["tp"].wait_recv()
-    for i in range(4):
-        stream_out[:, 128 * i:128 * i + 128] = gg[4 * tp + i] + tp_in[i]
-
     for n in range(6, 12):
         jobs[n]["core"].wait_send()
     remote(ring, ring, job_send.at[0], job_recv.at[0], other).wait_send()

time: 96 us -> 93.7 us (0.976)
  Pallas kernels: 95.2 us -> 92.9 us
    pallas_call x1, Pallas kernels: 92.8 us -> 90.5 us  [main(): pl.pallas_call(main_kernel, out_shape=[shape(3, 16, WIDTH), shape(WIDTH,...]
where the time goes in v6:
time: 93.7 us; the launch traced here: 93.5 us
  Pallas kernels  92.9 us (99%)
    pallas_call x1, Pallas kernels, main(): pl.pallas_call(main_kernel, out_shape=[shape(3, 16, WIDTH), shape(WIDTH,...  90.5 us
    pallas_call x1, Pallas kernels, emit(): pl.pallas_call(emit_kernel, out_shape=like[:5] + [row, row] + like[6:], i...  2.43 us

profile of v6, /device:TPU:1, one launch (start us, length us, event | category | flops | bytes accessed | tf_op | source)
XLA Modules:
  0.0 93.5 jit_solution(473325118421471235)
XLA Ops:
  0.6 90.5 %main.1 = (f32[3,16,1024]{2,1,0:T(8,128)}, f32[1024,128]{1,0:T(8,128)}, f32[16,1024]{1,0:T(8,128)}, f32[5,1024]{1,0:T(8,128)}, f32[1,1024]{1,0:T(1,128)}, /*index=5*/f32[16,256]{1,0:T(8,128)}, f32[256,512]{1,0:T(8,128)}) custom-call(s32[1,256]{1,0:T(1,128)} %base.1, bf16[1,256,1024]{2,1,0:T(8,128)(2,1)} %x.1, bf16[1,256,1024]{2,1,0:T(8,128)(2,1)} %up.1, ...), custom_call_target="tpu_custom_call" | custom-call | tf_op jit(solution)/shard_map/main/pallas_call | solution.py:634
  91.1 2.4 %emit.1 = (f32[3,16,1024]{2,1,0:T(8,128)}, f32[1024,128]{1,0:T(8,128)}, f32[16,1024]{1,0:T(8,128)}, f32[5,1024]{1,0:T(8,128)}, f32[1,1024]{1,0:T(1,128)}, /*inde...) custom-call(f32[3,16,1024]{2,1,0:T(8,128)} %get-tuple-element.23.grads, f32[1024,128]{1,0:T(8,128)} %get-tuple-element.24.mixer, ...), custom_call_target="tpu_custom_call" | custom-call | tf_op jit(solution)/shard_map/emit/pallas_call | solution.py:679

commit v7 on v6

--- a/solution.py
+++ b/solution.py
@@ -249,7 +249,7 @@
 
     def combine_half(half):
         to_core(8 * half, half, 8).wait_recv()
-        lax.fori_loop(8 * half, 8 * half + 8, combine, 0)
+        lax.fori_loop(0, 8, lambda i, c: combine(8 * half + i, c), 0, unroll=4)
 
     ends(0, 0, PAIRS)
     ends(1, 0, PAIRS // 2)
@@ -302,7 +302,7 @@
             to_chip(t).start()
         return carry * recv[t, 64:65, :] + recv[t, 0:64, :]
 
-    lax.fori_loop(0, CHIPS, scan, jnp.zeros((STATE, 128), F32))
+    lax.fori_loop(0, CHIPS, scan, jnp.zeros((STATE, 128), F32), unroll=4)
     res[chip] = scanned[chip]
 
     inside(1)
@@ -328,7 +328,7 @@
         ent[CHIPS * core + i] = first
         return c
 
-    lax.fori_loop(0, CHIPS, hand_on, 0)
+    lax.fori_loop(0, CHIPS, hand_on, 0, unroll=4)
 
     all_entering.wait_recv()
 

time: 93.7 us -> 93.7 us (level)
  no operation moved by 1% of the time
where the time goes in v7:
time: 93.7 us; the launch traced here: 93.5 us
  Pallas kernels  92.9 us (99%)
    pallas_call x1, Pallas kernels, main(): pl.pallas_call(main_kernel, out_shape=[shape(3, 16, WIDTH), shape(WIDTH,...  90.4 us
    pallas_call x1, Pallas kernels, emit(): pl.pallas_call(emit_kernel, out_shape=like[:5] + [row, row] + like[6:], i...  2.43 us

profile of v7, /device:TPU:1, one launch (start us, length us, event | category | flops | bytes accessed | tf_op | source)
XLA Modules:
  0.0 93.5 jit_solution(13720538484420357587)
XLA Ops:
  0.6 90.4 %main.1 = (f32[3,16,1024]{2,1,0:T(8,128)}, f32[1024,128]{1,0:T(8,128)}, f32[16,1024]{1,0:T(8,128)}, f32[5,1024]{1,0:T(8,128)}, f32[1,1024]{1,0:T(1,128)}, /*index=5*/f32[16,256]{1,0:T(8,128)}, f32[256,512]{1,0:T(8,128)}) custom-call(s32[1,256]{1,0:T(1,128)} %base.1, bf16[1,256,1024]{2,1,0:T(8,128)(2,1)} %x.1, bf16[1,256,1024]{2,1,0:T(8,128)(2,1)} %up.1, ...), custom_call_target="tpu_custom_call" | custom-call | tf_op jit(solution)/shard_map/main/pallas_call | solution.py:634
  91.1 2.4 %emit.1 = (f32[3,16,1024]{2,1,0:T(8,128)}, f32[1024,128]{1,0:T(8,128)}, f32[16,1024]{1,0:T(8,128)}, f32[5,1024]{1,0:T(8,128)}, f32[1,1024]{1,0:T(1,128)}, /*inde...) custom-call(f32[3,16,1024]{2,1,0:T(8,128)} %get-tuple-element.23.grads, f32[1024,128]{1,0:T(8,128)} %get-tuple-element.24.mixer, ...), custom_call_target="tpu_custom_call" | custom-call | tf_op jit(solution)/shard_map/emit/pallas_call | solution.py:679
